TPU v7x, 32 devices: a whole 2x2x4 slice. The times are simulated.
32 devices in a mesh: groups: 1, gx: 8 (over z, y), gy: 2 (over core), segment: 2 (over x).
Axes of the slice: x: 2, y: 2, z: 4, core: 2. Of those that a mesh axis runs over, the one named last changes fastest.
Arguments:
- activations: bfloat16 [2, 8, 128, 128, 128], P('segment', 'groups', 'gx', 'gy'), may hold values from -6 to 6
- cotangent: bfloat16 [8, 128, 128, 128], P('groups', 'gx', 'gy'), may hold values from -6 to 6
- spectral_weights: float32 [2, 32, 32, 8, 8, 32], P('segment', 'gy', 'gx'), may hold values from -6 to 6
- pointwise: float32 [2, 8, 8], P('segment'), may hold values from -2 to 2
- channel_bias: float32 [2, 8], P('segment'), may hold values from -3 to 3
Outputs:
- input_grads: bfloat16 [2, 8, 128, 128, 128], P('segment', 'groups', 'gx', 'gy')
- spectral_grads: float32 [2, 32, 32, 8, 8, 32], P('segment', 'gy', 'gx', 'groups')
All inputs are finite; a program needn't handle non-finite values.
Results may differ from a plain program's by a relative error of at most 0.0042.
Values may be sent and summed in bfloat16 or wider, within the bound.
No kernel may reach another device: no remote copies, remote signals or barrier semaphores. Data moves between devices by JAX's collectives and lax.ppermute only.
A program may use at most 64 MiB of HBM per device.

v0:
```python
import math

import jax
import jax.numpy as jnp
from jax import lax
from jax.sharding import PartitionSpec as P

MODES = 32


highest = lax.Precision.HIGHEST


def from_behind(block, axis, distance):
    devices = range(lax.axis_size(axis))
    route = [(i - distance, i) for i in devices if i - distance in devices]
    return lax.ppermute(block, axis, route)


def trig_basis(length, mode_count):
    half = mode_count // 2
    freqs = jnp.arange(half, dtype=jnp.int32)[:, None]
    points = jnp.arange(length, dtype=jnp.int32)[None, :]
    step_angle = 2.0 * math.pi / length
    cosine = jnp.cos((freqs * points % length).astype(jnp.float32) * step_angle)
    sine = jnp.sin(((freqs + 1) * points % length).astype(jnp.float32) * step_angle)
    rows_all = jnp.concatenate([cosine, sine], axis=0)
    scales = jnp.where(
        jnp.arange(mode_count) == 0, 1.0 / math.sqrt(length), math.sqrt(2.0 / length)
    ).astype(jnp.float32)
    return rows_all * scales[:, None]


def gelu_slope(value):
    normal_cdf = 0.5 * (1.0 + jax.scipy.special.erf(value * 0.7071067811865476))
    return normal_cdf + value * jnp.exp(-0.5 * value * value) * 0.3989422804014327


def channel_mix(matrix, field):
    return jnp.sum(matrix[:, :, None, None, None] * field[None], axis=1)


def body(activations, cotangent, spectral_weights, pointwise, channel_bias):
    inputs = activations[0].astype(jnp.float32)
    channels, rows_x, rows_y, length_z = inputs.shape
    count_x = lax.axis_size("gx")
    count_y = lax.axis_size("gy")
    mode_count = MODES
    along_x = trig_basis(rows_x * count_x, mode_count)
    along_z = trig_basis(length_z, mode_count)
    along_y = lax.dynamic_slice_in_dim(
        trig_basis(rows_y * count_y, mode_count), lax.axis_index("gy") * rows_y, rows_y, 1
    )
    weights = spectral_weights[0]
    mixing = pointwise[0]
    mixing_back = jnp.transpose(mixing)

    def analyse(field):
        third = jnp.einsum("ixyz,cz->cixy", field, along_z, precision=highest)
        partial_value = jnp.einsum(
            "cixy,ax->ciay",
            lax.all_to_all(third, "gx", split_axis=0, concat_axis=2, tiled=True),
            along_x,
            precision=highest,
        )
        return lax.psum_scatter(
            jnp.einsum("ciay,jy->jcia", partial_value, along_y, precision=highest),
            "gy",
            scatter_dimension=0,
            tiled=True,
        )

    def synthesise(spectrum):
        second = jnp.einsum(
            "jcia,jy->ciay",
            lax.all_gather(spectrum, "gy", axis=0, tiled=True),
            along_y,
            precision=highest,
        )
        spread = jnp.einsum("ciay,ax->cixy", second, along_x, precision=highest)
        return jnp.einsum(
            "cixy,cz->ixyz",
            lax.all_to_all(spread, "gx", split_axis=2, concat_axis=0, tiled=True),
            along_z,
            precision=highest,
        )

    input_modes = analyse(inputs)
    mixed = jnp.einsum("jcioa,jcia->jcoa", weights, input_modes, precision=highest)
    pre_act = channel_mix(mixing, inputs)
    pre_act = pre_act + channel_bias[0][:, None, None, None] + synthesise(mixed)
    slope_field = gelu_slope(pre_act)
    segment_index = lax.axis_index("segment")
    segment_count = lax.axis_size("segment")
    incoming = cotangent
    kept_grad = jnp.zeros(cotangent.shape, jnp.bfloat16)
    kept_modes = jnp.zeros(input_modes.shape, jnp.float32)
    for turn_index in range(segment_count):
        active = segment_index == segment_count - 1 - turn_index
        signal = incoming.astype(jnp.float32) * slope_field
        grad_modes = analyse(signal)
        back = jnp.einsum("jcioa,jcoa->jcia", weights, grad_modes, precision=highest)
        input_grad = channel_mix(mixing_back, signal) + synthesise(back)
        input_grad = input_grad.astype(jnp.bfloat16)
        kept_grad = jnp.where(active, input_grad, kept_grad)
        kept_modes = jnp.where(active, grad_modes, kept_modes)
        if turn_index + 1 < segment_count:
            incoming = from_behind(input_grad, "segment", -1)
    weight_grad = jnp.einsum("jcia,jcoa->jcioa", input_modes, kept_modes, precision=highest)
    return (kept_grad[None], weight_grad[None])


def solution(mesh):
    return jax.shard_map(
        body,
        mesh=mesh,
        in_specs=(
            P("segment", "groups", "gx", "gy", None),
            P("groups", "gx", "gy", None),
            P("segment", "gy", "gx", None, None, None),
            P("segment", None, None),
            P("segment", None),
        ),
        out_specs=(
            P("segment", "groups", "gx", "gy", None),
            P("segment", "gy", "gx", "groups", None, None),
        ),
        check_vma=False,
    )
```

profile of v0, /device:TPU:0, one launch (start us, length us, event | category | flops | bytes accessed | tf_op | source)
XLA Modules:
  0.0 441.0 jit_solution(13617722540841769567)
XLA Ops:
  7.4 7.4 %fusion.7 = f32[32,8,16,64]{3,0,2,1:T(8,128)S(1)} fusion(bf16[1,8,16,64,128]{4,3,2,1,0:T(8,128)(2,1)} %param.5, f32[32,128]{1,0:T(8,128)S(1)} %maximum_multiply_fusion), kind=kOutput, calls=%fused_computation.18 | convolution fusion | flops 402653184 | bytes 3162112 | tf_op jit(solution)/shard_map/ixyz,cz->cixy/dot_general | solution.py:59
  18.1 7.3 %all-to-all-start = ((f32[8,1,32768]{2,1,0:T(1,128)}), f32[8,1,32768]{2,1,0:T(1,128)S(1)}, u32[]{:S(2)}, u32[]{:S(2)}) async-start(f32[8,1,32768]{2,1,0:T(1,128)} %reshape.27), calls=%async_computation | async-start | bytes 2097152 | tf_op jit(solution)/shard_map/all_to_all | solution.py:62
  25.4 25.7 %all-to-all-done = f32[8,1,32768]{2,1,0:T(1,128)S(1)} async-done(((f32[8,1,32768]{2,1,0:T(1,128)}), f32[8,1,32768]{2,1,0:T(1,128)S(1)}, u32[]{:S(2)}, u32[]{:S(2)}) %all-to-all-start) | async-done | bytes 1048608 | tf_op jit(solution)/shard_map/all_to_all | solution.py:62
  60.4 7.1 %reduce-scatter.4.cloned.1.call-done = f32[16,4,8,32]{3,0,2,1:T(8,128)} async-done(((f32[32,4,8,32]{3,0,2,1:T(8,128)}), f32[16,4,8,32]{3,0,2,1:T(8,128)}) %reduce-scatter.4.cloned.1.call-update) | async-done | bytes 65552 | tf_op jit(solution)/shard_map/reduce_scatter | solution.py:66
  80.6 5.7 %all-to-all-start.1 = ((f32[8,1,32768]{2,1,0:T(1,128)}), f32[8,1,32768]{2,1,0:T(1,128)}, u32[]{:S(2)}, u32[]{:S(2)}) async-start(f32[8,1,32768]{2,1,0:T(1,128)} %reshape.29), calls=%async_computation.2 | async-start | bytes 2097152 | tf_op jit(solution)/shard_map/all_to_all | solution.py:83
  90.5 7.2 %multiply_reduce_fusion.2 = f32[8,16,64,128]{3,2,1,0:T(8,128)} fusion(f32[8,16,64,128]{3,2,1,0:T(8,128)} %bitcast_convert_fusion, f32[8,8]{1,0:T(8,128)S(1)} %bitcast.160), kind=kLoop, calls=%fused_computation.2 | loop fusion | flops 15728640 | bytes 8388864 | tf_op jit(solution)/shard_map/reduce_sum | solution.py:40
  97.6 15.1 %all-to-all-done.1 = f32[8,1,32768]{2,1,0:T(1,128)} async-done(((f32[8,1,32768]{2,1,0:T(1,128)}), f32[8,1,32768]{2,1,0:T(1,128)}, u32[]{:S(2)}, u32[]{:S(2)}) %all-to-all-start.1) | async-done | bytes 1048608 | tf_op jit(solution)/shard_map/all_to_all | solution.py:83
  122.1 11.8 %convert_multiply_fusion.1 = (f32[8,16,64,128]{3,2,1,0:T(8,128)S(1)}, f32[8,16,64,128]{3,2,1,0:T(8,128)}) fusion(bf16[8,16,64,128]{3,2,1,0:T(8,128)(2,1)} %param.6, f32[32,8,16,64]{3,0,2,1:T(8,128)S(1)} %bitcast.153, f32[32,128]{1,0:T(8,128)S(1)} %maximum_multiply_fusion, f32[8,16,64,128]{3,2,1,0:T(8,128)S(1)} %copy-done.6, f32[8]{0:T(128)S(1)} %bitcast.162), kind=kOutput, calls=%fused_computation.11 | convolution fusion | flops 415236096 | bytes 15745056 | tf_op jit(solution)/shard_map/cixy,cz->ixyz/dot_general | solution.py:81
  133.9 11.3 %fusion.32 = f32[32,8,16,64]{3,0,2,1:T(8,128)S(1)} fusion(f32[8,16,64,128]{3,2,1,0:T(8,128)S(1)} %get-tuple-element.2, f32[32,128]{1,0:T(8,128)S(1)} %maximum_multiply_fusion), kind=kOutput, calls=%fused_computation.54 | convolution fusion | flops 402653184 | bytes 5259264 | tf_op jit(solution)/shard_map/ixyz,cz->cixy/dot_general | solution.py:59
  150.3 29.7 %all_to_all.108 = f32[8,1,32768]{2,1,0:T(1,128)} all-to-all(f32[8,1,32768]{2,1,0:T(1,128)S(1)} %reshape.31), channel_id=1, replica_groups=mesh['groups'=1,'gx'=8,'gy'=2,'segment'=2] {'gx'}, dimensions={0} | all-to-all | bytes 2097152 | tf_op jit(solution)/shard_map/all_to_all | solution.py:62
  192.8 7.1 %reduce-scatter.6.cloned.1.call-done = f32[16,4,8,32]{3,0,2,1:T(8,128)} async-done(((f32[32,4,8,32]{3,0,2,1:T(8,128)}), f32[16,4,8,32]{3,0,2,1:T(8,128)}) %reduce-scatter.6.cloned.1.call-update) | async-done | bytes 65552 | tf_op jit(solution)/shard_map/reduce_scatter | solution.py:66
  213.2 5.7 %all-to-all-start.3 = ((f32[8,1,32768]{2,1,0:T(1,128)}), f32[8,1,32768]{2,1,0:T(1,128)}, u32[]{:S(2)}, u32[]{:S(2)}) async-start(f32[8,1,32768]{2,1,0:T(1,128)} %reshape.33), calls=%async_computation.5 | async-start | bytes 2097152 | tf_op jit(solution)/shard_map/all_to_all | solution.py:83
  219.4 7.2 %multiply_reduce_fusion.1 = f32[8,16,64,128]{3,2,1,0:T(8,128)} fusion(f32[8,16,64,128]{3,2,1,0:T(8,128)} %copy-done.1, f32[8,8]{1,0:T(8,128)S(1)} %copy.49), kind=kLoop, calls=%fused_computation.1 | loop fusion | flops 15728640 | bytes 8388864 | tf_op jit(solution)/shard_map/reduce_sum | solution.py:40
  226.6 18.6 %all-to-all-done.3 = f32[8,1,32768]{2,1,0:T(1,128)} async-done(((f32[8,1,32768]{2,1,0:T(1,128)}), f32[8,1,32768]{2,1,0:T(1,128)}, u32[]{:S(2)}, u32[]{:S(2)}) %all-to-all-start.3) | async-done | bytes 1048608 | tf_op jit(solution)/shard_map/all_to_all | solution.py:83
  245.3 4.3 reduce.9
  254.6 7.1 %add_convert_fusion.1 = bf16[8,16,64,128]{3,2,1,0:T(8,128)(2,1)S(1)} fusion(f32[8,16,64,128]{3,2,1,0:T(8,128)S(1)} %copy-done.4, f32[32,8,16,64]{3,0,2,1:T(8,128)S(1)} %bitcast.152, f32[32,128]{1,0:T(8,128)S(1)} %maximum_multiply_fusion), kind=kOutput, calls=%fused_computation.10 | convolution fusion | flops 404750336 | bytes 7356416 | tf_op jit(solution)/shard_map/cixy,cz->ixyz/dot_general | solution.py:81
  263.1 47.1 %collective-permute-done = bf16[8,16,64,128]{3,2,1,0:T(8,128)(2,1)S(1)} collective-permute-done((bf16[8,16,64,128]{3,2,1,0:T(8,128)(2,1)S(1)}, bf16[8,16,64,128]{3,2,1,0:T(8,128)(2,1)S(1)}, u32[]{:S(2)}, u32[]{:S(2)}) %collective-permute-start) | collective-permute-done | bytes 2097184 | tf_op jit(solution)/shard_map/ppermute | solution.py:17
  311.3 11.3 %fusion.27 = f32[32,8,16,64]{3,0,2,1:T(8,128)S(1)} fusion(f32[8,16,64,128]{3,2,1,0:T(8,128)S(1)} %convert_multiply_fusion, f32[32,128]{1,0:T(8,128)S(1)} %maximum_multiply_fusion), kind=kOutput, calls=%fused_computation.49 | convolution fusion | flops 402653184 | bytes 5259264 | tf_op jit(solution)/shard_map/ixyz,cz->cixy/dot_general | solution.py:59
  327.8 29.7 %all_to_all.109 = f32[8,1,32768]{2,1,0:T(1,128)} all-to-all(f32[8,1,32768]{2,1,0:T(1,128)S(1)} %reshape.35), channel_id=1, replica_groups=mesh['groups'=1,'gx'=8,'gy'=2,'segment'=2] {'gx'}, dimensions={0} | all-to-all | bytes 2097152 | tf_op jit(solution)/shard_map/all_to_all | solution.py:62
  370.4 6.1 %reduce-scatter.8.cloned.1.call-done = f32[16,4,8,32]{3,0,2,1:T(8,128)} async-done(((f32[32,4,8,32]{3,0,2,1:T(8,128)}), f32[16,4,8,32]{3,0,2,1:T(8,128)}) %reduce-scatter.8.cloned.1.call-update) | async-done | bytes 65552 | tf_op jit(solution)/shard_map/reduce_scatter | solution.py:66
  387.6 6.0 %all-to-all-start.5 = ((f32[8,1,32768]{2,1,0:T(1,128)}), f32[8,1,32768]{2,1,0:T(1,128)S(1)}, u32[]{:S(2)}, u32[]{:S(2)}) async-start(f32[8,1,32768]{2,1,0:T(1,128)} %reshape.37), calls=%async_computation.8 | async-start | bytes 2097152 | tf_op jit(solution)/shard_map/all_to_all | solution.py:83
  393.7 7.2 %multiply_reduce_fusion = f32[8,16,64,128]{3,2,1,0:T(8,128)} fusion(f32[8,16,64,128]{3,2,1,0:T(8,128)} %copy-done, f32[8,8]{1,0:T(8,128)S(1)} %copy.49), kind=kLoop, calls=%fused_computation | loop fusion | flops 15728640 | bytes 8388864 | tf_op jit(solution)/shard_map/reduce_sum | solution.py:40
  402.7 17.2 %all-to-all-done.5 = f32[8,1,32768]{2,1,0:T(1,128)S(1)} async-done(((f32[8,1,32768]{2,1,0:T(1,128)}), f32[8,1,32768]{2,1,0:T(1,128)S(1)}, u32[]{:S(2)}, u32[]{:S(2)}) %all-to-all-start.5) | async-done | bytes 1048608 | tf_op jit(solution)/shard_map/all_to_all | solution.py:83
  426.0 8.0 %select_bitcast_fusion = bf16[1,8,16,64,128]{4,3,2,1,0:T(8,128)(2,1)} fusion(bf16[8,16,64,128]{3,2,1,0:T(8,128)(2,1)} %copy-done.7, pred[]{:T(512)S(6)} %eq.24, pred[]{:T(512)S(6)} %eq.22, f32[8,16,64,128]{3,2,1,0:T(8,128)S(1)} %copy-done.3, f32[32,8,16,64]{3,0,2,1:T(8,128)S(1)} %bitcast.151, f32[32,128]{1,0:T(8,128)S(1)} %maximum_multiply_fusion), kind=kOutput, calls=%fused_computation.22 | convolution fusion | flops 406847488 | bytes 9453570 | tf_op jit(solution)/shard_map/cixy,cz->ixyz/dot_general | solution.py:81
  (92 shorter events, 115.1 us)
Async XLA Ops:
  18.1 33.0 %all-to-all-start = ((f32[8,1,32768]{2,1,0:T(1,128)}), f32[8,1,32768]{2,1,0:T(1,128)S(1)}, u32[]{:S(2)}, u32[]{:S(2)}) async-start(f32[8,1,32768]{2,1,0:T(1,128)} %reshape.27), calls=%async_computation | async-start | bytes 2097152 | tf_op jit(solution)/shard_map/all_to_all | solution.py:62
  25.4 42.1 %reduce-scatter.4.cloned.1.call-start = ((), (), s32[]{:S(2)}) async-start(), calls=%async_computation.9 | async-start | bytes 786432 | tf_op jit(solution)/shard_map/reduce_scatter | solution.py:66
  55.9 12.7 %copy-start.2 = (f32[1,16,4,8,8,32]{5,4,3,2,1,0:T(8,128)S(1)}, f32[1,16,4,8,8,32]{5,4,3,2,1,0:T(8,128)}, u32[]{:S(2)}) copy-start(f32[1,16,4,8,8,32]{5,4,3,2,1,0:T(8,128)} %param.7) | copy-start | bytes 1572868
  80.6 32.1 %all-to-all-start.1 = ((f32[8,1,32768]{2,1,0:T(1,128)}), f32[8,1,32768]{2,1,0:T(1,128)}, u32[]{:S(2)}, u32[]{:S(2)}) async-start(f32[8,1,32768]{2,1,0:T(1,128)} %reshape.29), calls=%async_computation.2 | async-start | bytes 2097152 | tf_op jit(solution)/shard_map/all_to_all | solution.py:83
  86.4 4.1 copy-start.10
  86.4 113.6 %reduce-scatter.6.cloned.1.call-start = ((), (), s32[]{:S(2)}) async-start(), calls=%async_computation.10 | async-start | bytes 786432 | tf_op jit(solution)/shard_map/reduce_scatter | solution.py:66
  119.2 2.8 copy-start.6
  119.2 2.8 copy-start.11
  133.9 11.4 %copy-start.1 = (f32[8,16,64,128]{3,2,1,0:T(8,128)}, f32[8,16,64,128]{3,2,1,0:T(8,128)S(1)}, u32[]{:S(2)}) copy-start(f32[8,16,64,128]{3,2,1,0:T(8,128)S(1)} %get-tuple-element.2) | copy-start | bytes 12582916
  213.2 32.1 %all-to-all-start.3 = ((f32[8,1,32768]{2,1,0:T(1,128)}), f32[8,1,32768]{2,1,0:T(1,128)}, u32[]{:S(2)}, u32[]{:S(2)}) async-start(f32[8,1,32768]{2,1,0:T(1,128)} %reshape.33), calls=%async_computation.5 | async-start | bytes 2097152 | tf_op jit(solution)/shard_map/all_to_all | solution.py:83
  218.9 157.6 %reduce-scatter.8.cloned.1.call-start = ((), (), s32[]{:S(2)}) async-start(), calls=%async_computation.11 | async-start | bytes 786432 | tf_op jit(solution)/shard_map/reduce_scatter | solution.py:66
  251.7 2.8 copy-start.4
  254.6 55.7 %copy-start.5 = (f32[8,16,64,128]{3,2,1,0:T(8,128)S(1)}, f32[8,16,64,128]{3,2,1,0:T(8,128)}, u32[]{:S(2)}) copy-start(f32[8,16,64,128]{3,2,1,0:T(8,128)} %get-tuple-element.3) | copy-start | bytes 12582916
  261.6 48.6 %copy-start.7 = (bf16[8,16,64,128]{3,2,1,0:T(8,128)(2,1)}, bf16[8,16,64,128]{3,2,1,0:T(8,128)(2,1)S(1)}, u32[]{:S(2)}) copy-start(bf16[8,16,64,128]{3,2,1,0:T(8,128)(2,1)S(1)} %add_convert_fusion.1) | copy-start | bytes 6291460
  261.6 48.6 %collective-permute-start = (bf16[8,16,64,128]{3,2,1,0:T(8,128)(2,1)S(1)}, bf16[8,16,64,128]{3,2,1,0:T(8,128)(2,1)S(1)}, u32[]{:S(2)}, u32[]{:S(2)}) collective-permute-start(bf16[8,16,64,128]{3,2,1,0:T(8,128)(2,1)S(1)} %add_convert_fusion.1), channel_id=1, source_target_pairs={{1,0},{3,2},{5,4},{7,6},{9,8},{11,10},{13,12},{15,14},{17,16},{19,... | collective-permute-start | bytes 6291464 | tf_op jit(solution)/shard_map/ppermute | solution.py:17
  311.3 11.4 %copy-start = (f32[8,16,64,128]{3,2,1,0:T(8,128)}, f32[8,16,64,128]{3,2,1,0:T(8,128)S(1)}, u32[]{:S(2)}) copy-start(f32[8,16,64,128]{3,2,1,0:T(8,128)S(1)} %convert_multiply_fusion) | copy-start | bytes 12582916
  387.6 32.3 %all-to-all-start.5 = ((f32[8,1,32768]{2,1,0:T(1,128)}), f32[8,1,32768]{2,1,0:T(1,128)S(1)}, u32[]{:S(2)}, u32[]{:S(2)}) async-start(f32[8,1,32768]{2,1,0:T(1,128)} %reshape.37), calls=%async_computation.8 | async-start | bytes 2097152 | tf_op jit(solution)/shard_map/all_to_all | solution.py:83
  393.7 7.2 %copy-start.8 = (f32[16,4,8,32]{3,0,2,1:T(8,128)S(1)}, f32[16,4,8,32]{3,0,2,1:T(8,128)}, u32[]{:S(2)}) copy-start(f32[16,4,8,32]{3,0,2,1:T(8,128)} %reduce-scatter.6.cloned.1.call-done) | copy-start | bytes 196612
  393.7 7.2 %copy-start.9 = (f32[16,4,8,32]{3,0,2,1:T(8,128)S(1)}, f32[16,4,8,32]{3,0,2,1:T(8,128)}, u32[]{:S(2)}) copy-start(f32[16,4,8,32]{3,0,2,1:T(8,128)} %reduce-scatter.8.cloned.1.call-done) | copy-start | bytes 196612
  423.8 2.2 copy-start.3
Sparse Core Ops, SparseCore 0:
  60.5 6.9 reduce-scatter.3
  193.0 6.9 reduce-scatter.5
  370.5 5.9 reduce-scatter.7
where the time goes:
time: 450 us; the launch traced here: 441 us
  waiting for transfers between devices  144 us (32%)
  matrix products  79.5 us (18%)
  blocking collectives  66.3 us (15%)
  local copies, waits for them, and re-layouts  55.7 us (12%)
  other arithmetic  53.9 us (12%)
  starting transfers between devices  26.8 us (6%)
  between operations  14.6 us (3%)
    all_to_all x2, blocking collectives, analyse(): lax.all_to_all(third, 'gx', split_axis=0, concat_axis=2, tiled=True)  59.4 us
    all_to_all x3, waiting for transfers between devices, synthesise(): lax.all_to_all(spread, 'gx', split_axis=2, concat_axis=0, tiled=True)  51 us
    ppermute x1, waiting for transfers between devices, from_behind(): return lax.ppermute(block, axis, route)  47.1 us
    unnamed x39, local copies, waits for them, and re-layouts  32.2 us
    dot_general x3, matrix products, analyse(): third = jnp.einsum('ixyz,cz->cixy', field, along_z, precision=highest)  30.1 us
    dot_general x3, matrix products, synthesise(): jnp.einsum('cixy,cz->ixyz', lax.all_to_all(spread, 'gx', split_axis=2, co...  26.9 us
    all_to_all x1, waiting for transfers between devices, analyse(): lax.all_to_all(third, 'gx', split_axis=0, concat_axis=2, tiled=True)  25.7 us
    reduce_sum x3, other arithmetic, channel_mix(): return jnp.sum(matrix[:, :, None, None, None] * field[None], axis=1)  21.6 us
  transfers between devices with their start and end apart: 8, of which 8 were waited for; matrix products, arithmetic and copies ran while one was open for 6% of the time, Pallas kernels for 0%

commit v1 on v0

v1 whole, which is shorter than its diff:
```python
import functools
import math

import jax
import jax.numpy as jnp
import ml_dtypes
import numpy as np
from jax import lax
from jax.experimental import pallas as pl
from jax.experimental.pallas import tpu as pltpu
from jax.sharding import PartitionSpec as P

MODES = 32
LANES = 128
PLANE = ("gx", "gy")
F32 = jnp.float32
BF16 = jnp.bfloat16
VMEM_LIMIT = 40 * 1024 * 1024


def trig_basis(length):
    half = MODES // 2
    points = np.arange(length)[None, :]
    freqs = np.arange(half)[:, None]
    angle = 2.0 * math.pi / length
    rows = np.concatenate(
        [np.cos((freqs * points % length) * angle), np.sin(((freqs + 1) * points % length) * angle)], axis=0
    )
    scales = np.where(np.arange(MODES) == 0, 1.0 / math.sqrt(length), math.sqrt(2.0 / length))
    return rows * scales[:, None]


def high_low(values):
    high = values.astype(np.float32).astype(ml_dtypes.bfloat16)
    low = (values - high.astype(np.float64)).astype(np.float32).astype(ml_dtypes.bfloat16)
    return np.stack([high, low])


class Plan:
    def __init__(self, channels, rows_x, rows_y, length_z, count_x, count_y):
        self.channels, self.rows_x, self.rows_y, self.length_z = channels, rows_x, rows_y, length_z
        self.count_x, self.count_y = count_x, count_y
        self.devices = count_x * count_y
        self.padded_x = -(-rows_x // 16) * 16
        self.block_x = math.gcd(rows_x, 4)
        self.blocks = rows_x // self.block_x
        self.rows = self.block_x * rows_y
        self.own_third = MODES // count_x
        self.own_second = MODES // count_y
        self.width = self.own_third * channels
        self.per_tile = LANES // self.width
        self.tiles = self.own_second // self.per_tile
        self.halves = MODES * channels // LANES
        self.wire = (self.devices, self.padded_x, self.own_second * self.width)
        self.pairs = self.own_second * self.own_third
        along_x = trig_basis(rows_x * count_x)
        along_y = trig_basis(rows_y * count_y)
        along_z = trig_basis(length_z)
        third = np.einsum("ik,cz->izck", np.eye(channels), along_z)
        third = third.reshape(channels * length_z, MODES * channels)
        self.third = high_low(third)
        self.third_t = high_low(third.T)
        slabs = along_y.reshape(MODES, count_y, rows_y)
        pick = np.zeros((self.padded_x, self.blocks, self.block_x))
        for x in range(rows_x):
            pick[x, x // self.block_x, x % self.block_x] = 1.0
        second = np.einsum("jhy,xbk->hbjxky", slabs, pick)
        second = second.reshape(count_y, self.blocks, MODES * self.padded_x, self.rows)
        self.second = np.moveaxis(high_low(second), 0, 2)
        self.second_t = np.moveaxis(high_low(np.swapaxes(second, 2, 3)), 0, 2)
        padded = np.zeros((MODES, count_x, self.padded_x))
        padded[:, :, :rows_x] = along_x.reshape(MODES, count_x, rows_x)
        first = np.repeat(padded[:, :, None, :], count_y, axis=2)
        self.first = high_low(first.reshape(MODES, self.devices * self.padded_x))
        self.first_t = high_low(padded.reshape(MODES, count_x * self.padded_x).T)


def dot(a, b):
    return jnp.dot(a, b, preferred_element_type=F32)


def split(value):
    high = value.astype(BF16)
    return high, (value - high.astype(F32)).astype(BF16)


def swap_groups(parts, width):
    parts = list(parts)
    lane = lax.broadcasted_iota(jnp.int32, parts[0].shape, 1)
    bit = len(parts) // 2
    while bit:
        shift = bit * width
        low = (lane // shift) % 2 == 0
        for at in range(len(parts)):
            if at & bit:
                continue
            a, b = parts[at], parts[at | bit]
            parts[at] = jnp.where(low, a, pltpu.roll(b, shift, 1))
            parts[at | bit] = jnp.where(low, pltpu.roll(a, LANES - shift, 1), b)
        bit //= 2
    return parts


def pack_wire(plan, total_ref, wire_ref):
    px, group = plan.padded_x, plan.per_tile
    for half in range(plan.halves):
        for block in range(MODES // group):
            parts = [
                total_ref[pl.ds((block * group + j) * px, px), pl.ds(half * LANES, LANES)] for j in range(group)
            ]
            parts = swap_groups(parts, plan.width)
            owner_y, tile = block // plan.tiles, block % plan.tiles
            for g in range(group):
                target = (half * group + g) * plan.count_y + owner_y
                wire_ref[target, :, pl.ds(tile * LANES, LANES)] = parts[g].astype(BF16)


def unpack_wire(plan, wire_ref, spectrum_ref):
    px, group = plan.padded_x, plan.per_tile
    for half in range(plan.halves):
        for block in range(MODES // group):
            owner_y, tile = block // plan.tiles, block % plan.tiles
            parts = [
                wire_ref[(half * group + g) * plan.count_y + owner_y, :, pl.ds(tile * LANES, LANES)].astype(F32)
                for g in range(group)
            ]
            parts = swap_groups(parts, plan.width)
            for j in range(group):
                spectrum_ref[pl.ds((block * group + j) * px, px), pl.ds(half * LANES, LANES)] = parts[j].astype(BF16)


def analyse_block(plan, block, fields, third_ref, second_ref, total_ref, wire_ref):
    step = pl.program_id(0)
    inner = dot(fields, third_ref[0]) + dot(fields, third_ref[1])
    high, low = split(inner)
    part = dot(second_ref[0], high) + dot(second_ref[0], low) + dot(second_ref[1], high)

    @pl.when(step == 0)
    def _():
        total_ref[...] = part

    @pl.when(step > 0)
    def _():
        total_ref[...] += part

    @pl.when(step == plan.blocks - 1)
    def _():
        pack_wire(plan, total_ref, wire_ref)


def synthesise_block(plan, wire_ref, second_t_ref, third_t_ref, spectrum_ref, field_ref):
    @pl.when(pl.program_id(0) == 0)
    def _():
        unpack_wire(plan, wire_ref, spectrum_ref)

    spectrum = spectrum_ref[...]
    inner = (dot(second_t_ref[0], spectrum) + dot(second_t_ref[1], spectrum)).astype(BF16)
    field_ref[...] = dot(inner, third_t_ref[0]) + dot(inner, third_t_ref[1])


def gelu_slope(value):
    size = jnp.abs(value)
    t = 1.0 / (1.0 + (0.3275911 * 0.7071067811865476) * size)
    poly = 0.5 * 1.061405429
    for c in (-1.453152027, 1.421413741, -0.284496736, 0.254829592):
        poly = poly * t + 0.5 * c
    bell = jnp.exp(-0.5 * value * value)
    tail = bell * (poly * t - 0.3989422804014327 * size)
    return jnp.where(value >= 0, 1.0 - tail, tail)


CHUNK = 32


def each_chunk(plan, work):
    def step(k, carry):
        work(pl.ds(pl.multiple_of(k * CHUNK, CHUNK), CHUNK))
        return carry

    lax.fori_loop(0, plan.rows // CHUNK, step, 0)


def lanes_of(plan, channel):
    return pl.ds(channel * plan.length_z, plan.length_z)


def send_back(plan, rows, signals, mixing_ref, fields_ref, local_ref):
    for o, signal in enumerate(signals):
        fields_ref[rows, lanes_of(plan, o)] = signal.astype(BF16)
    for i in range(plan.channels):
        value = mixing_ref[0, i] * signals[0]
        for o in range(1, plan.channels):
            value = value + mixing_ref[o, i] * signals[o]
        local_ref[i, rows, :] = value.astype(BF16)


def input_kernel(plan, flags, act_ref, third_ref, second_ref, wire_ref, total_ref):
    fields = jnp.concatenate([act_ref[i] for i in range(plan.channels)], axis=1)
    analyse_block(plan, None, fields, third_ref, second_ref, total_ref, wire_ref)


def first_kernel(
    plan, flags, mixing_ref, bias_ref, act_ref, cot_ref, wire_in_ref, third_ref, third_t_ref, second_ref, second_t_ref,
    wire_ref, slope_ref, local_ref, total_ref, spectrum_ref, field_ref, fields_ref,
):
    synthesise_block(plan, wire_in_ref, second_t_ref, third_t_ref, spectrum_ref, field_ref)

    def work(rows):
        inputs = [act_ref[i, rows, :].astype(F32) for i in range(plan.channels)]
        signals = []
        for o in range(plan.channels):
            pre = field_ref[rows, lanes_of(plan, o)] + bias_ref[0, o]
            for i in range(plan.channels):
                pre = pre + mixing_ref[o, i] * inputs[i]
            slope = gelu_slope(pre)
            slope_ref[o, rows, :] = slope
            signals.append(cot_ref[o, rows, :].astype(F32) * slope)
        send_back(plan, rows, signals, mixing_ref, fields_ref, local_ref)

    each_chunk(plan, work)
    analyse_block(plan, None, fields_ref[...], third_ref, second_ref, total_ref, wire_ref)


def middle_kernel(
    plan, flags, mixing_ref, own_ref, other_ref, slope_ref, wire_in_ref, third_ref, third_t_ref, second_ref,
    second_t_ref, wire_ref, grad_ref, local_ref, total_ref, spectrum_ref, field_ref, fields_ref,
):
    synthesise_block(plan, wire_in_ref, second_t_ref, third_t_ref, spectrum_ref, field_ref)
    active = flags[1] > 0

    def work(rows):
        signals = []
        for i in range(plan.channels):
            local = jnp.where(active, own_ref[i, rows, :].astype(F32), other_ref[i, rows, :].astype(F32))
            grad = local + field_ref[rows, lanes_of(plan, i)]
            grad_ref[i, rows, :] = grad.astype(BF16)
            signals.append(grad * slope_ref[i, rows, :])
        send_back(plan, rows, signals, mixing_ref, fields_ref, local_ref)

    each_chunk(plan, work)
    analyse_block(plan, None, fields_ref[...], third_ref, second_ref, total_ref, wire_ref)


def last_kernel(
    plan, flags, own_ref, kept_ref, wire_in_ref, third_t_ref, second_t_ref, grad_ref, spectrum_ref, field_ref
):
    synthesise_block(plan, wire_in_ref, second_t_ref, third_t_ref, spectrum_ref, field_ref)
    active = flags[1] > 0

    def work(rows):
        for i in range(plan.channels):
            grad = own_ref[i, rows, :].astype(F32) + field_ref[rows, lanes_of(plan, i)]
            grad_ref[i, rows, :] = jnp.where(active, grad.astype(BF16), kept_ref[i, rows, :])

    each_chunk(plan, work)


def mode_sums(plan, wire_ref, first_ref):
    received = wire_ref[...].reshape(plan.devices * plan.padded_x, plan.own_second * plan.width)
    modes = dot(first_ref[0], received) + dot(first_ref[1], received)
    return modes.T.reshape(plan.pairs, plan.channels, MODES)


def mix_modes(plan, modes, weights_ref, backward):
    if not backward:
        mixed = weights_ref[:, 0] * modes[:, 0:1, :]
        for i in range(1, plan.channels):
            mixed = mixed + weights_ref[:, i] * modes[:, i : i + 1, :]
        return mixed
    row = lax.broadcasted_iota(jnp.int32, modes.shape, 1)
    mixed = jnp.zeros_like(modes)
    for i in range(plan.channels):
        mixed = jnp.where(row == i, jnp.sum(weights_ref[:, i] * modes, axis=1, keepdims=True), mixed)
    return mixed


def spread_modes(plan, mixed, first_t_ref, wire_out_ref):
    flat = mixed.reshape(plan.pairs * plan.channels, MODES)
    high, low = split(flat)

    def across(a, b):
        return lax.dot_general(a, b, (((1,), (1,)), ((), ())), preferred_element_type=F32)

    spread = across(first_t_ref[0], high) + across(first_t_ref[0], low) + across(first_t_ref[1], high)
    spread = spread.astype(BF16)
    for g in range(plan.count_x):
        piece = spread[g * plan.padded_x : (g + 1) * plan.padded_x]
        for h in range(plan.count_y):
            wire_out_ref[g * plan.count_y + h] = piece


def spectral_kernel(plan, backward, wire_ref, weights_ref, first_ref, first_t_ref, modes_ref, wire_out_ref):
    modes = mode_sums(plan, wire_ref, first_ref)
    modes_ref[...] = modes
    spread_modes(plan, mix_modes(plan, modes, weights_ref, backward), first_t_ref, wire_out_ref)


def mixing_kernel(plan, wire_ref, weights_ref, first_ref, modes_ref, mixed_ref):
    modes = mode_sums(plan, wire_ref, first_ref)
    modes_ref[...] = modes
    mixed_ref[...] = mix_modes(plan, modes, weights_ref, True)


def spread_kernel(plan, flags, own_ref, other_ref, first_t_ref, wire_out_ref):
    mixed = jnp.where(flags[1] > 0, own_ref[...], other_ref[...])
    spread_modes(plan, mixed, first_t_ref, wire_out_ref)


def params():
    return pltpu.CompilerParams(vmem_limit_bytes=VMEM_LIMIT)


class Calls:
    def __init__(self, plan):
        self.plan = p = plan
        self.field_block = pl.BlockSpec((p.channels, p.rows, p.length_z), lambda b, f: (0, b, 0))
        self.wire_block = pl.BlockSpec(p.wire, lambda b, f: (0, 0, 0))
        self.third = pl.BlockSpec(p.third.shape, lambda b, f: (0, 0, 0))
        self.third_t = pl.BlockSpec(p.third_t.shape, lambda b, f: (0, 0, 0))
        self.second = pl.BlockSpec((None, None) + p.second.shape[2:], lambda b, f: (f[0], b, 0, 0, 0))
        self.second_t = pl.BlockSpec((None, None) + p.second_t.shape[2:], lambda b, f: (f[0], b, 0, 0, 0))
        self.small = pl.BlockSpec(memory_space=pltpu.SMEM)
        self.total = pltpu.VMEM((MODES * p.padded_x, MODES * p.channels), F32)
        self.spectrum = pltpu.VMEM((MODES * p.padded_x, MODES * p.channels), BF16)
        self.field = pltpu.VMEM((p.rows, p.channels * p.length_z), F32)
        self.fields = pltpu.VMEM((p.rows, p.channels * p.length_z), BF16)
        self.wire_shape = jax.ShapeDtypeStruct(p.wire, BF16)
        self.modes_shape = jax.ShapeDtypeStruct((p.pairs, p.channels, MODES), F32)

    def field_shape(self, dtype):
        p = self.plan
        return jax.ShapeDtypeStruct((p.channels, p.rows_x * p.rows_y, p.length_z), dtype)

    def over_blocks(self, kernel, name, flags, args, in_specs, out_specs, out_shape, scratch):
        return pl.pallas_call(
            functools.partial(kernel, self.plan),
            grid_spec=pltpu.PrefetchScalarGridSpec(
                num_scalar_prefetch=1, grid=(self.plan.blocks,), in_specs=in_specs, out_specs=out_specs,
                scratch_shapes=scratch,
            ),
            out_shape=out_shape, compiler_params=params(), name=name,
        )(flags, *args)

    def whole(self, kernel, name, args, out_shape, flags=None):
        specs = [pl.BlockSpec(memory_space=pltpu.VMEM)] * len(args)
        if flags is not None:
            args, specs = (flags, *args), [self.small] + specs
        return pl.pallas_call(
            kernel, in_specs=specs,
            out_specs=jax.tree.map(lambda _: pl.BlockSpec(memory_space=pltpu.VMEM), out_shape),
            out_shape=out_shape, compiler_params=params(), name=name,
        )(*args)


def exchange(wire):
    return lax.all_to_all(wire, PLANE, split_axis=0, concat_axis=0, tiled=True)


def from_behind(block, distance):
    devices = range(lax.axis_size("segment"))
    route = [(i - distance, i) for i in devices if i - distance in devices]
    return lax.ppermute(block, "segment", route)


def body(activations, cotangent, spectral_weights, pointwise, channel_bias):
    _, channels, rows_x, rows_y, length_z = activations.shape
    plan = Plan(channels, rows_x, rows_y, length_z, lax.axis_size("gx"), lax.axis_size("gy"))
    calls = Calls(plan)
    act = activations.reshape(channels, rows_x * rows_y, length_z)
    cot = cotangent.reshape(channels, rows_x * rows_y, length_z)
    weights = spectral_weights.reshape(plan.pairs, channels, channels, MODES)
    mixing = pointwise[0]
    third, third_t = jnp.asarray(plan.third), jnp.asarray(plan.third_t)
    second, second_t = jnp.asarray(plan.second), jnp.asarray(plan.second_t)
    first, first_t = jnp.asarray(plan.first), jnp.asarray(plan.first_t)
    segment = lax.axis_index("segment")
    segments = lax.axis_size("segment")
    half = lax.axis_index("gy")

    def flags(turn):
        return jnp.stack([half, (segment == segments - 1 - turn).astype(jnp.int32)])

    wire = calls.over_blocks(
        input_kernel, "input_modes", flags(0), (act, third, second),
        [calls.field_block, calls.third, calls.second], calls.wire_block, calls.wire_shape, [calls.total],
    )
    input_modes, wire = calls.whole(
        functools.partial(spectral_kernel, plan, False), "mix_inputs", (exchange(wire), weights, first, first_t),
        (calls.modes_shape, calls.wire_shape),
    )
    wire, slope, local = calls.over_blocks(
        first_kernel, "first_signal", flags(0),
        (mixing, channel_bias, act, cot, exchange(wire), third, third_t, second, second_t),
        [calls.small, calls.small, calls.field_block, calls.field_block, calls.wire_block, calls.third, calls.third_t,
         calls.second, calls.second_t],
        [calls.wire_block, calls.field_block, calls.field_block],
        [calls.wire_shape, calls.field_shape(F32), calls.field_shape(BF16)],
        [calls.total, calls.spectrum, calls.field, calls.fields],
    )
    kept_grad = kept_modes = None
    for turn in range(segments - 1):
        active = segment == segments - 1 - turn
        other_local = from_behind(local, -1)
        modes, mixed = calls.whole(
            functools.partial(mixing_kernel, plan), "mix_signal", (exchange(wire), weights, first),
            (calls.modes_shape, calls.modes_shape),
        )
        kept_modes = modes if kept_modes is None else jnp.where(active, modes, kept_modes)
        wire = calls.whole(
            functools.partial(spread_kernel, plan), "spread_signal", (mixed, from_behind(mixed, -1), first_t),
            calls.wire_shape, flags(turn),
        )
        wire, grad, local = calls.over_blocks(
            middle_kernel, "next_signal", flags(turn),
            (mixing, local, other_local, slope, exchange(wire), third, third_t, second, second_t),
            [calls.small, calls.field_block, calls.field_block, calls.field_block, calls.wire_block, calls.third,
             calls.third_t, calls.second, calls.second_t],
            [calls.wire_block, calls.field_block, calls.field_block],
            [calls.wire_shape, calls.field_shape(BF16), calls.field_shape(BF16)],
            [calls.total, calls.spectrum, calls.field, calls.fields],
        )
        kept_grad = grad if kept_grad is None else jnp.where(active, grad, kept_grad)
    modes, wire = calls.whole(
        functools.partial(spectral_kernel, plan, True), "mix_last", (exchange(wire), weights, first, first_t),
        (calls.modes_shape, calls.wire_shape),
    )
    if kept_modes is not None:
        modes = jnp.where(segment == 0, modes, kept_modes)
    weight_grad = input_modes[:, :, None, :] * modes[:, None, :, :]
    grad = calls.over_blocks(
        last_kernel, "last_grad", flags(segments - 1),
        (local, local if kept_grad is None else kept_grad, exchange(wire), third_t, second_t),
        [calls.field_block, calls.field_block, calls.wire_block, calls.third_t, calls.second_t],
        calls.field_block, calls.field_shape(BF16), [calls.spectrum, calls.field],
    )
    return (
        grad.reshape(activations.shape),
        weight_grad.reshape(spectral_weights.shape),
    )


def solution(mesh):
    return jax.shard_map(
        body,
        mesh=mesh,
        in_specs=(
            P("segment", "groups", "gx", "gy", None),
            P("groups", "gx", "gy", None),
            P("segment", "gy", "gx", None, None, None),
            P("segment", None, None),
            P("segment", None),
        ),
        out_specs=(
            P("segment", "groups", "gx", "gy", None),
            P("segment", "gy", "gx", "groups", None, None),
        ),
        check_vma=False,
    )
```

time: 450 us -> 194 us (0.43); the launches traced: 441 us -> 193 us
  waiting for transfers between devices: 144 us -> 54.3 us
  matrix products: 79.5 us -> 0 us
  Pallas kernels: 0 us -> 54.1 us
  other arithmetic: 53.9 us -> 3.73 us
  local copies, waits for them, and re-layouts: 55.7 us -> 14.3 us
  starting transfers between devices: 26.8 us -> 9.77 us
  between operations: 14.6 us -> 0.87 us
  blocking collectives: 66.3 us -> 56.2 us
    dot_general x18 -> x0, matrix products: 79.5 us -> none  [the longest x3 30.1 us: analyse(): third = jnp.einsum('ixyz,cz->cixy', field, along_z, precision=highest)]
    all_to_all x4 -> x2, waiting for transfers between devices: 76.7 us -> 16.3 us  [exchange(): return lax.all_to_all(wire, PLANE, split_axis=0, concat_axis=0, tiled=True)]
    pallas_call x0 -> x8, Pallas kernels: none -> 54.1 us  [the longest x4 50.6 us: over_blocks(): pl.pallas_call(functools.partial(kernel, self.plan), grid_spec=pltpu.Pref...]
    all_to_all x6 -> x0, other arithmetic: 23.5 us -> none  [the longest x3 11.8 us: synthesise(): lax.all_to_all(spread, 'gx', split_axis=2, concat_axis=0, tiled=True)]
    reduce_sum x3 -> x0, other arithmetic: 21.6 us -> none  [channel_mix(): return jnp.sum(matrix[:, :, None, None, None] * field[None], axis=1)]
    reduce_scatter x3 -> x0, waiting for transfers between devices: 20.4 us -> none  [analyse(): lax.psum_scatter(jnp.einsum('ciay,jy->jcia', partial_value, along_y, prec...]
    unnamed x39 -> x46, local copies, waits for them, and re-layouts: 32.2 us -> 14.3 us
    all_to_all x4 -> x2, starting transfers between devices: 24.8 us -> 7.2 us  [exchange(): return lax.all_to_all(wire, PLANE, split_axis=0, concat_axis=0, tiled=True)]
  transfers between devices with their start and end apart: 8 -> 4, of which waited for: 8 -> 3; matrix products, arithmetic and copies ran while one was open for 6% -> 2% of each run, Pallas kernels for 0% -> 1%
where the time goes in v1:
time: 194 us; the launch traced here: 193 us
  blocking collectives  56.2 us (29%)
  waiting for transfers between devices  54.3 us (28%)
  Pallas kernels  54.1 us (28%)
  local copies, waits for them, and re-layouts  14.3 us (7%)
  starting transfers between devices  9.77 us (5%)
  other arithmetic  3.73 us (2%)
    all_to_all x4, blocking collectives, exchange(): return lax.all_to_all(wire, PLANE, split_axis=0, concat_axis=0, tiled=True)  56.2 us
    pallas_call x4, Pallas kernels, over_blocks(): pl.pallas_call(functools.partial(kernel, self.plan), grid_spec=pltpu.Pref...  50.6 us
    ppermute x2, waiting for transfers between devices, from_behind(): return lax.ppermute(block, 'segment', route)  37.9 us
    all_to_all x2, waiting for transfers between devices, exchange(): return lax.all_to_all(wire, PLANE, split_axis=0, concat_axis=0, tiled=True)  16.3 us
    unnamed x46, local copies, waits for them, and re-layouts  14.3 us
    all_to_all x2, starting transfers between devices, exchange(): return lax.all_to_all(wire, PLANE, split_axis=0, concat_axis=0, tiled=True)  7.2 us
  transfers between devices with their start and end apart: 4, of which 3 were waited for; matrix products, arithmetic and copies ran while one was open for 2% of the time, Pallas kernels for 1%

profile of v1, /device:TPU:0, one launch (start us, length us, event | category | flops | bytes accessed | tf_op | source)
XLA Modules:
  0.0 193.2 jit_solution(16170172791748510362)
XLA Ops:
  0.7 2.2 %copy-done.1 = bf16[2,4,2,512,256]{4,3,2,1,0:T(8,128)(2,1)S(1)} copy-done((bf16[2,4,2,512,256]{4,3,2,1,0:T(8,128)(2,1)S(1)}, bf16[2,4,2,512,256]{4,3,2,1,0:T(8,128)(2,1)}, u32[]{:S(2)}) %copy-start.1) | copy-done | bytes 4194328
  2.9 1.2 copy-done.4
  4.1 1.6 copy-done.6
  5.7 6.1 %input_modes.1 = bf16[16,16,512]{2,1,0:T(8,128)(2,1)S(1)} custom-call(s32[2]{0:T(128)S(1)} %pad_add_fusion.1.flags, bf16[8,1024,128]{2,1,0:T(8,128)(2,1)S(1)} %bitcast.13, bf16[2,1024,256]{2,1,0:T(8,128)(2,1)S(1)} %copy-done.4, bf16[2,4,2,512,256]{4,3,2,1,0:T(8,128)(2,1)S(1)} %copy-done.1), custom_call_target="tpu_custom_call" | custom-call | tf_op jit(solution)/shard_map/input_modes/pallas_call | solution.py:335
  11.9 17.4 %all_to_all.30.wire_ref = bf16[16,16,512]{2,1,0:T(8,128)(2,1)S(1)} all-to-all(bf16[16,16,512]{2,1,0:T(8,128)(2,1)S(1)} %input_modes.1), channel_id=1, replica_groups=mesh['groups'=1,'gx'=8,'gy'=2,'segment'=2] {'gx','gy'}, dimensions={0} | all-to-all | bytes 524288 | tf_op jit(solution)/shard_map/all_to_all | solution.py:356
  30.0 12.8 %all_to_all.31.wire_in_ref = bf16[16,16,512]{2,1,0:T(8,128)(2,1)S(1)} all-to-all(bf16[16,16,512]{2,1,0:T(8,128)(2,1)S(1)} %get-tuple-element.14), channel_id=1, replica_groups=mesh['groups'=1,'gx'=8,'gy'=2,'segment'=2] {'gx','gy'}, dimensions={0} | all-to-all | bytes 524288 | tf_op jit(solution)/shard_map/all_to_all | solution.py:356
  42.9 21.5 %first_signal.1 = (bf16[16,16,512]{2,1,0:T(8,128)(2,1)S(1)}, f32[8,1024,128]{2,1,0:T(8,128)S(1)}, bf16[8,1024,128]{2,1,0:T(8,128)(2,1)S(1)}) custom-call(s32[2]{0:T(128)S(1)} %pad_add_fusion.1.flags, f32[8,8]{1,0:T(8,128)S(1)} %bitcast.17, f32[1,8]{1,0:T(1,128)S(1)} %copy-done.22, bf16[8,1024,128]{2,1,0:T(8,128)(2,1)S(1)} %bitcast.14, ...), custom_call_target="tpu_custom_call" | custom-call | tf_op jit(solution)/shard_map/first_signal/pallas_call | solution.py:335
  64.4 1.3 collective-permute-start
  65.7 12.8 %all_to_all.32.wire_ref = bf16[16,16,512]{2,1,0:T(8,128)(2,1)S(1)} all-to-all(bf16[16,16,512]{2,1,0:T(8,128)(2,1)S(1)} %get-tuple-element.17), channel_id=1, replica_groups=mesh['groups'=1,'gx'=8,'gy'=2,'segment'=2] {'gx','gy'}, dimensions={0} | all-to-all | bytes 524288 | tf_op jit(solution)/shard_map/all_to_all | solution.py:356
  80.1 1.3 collective-permute-start.1
  81.4 37.9 %collective-permute-done.1.other_ref = f32[64,8,32]{2,1,0:T(8,128)S(1)} collective-permute-done((f32[64,8,32]{2,1,0:T(8,128)S(1)}, f32[64,8,32]{2,1,0:T(8,128)S(1)}, u32[]{:S(2)}, u32[]{:S(2)}) %collective-permute-start.1) | collective-permute-done | bytes 65568 | tf_op jit(solution)/shard_map/ppermute | solution.py:362
  120.1 13.2 %all_to_all.33.wire_in_ref = bf16[16,16,512]{2,1,0:T(8,128)(2,1)S(1)} all-to-all(bf16[16,16,512]{2,1,0:T(8,128)(2,1)S(1)} %spread_signal.1), channel_id=1, replica_groups=mesh['groups'=1,'gx'=8,'gy'=2,'segment'=2] {'gx','gy'}, dimensions={0} | all-to-all | bytes 524288 | tf_op jit(solution)/shard_map/all_to_all | solution.py:356
  133.3 16.3 %next_signal.1 = (bf16[16,16,512]{2,1,0:T(8,128)(2,1)S(1)}, bf16[8,1024,128]{2,1,0:T(8,128)(2,1)S(1)}, bf16[8,1024,128]{2,1,0:T(8,128)(2,1)S(1)}) custom-call(s32[2]{0:T(128)S(1)} %pad_add_fusion.1.flags, f32[8,8]{1,0:T(8,128)S(1)} %bitcast.18, bf16[8,1024,128]{2,1,0:T(8,128)(2,1)S(1)} %get-tuple-element.15.own_ref, ...), custom_call_target="tpu_custom_call" | custom-call | tf_op jit(solution)/shard_map/next_signal/pallas_call | solution.py:335
  149.7 1.3 copy-done.10
  151.0 1.3 copy-done.12
  153.0 3.5 %all-to-all-start.4 = ((bf16[16,16,512]{2,1,0:T(8,128)(2,1)}), bf16[16,16,512]{2,1,0:T(8,128)(2,1)S(1)}, u32[]{:S(2)}, u32[]{:S(2)}) async-start(bf16[16,16,512]{2,1,0:T(8,128)(2,1)} %copy-done.17), calls=%async_computation.4 | async-start | bytes 524288 | tf_op jit(solution)/shard_map/all_to_all | solution.py:356
  156.6 9.9 %all-to-all-done.4.wire_ref = bf16[16,16,512]{2,1,0:T(8,128)(2,1)S(1)} async-done(((bf16[16,16,512]{2,1,0:T(8,128)(2,1)}), bf16[16,16,512]{2,1,0:T(8,128)(2,1)S(1)}, u32[]{:S(2)}, u32[]{:S(2)}) %all-to-all-start.4) | async-done | bytes 262176 | tf_op jit(solution)/shard_map/all_to_all | solution.py:356
  166.6 1.1 mix_last.1
  169.1 3.7 %all-to-all-start.5 = ((bf16[16,16,512]{2,1,0:T(8,128)(2,1)}), bf16[16,16,512]{2,1,0:T(8,128)(2,1)S(1)}, u32[]{:S(2)}, u32[]{:S(2)}) async-start(bf16[16,16,512]{2,1,0:T(8,128)(2,1)} %copy-done.18), calls=%async_computation.5 | async-start | bytes 524288 | tf_op jit(solution)/shard_map/all_to_all | solution.py:356
  173.8 2.6 %broadcast_multiply_fusion = f32[1,16,4,8,8,32]{5,4,3,2,1,0:T(8,128)} fusion(f32[16,4,8,32]{3,2,1,0:T(8,128)S(1)} %bitcast.20, f32[16,4,8,32]{3,2,1,0:T(8,128)} %bitcast.16), kind=kLoop, calls=%fused_computation | loop fusion | flops 131072 | bytes 655360 | tf_op jit(solution)/shard_map/mul | solution.py:429
  176.4 6.4 %all-to-all-done.5.wire_in_ref = bf16[16,16,512]{2,1,0:T(8,128)(2,1)S(1)} async-done(((bf16[16,16,512]{2,1,0:T(8,128)(2,1)}), bf16[16,16,512]{2,1,0:T(8,128)(2,1)S(1)}, u32[]{:S(2)}, u32[]{:S(2)}) %all-to-all-start.5) | async-done | bytes 262176 | tf_op jit(solution)/shard_map/all_to_all | solution.py:356
  182.8 2.2 %copy-done = bf16[2,4,2,256,512]{4,3,2,1,0:T(8,128)(2,1)S(1)} copy-done((bf16[2,4,2,256,512]{4,3,2,1,0:T(8,128)(2,1)S(1)}, bf16[2,4,2,256,512]{4,3,2,1,0:T(8,128)(2,1)}, u32[]{:S(2)}) %copy-start) | copy-done | bytes 4194328
  185.0 1.6 copy-done.13
  186.6 6.6 %last_grad.1 = bf16[8,1024,128]{2,1,0:T(8,128)(2,1)} custom-call(s32[2]{0:T(128)S(1)} %pad_add_fusion.flags, bf16[8,1024,128]{2,1,0:T(8,128)(2,1)S(1)} %copy-done.13, bf16[8,1024,128]{2,1,0:T(8,128)(2,1)S(1)} %copy-done.11, bf16[16,16,512]{2,1,0:T(8,128)(2,1)S(1)} %all-to-all-done.5.wire_in_ref, bf16[2,256,1024]{2,1,0:T(8,128)(2,1)S(1)} %copy-done.3, ...), custom_call_target="tpu_custom_call" | custom-call | tf_op jit(solution)/shard_map/last_grad/pallas_call | solution.py:335
  (46 shorter events, 6.4 us)
Async XLA Ops:
  0.7 2.2 %copy-start.1 = (bf16[2,4,2,512,256]{4,3,2,1,0:T(8,128)(2,1)S(1)}, bf16[2,4,2,512,256]{4,3,2,1,0:T(8,128)(2,1)}, u32[]{:S(2)}) copy-start(bf16[2,4,2,512,256]{4,3,2,1,0:T(8,128)(2,1)} %constant.24.clone.second_ref) | copy-start | bytes 12582916
  2.9 1.2 copy-start.4
  4.1 1.6 copy-start.6
  5.7 23.5 %copy-start.2 = (f32[1,16,4,8,8,32]{5,4,3,2,1,0:T(8,128)S(1)}, f32[1,16,4,8,8,32]{5,4,3,2,1,0:T(8,128)}, u32[]{:S(2)}) copy-start(f32[1,16,4,8,8,32]{5,4,3,2,1,0:T(8,128)} %param.13) | copy-start | bytes 1572868
  5.7 23.5 %copy-start.14 = (bf16[2,128,32]{2,1,0:T(8,128)(2,1)S(1)}, bf16[2,128,32]{2,1,0:T(8,128)(2,1)}, u32[]{:S(2)}) copy-start(bf16[2,128,32]{2,1,0:T(8,128)(2,1)} %constant.27.clone.first_t_ref) | copy-start | bytes 49156
  5.7 23.5 %copy-start.15 = (bf16[2,32,256]{2,1,0:T(8,128)(2,1)S(1)}, bf16[2,32,256]{2,1,0:T(8,128)(2,1)}, u32[]{:S(2)}) copy-start(bf16[2,32,256]{2,1,0:T(8,128)(2,1)} %constant.26.clone.first_ref) | copy-start | bytes 98308
  5.7 37.1 %copy-start.7 = (bf16[1,8,16,64,128]{4,3,2,1,0:T(8,128)(2,1)S(1)}, bf16[1,8,16,64,128]{4,3,2,1,0:T(8,128)(2,1)}, u32[]{:S(2)}) copy-start(bf16[1,8,16,64,128]{4,3,2,1,0:T(8,128)(2,1)} %param.11) | copy-start | bytes 6291460
  5.7 37.1 %copy-start.9 = (bf16[8,16,64,128]{3,2,1,0:T(8,128)(2,1)S(1)}, bf16[8,16,64,128]{3,2,1,0:T(8,128)(2,1)}, u32[]{:S(2)}) copy-start(bf16[8,16,64,128]{3,2,1,0:T(8,128)(2,1)} %param.12) | copy-start | bytes 6291460
  11.8 31.0 %copy-start.3 = (bf16[2,256,1024]{2,1,0:T(8,128)(2,1)S(1)}, bf16[2,256,1024]{2,1,0:T(8,128)(2,1)}, u32[]{:S(2)}) copy-start(bf16[2,256,1024]{2,1,0:T(8,128)(2,1)} %constant.23.clone.third_t_ref) | copy-start | bytes 3145732
  11.8 31.0 %copy-start.5 = (bf16[2,1024,256]{2,1,0:T(8,128)(2,1)S(1)}, bf16[2,1024,256]{2,1,0:T(8,128)(2,1)}, u32[]{:S(2)}) copy-start(bf16[2,1024,256]{2,1,0:T(8,128)(2,1)} %constant.22.clone.third_ref) | copy-start | bytes 3145732
  11.9 31.0 %copy-start.21 = (f32[1,8,8]{2,1,0:T(8,128)S(1)}, f32[1,8,8]{2,1,0:T(8,128)}, u32[]{:S(2)}) copy-start(f32[1,8,8]{2,1,0:T(8,128)} %param.14) | copy-start | bytes 772
  11.9 31.0 %copy-start.22 = (f32[1,8]{1,0:T(1,128)S(1)}, f32[1,8]{1,0:T(1,128)}, u32[]{:S(2)}) copy-start(f32[1,8]{1,0:T(1,128)} %bias_ref.1) | copy-start | bytes 100
  30.0 12.8 %copy-start.16 = (f32[64,8,32]{2,1,0:T(8,128)}, f32[64,8,32]{2,1,0:T(8,128)S(1)}, u32[]{:S(2)}) copy-start(f32[64,8,32]{2,1,0:T(8,128)S(1)} %get-tuple-element.23) | copy-start | bytes 196612
  64.4 68.9 %copy-start.8 = (f32[8,1024,128]{2,1,0:T(8,128)}, f32[8,1024,128]{2,1,0:T(8,128)S(1)}, u32[]{:S(2)}) copy-start(f32[8,1024,128]{2,1,0:T(8,128)S(1)} %get-tuple-element.16.slope_ref) | copy-start | bytes 12582916
  64.4 68.9 %collective-permute-start = (bf16[8,1024,128]{2,1,0:T(8,128)(2,1)S(1)}, bf16[8,1024,128]{2,1,0:T(8,128)(2,1)S(1)}, u32[]{:S(2)}, u32[]{:S(2)}) collective-permute-start(bf16[8,1024,128]{2,1,0:T(8,128)(2,1)S(1)} %get-tuple-element.15.own_ref), channel_id=1, source_target_pairs={{1,0},{3,2},{5,4},{7,6},{9,8},{11,10},{13,12},{15,14},{17,16},{19,... | collective-permute-start | bytes 6291464 | tf_op jit(solution)/shard_map/ppermute | solution.py:362
  80.1 39.2 %collective-permute-start.1 = (f32[64,8,32]{2,1,0:T(8,128)S(1)}, f32[64,8,32]{2,1,0:T(8,128)S(1)}, u32[]{:S(2)}, u32[]{:S(2)}) collective-permute-start(f32[64,8,32]{2,1,0:T(8,128)S(1)} %get-tuple-element.18.own_ref), channel_id=1, source_target_pairs={{1,0},{3,2},{5,4},{7,6},{9,8},{11,10},{13,12},{15,14},{17,16},{19,... | collective-permute-start | bytes 196616 | tf_op jit(solution)/shard_map/ppermute | solution.py:362
  149.6 1.4 copy-start.10
  151.0 1.3 copy-start.12
  153.0 13.5 %all-to-all-start.4 = ((bf16[16,16,512]{2,1,0:T(8,128)(2,1)}), bf16[16,16,512]{2,1,0:T(8,128)(2,1)S(1)}, u32[]{:S(2)}, u32[]{:S(2)}) async-start(bf16[16,16,512]{2,1,0:T(8,128)(2,1)} %copy-done.17), calls=%async_computation.4 | async-start | bytes 524288 | tf_op jit(solution)/shard_map/all_to_all | solution.py:356
  167.7 0.7 copy-start.18
  169.1 13.7 %copy-start.11 = (bf16[8,1024,128]{2,1,0:T(8,128)(2,1)S(1)}, bf16[8,1024,128]{2,1,0:T(8,128)(2,1)}, u32[]{:S(2)}) copy-start(bf16[8,1024,128]{2,1,0:T(8,128)(2,1)} %copy-done.10) | copy-start | bytes 6291460
  169.1 13.7 %all-to-all-start.5 = ((bf16[16,16,512]{2,1,0:T(8,128)(2,1)}), bf16[16,16,512]{2,1,0:T(8,128)(2,1)S(1)}, u32[]{:S(2)}, u32[]{:S(2)}) async-start(bf16[16,16,512]{2,1,0:T(8,128)(2,1)} %copy-done.18), calls=%async_computation.5 | async-start | bytes 524288 | tf_op jit(solution)/shard_map/all_to_all | solution.py:356
  182.8 2.2 %copy-start = (bf16[2,4,2,256,512]{4,3,2,1,0:T(8,128)(2,1)S(1)}, bf16[2,4,2,256,512]{4,3,2,1,0:T(8,128)(2,1)}, u32[]{:S(2)}) copy-start(bf16[2,4,2,256,512]{4,3,2,1,0:T(8,128)(2,1)} %constant.25.clone.second_t_ref) | copy-start | bytes 12582916
  185.0 1.6 copy-start.13
  (3 other events, 2.1 us)

commit v2 on v0

v2 whole, which is shorter than its diff:
```python
import functools
import math

import jax
import jax.numpy as jnp
import ml_dtypes
import numpy as np
from jax import lax
from jax.experimental import pallas as pl
from jax.experimental.pallas import tpu as pltpu
from jax.sharding import PartitionSpec as P

MODES = 32
LANES = 128
PLANE = ("gx", "gy")
WHOLE = ("segment",) + PLANE
F32 = jnp.float32
BF16 = jnp.bfloat16
VMEM_LIMIT = 28 * 1024 * 1024


def trig_basis(length):
    half = MODES // 2
    points = np.arange(length)[None, :]
    freqs = np.arange(half)[:, None]
    angle = 2.0 * math.pi / length
    rows = np.concatenate(
        [np.cos((freqs * points % length) * angle), np.sin(((freqs + 1) * points % length) * angle)], axis=0
    )
    scales = np.where(np.arange(MODES) == 0, 1.0 / math.sqrt(length), math.sqrt(2.0 / length))
    return rows * scales[:, None]


def high_low(values):
    high = values.astype(np.float32).astype(ml_dtypes.bfloat16)
    low = (values - high.astype(np.float64)).astype(np.float32).astype(ml_dtypes.bfloat16)
    return np.stack([high, low])


class Plan:
    def __init__(self, channels, rows_x, rows_y, length_z, count_x, count_y):
        self.channels, self.length_z = channels, length_z
        self.count_x, self.count_y = count_x, count_y
        self.devices = count_x * count_y
        share = rows_x // count_y
        self.side = share * rows_y
        self.rows = self.side * count_y
        self.block = min(128, self.side // 2)
        self.steps = self.side // self.block // 2
        self.pieces = self.steps * count_y
        self.piece = self.rows // self.pieces
        self.own_third = MODES // count_x
        self.own_second = MODES // count_y
        self.width = self.own_third * channels
        self.parts = 2 if share <= 8 and self.own_second // 2 * self.width >= LANES else 1
        padded = 8 if self.parts == 2 else -(-share // 16) * 16
        self.in_part = self.own_second // self.parts
        self.slot = self.parts * padded
        self.per_tile = LANES // self.width
        self.tiles = self.in_part // self.per_tile
        self.groups = MODES // self.parts // self.per_tile
        self.halves = MODES * channels // LANES
        self.lanes = self.in_part * self.width
        self.wire = (self.devices, self.slot, self.lanes)
        self.modes = self.own_second * self.own_third
        self.spectrum = (MODES * padded, MODES * channels)
        self.field = (channels, self.rows, length_z)
        along_x = trig_basis(rows_x * count_x).reshape(MODES, self.devices, share)
        along_y = trig_basis(rows_y * count_y).reshape(MODES, count_y, rows_y)
        along_z = trig_basis(length_z)
        third = np.einsum("ik,cz->izck", np.eye(channels), along_z)
        third = third.reshape(channels * length_z, MODES * channels)
        self.third = high_low(third)
        self.third_t = high_low(third.T)
        order = [[(own + k) % count_y for k in range(count_y)] for own in range(count_y)]
        slabs = along_y[:, np.array(order)].reshape(count_y, self.parts, self.in_part, count_y, count_y, rows_y)
        second = np.einsum("opqdsy,xk->doqpxsky", slabs, np.eye(padded, share))
        second = second.reshape(count_y, MODES * padded, self.rows)
        self.second = np.moveaxis(high_low(second), 0, 1)
        self.second_t = np.moveaxis(high_low(np.swapaxes(second, 1, 2)), 0, 1)
        spread = np.zeros((MODES, self.devices, padded))
        spread[:, :, :share] = along_x
        first = np.einsum("pq,adx->padqx", np.eye(self.parts), spread)
        first = first.reshape(self.parts * MODES, self.devices * self.slot)
        self.first = high_low(first)
        self.first_t = high_low(first.T)


def dot(a, b):
    return jnp.dot(a, b, preferred_element_type=F32)


def join(arrays, axis):
    return jnp.concatenate(arrays, axis=axis)


def split(value):
    high = value.astype(BF16)
    return high, (value - high.astype(F32)).astype(BF16)


def swap_groups(parts, width):
    parts = list(parts)
    lane = lax.broadcasted_iota(jnp.int32, parts[0].shape, 1)
    bit = len(parts) // 2
    while bit:
        shift = bit * width
        low = (lane // shift) % 2 == 0
        for at in range(len(parts)):
            if at & bit:
                continue
            a, b = parts[at], parts[at | bit]
            parts[at] = jnp.where(low, a, pltpu.roll(b, shift, 1))
            parts[at | bit] = jnp.where(low, pltpu.roll(a, LANES - shift, 1), b)
        bit //= 2
    return parts


def pack_wire(plan, total_ref, wire_ref):
    slot, group = plan.slot, plan.per_tile
    for half in range(plan.halves):
        for block in range(plan.groups):
            parts = [
                total_ref[pl.ds((block * group + j) * slot, slot), pl.ds(half * LANES, LANES)] for j in range(group)
            ]
            parts = swap_groups(parts, plan.width)
            owner_y, tile = block // plan.tiles, block % plan.tiles
            for g in range(group):
                target = (half * group + g) * plan.count_y + owner_y
                wire_ref[target, :, pl.ds(tile * LANES, LANES)] = parts[g].astype(BF16)


def unpack_wire(plan, load, spectrum_ref):
    slot, group = plan.slot, plan.per_tile
    for half in range(plan.halves):
        for block in range(plan.groups):
            owner_y, tile = block // plan.tiles, block % plan.tiles
            parts = [
                load((half * group + g) * plan.count_y + owner_y, pl.ds(tile * LANES, LANES)).astype(F32)
                for g in range(group)
            ]
            parts = swap_groups(parts, plan.width)
            for j in range(group):
                spectrum_ref[pl.ds((block * group + j) * slot, slot), pl.ds(half * LANES, LANES)] = parts[j].astype(BF16)


def blocks_of(wire_ref):
    return lambda device, lanes: wire_ref[device, :, lanes]


def synthesise(plan, load, second_t, spectrum_ref, inner_ref):
    unpack_wire(plan, load, spectrum_ref)
    spectrum = spectrum_ref[...]
    inner_ref[...] = dot(join([second_t(0), second_t(1)], 1), join([spectrum, spectrum], 0)).astype(BF16)


def piece_rows(plan, k):
    return pl.ds(pl.multiple_of(k * plan.piece, 16), plan.piece)


def run_blocks(plan, inner_ref, third_t_ref, slots, work, third_ref=None, sums_ref=None, leaving=()):
    fields, signals = slots[:2], slots[2:]
    per_side = plan.side // plan.block
    count = per_side * plan.count_y

    def rows_of(k):
        return pl.ds(pl.multiple_of(k * plan.block, 16), plan.block)

    def cells(k, ref):
        inner = inner_ref[rows_of(k), :]
        ref[...] = dot(join([inner, inner], 1), join([third_t_ref[0], third_t_ref[1]], 0))

    def sums(k, ref):
        if third_ref is not None:
            values = ref[...]
            sums_ref[rows_of(k), :] = dot(join([values, values], 1), join([third_ref[0], third_ref[1]], 0))

    cells(0, fields[0])
    if third_ref is not None:
        signals[1][...] = jnp.zeros_like(signals[1])
    for y in range(plan.count_y):

        def one(step, carry):
            here = 2 * step
            k = y * per_side + here
            sums(lax.rem(k + count - 1, count), signals[1])
            cells(k + 1, fields[1])
            work(y, rows_of(here), rows_of(k), fields[0], signals[0])
            sums(k, signals[0])
            cells(lax.rem(k + 2, count), fields[0])
            work(y, rows_of(here + 1), rows_of(k + 1), fields[1], signals[1])
            piece = y * plan.steps + step
            for ref, target, sems in leaving:
                rows = piece_rows(plan, piece)
                pltpu.make_async_copy(ref.at[:, rows], target.at[:, rows], sems.at[piece]).start()
            return carry

        lax.fori_loop(0, plan.steps, one, 0)
    sums(count - 1, signals[1])


def wait_pieces(plan, leaving):
    for ref, target, sems in leaving:
        for p in range(plan.pieces):
            rows = piece_rows(plan, p)
            pltpu.make_async_copy(ref.at[:, rows], target.at[:, rows], sems.at[p]).wait()


def finish(plan, sums_ref, second, total_ref, wire_ref):
    high, low = split(sums_ref[...])
    total_ref[...] = dot(join([second(0), second(0), second(1)], 1), join([high, low, high], 0))
    pack_wire(plan, total_ref, wire_ref)


def gelu_slope(value):
    size = jnp.abs(value)
    t = 1.0 / (1.0 + (0.3275911 * 0.7071067811865476) * size)
    poly = 0.5 * 1.061405429
    for c in (-1.453152027, 1.421413741, -0.284496736, 0.254829592):
        poly = poly * t + 0.5 * c
    bell = jnp.exp(-0.5 * value * value)
    tail = bell * (poly * t - 0.3989422804014327 * size)
    return jnp.where(value >= 0, 1.0 - tail, tail)


def each_chunk(total, chunk, work):
    def step(k, carry):
        work(pl.ds(pl.multiple_of(k * chunk, chunk), chunk))
        return carry

    lax.fori_loop(0, total // chunk, step, 0)


def shifted(rows, by):
    return pl.ds(pl.multiple_of(rows.start + by, 16), rows.size)


def lanes_of(plan, channel):
    return pl.ds(channel * plan.length_z, plan.length_z)


def mixed_with(plan, mixing_ref, values, out, transposed):
    total = None
    for k, value in enumerate(values):
        term = (mixing_ref[k, out] if transposed else mixing_ref[out, k]) * value
        total = term if total is None else total + term
    return total


def starts(copies, sems):
    copies = [pltpu.make_async_copy(source, target, sems.at[k]) for k, (source, target) in enumerate(copies)]
    for copy in copies:
        copy.start()
    return copies


def waits(copies):
    for copy in copies:
        copy.wait()


def side(plan, k):
    return pl.ds(k * plan.side, plan.side)


def own_side(plan, flags, k=0):
    at = flags[0] if k == 0 else 1 - flags[0]
    return pl.ds(pl.multiple_of(at * plan.side, 16), plan.side)


def input_kernel(
    plan, flags, act_hbm, third_hbm, second_hbm, other_ref, wire_ref, own_ref, third_ref, second_ref, sums_ref,
    total_ref, sems,
):
    copies = starts(
        [(third_hbm, third_ref), (act_hbm.at[:, own_side(plan, flags)], own_ref),
         (second_hbm.at[flags[0]], second_ref)], sems,
    )
    waits(copies[:2])
    fields = join([join([ref[i] for i in range(plan.channels)], 1) for ref in (own_ref, other_ref)], 0)
    sums_ref[...] = dot(join([fields, fields], 1), join([third_ref[0], third_ref[1]], 0))
    waits(copies[2:])
    finish(plan, sums_ref, lambda k: second_ref[k], total_ref, wire_ref)


CHUNK = 32


def chunks_of(plan, *spans):
    for at in range(0, plan.block, CHUNK):
        yield *(pl.ds(pl.multiple_of(rows.start + at, 16), CHUNK) for rows in spans), pl.ds(at, CHUNK)


def cells_of(plan, flags, own_ref, other_ref):
    def load(y, channel, rows):
        if y == 0:
            rows = pl.ds(pl.multiple_of(flags[0] * plan.side + rows.start, 16), rows.size)
        return (other_ref if y else own_ref)[channel, rows, :].astype(F32)

    return load


def slopes(plan, mixing_ref, load_input, y, there, here, cells_ref):
    inputs = [load_input(y, i, there) for i in range(plan.channels)]
    for o in range(plan.channels):
        pre = mixed_with(plan, mixing_ref, inputs, o, False) + mixing_ref[o, plan.channels]
        yield gelu_slope(pre + cells_ref[here, lanes_of(plan, o)])


def first_kernel(
    plan, segments, flags, mixing_ref, act_ref, cot_ref, act_other_ref, cot_other_ref, wire_in_ref, third_ref,
    third_t_ref, second_ref, second_t_ref, wire_ref, kept_hbm,
    kept_ref, total_ref, spectrum_ref, inner_ref, sums_ref, field_a, field_b, signal_a, signal_b, sems,
):
    half, last = flags[0], flags[1] == segments - 1
    load_input = cells_of(plan, flags, act_ref, act_other_ref)
    load_cotangent = cells_of(plan, flags, cot_ref, cot_other_ref)
    synthesise(plan, blocks_of(wire_in_ref), lambda k: second_t_ref[half, k], spectrum_ref, inner_ref)
    slots = [field_a, field_b, signal_a, signal_b]
    leaving = [(kept_ref, kept_hbm, sems)]

    @pl.when(last)
    def _():
        def work(y, in_side, rows, cells, out):
            for there, everywhere, here in chunks_of(plan, in_side, rows):
                for o, slope in enumerate(slopes(plan, mixing_ref, load_input, y, there, here, cells)):
                    signal = load_cotangent(y, o, there) * slope
                    kept_ref[o, everywhere, :] = signal
                    out[here, lanes_of(plan, o)] = signal.astype(BF16)

        run_blocks(plan, inner_ref, third_t_ref, slots, work, third_ref, sums_ref, leaving)
        finish(plan, sums_ref, lambda k: second_ref[half, k], total_ref, wire_ref)

    @pl.when(jnp.logical_not(last))
    def _():
        def work(y, in_side, rows, cells, out):
            for there, everywhere, here in chunks_of(plan, in_side, rows):
                for o, slope in enumerate(slopes(plan, mixing_ref, load_input, y, there, here, cells)):
                    kept_ref[o, everywhere, :] = slope

        run_blocks(plan, inner_ref, third_t_ref, slots, work, leaving=leaving)

    wait_pieces(plan, leaving)


def shared_kernel(
    plan, flags, mixing_ref, act_own_ref, act_other_ref, cot_ref, cot_other_ref, wire_ref, third_t_ref, second_t_ref,
    local_hbm, local_ref, spectrum_ref, inner_ref, field_a, field_b, sems,
):
    half = flags[0]
    load_cotangent = cells_of(plan, flags, cot_ref, cot_other_ref)
    synthesise(plan, blocks_of(wire_ref), lambda k: second_t_ref[half, k], spectrum_ref, inner_ref)

    def load_input(y, channel, rows):
        return (act_other_ref if y else act_own_ref)[channel, rows, :].astype(F32)

    def work(y, in_side, rows, cells, out):
        for there, everywhere, here in chunks_of(plan, in_side, rows):
            signals = [
                load_cotangent(y, o, there) * slope
                for o, slope in enumerate(slopes(plan, mixing_ref, load_input, y, there, here, cells))
            ]
            for i in range(plan.channels):
                local_ref[i, everywhere, :] = mixed_with(plan, mixing_ref, signals, i, True)

    leaving = [(local_ref, local_hbm, sems)]
    run_blocks(plan, inner_ref, third_t_ref, [field_a, field_b, None, None], work, leaving=leaving)
    wait_pieces(plan, leaving)


def middle_kernel(
    plan, segments, turn, flags, mixing_ref, local_ref, kept_ref, wire_in_ref, third_ref, third_t_ref, second_ref,
    second_t_ref, wire_ref, local_out_hbm,
    local_out_ref, total_ref, spectrum_ref, inner_ref, sums_ref, field_a, field_b, signal_a, signal_b, sems,
):
    half, segment = flags[0], flags[1]
    active = segments - 1 - turn
    leaving = [(local_out_ref, local_out_hbm, sems)]

    @pl.when(segment < active)
    def _():
        synthesise(plan, lambda device, lanes: wire_in_ref[active * plan.devices + device, :, lanes],
                   lambda k: second_t_ref[half, k], spectrum_ref, inner_ref)

        def work(y, in_side, rows, cells, out):
            for there, here in chunks_of(plan, rows):
                signals = []
                for i in range(plan.channels):
                    grad = local_ref[i, there, :] + cells[here, lanes_of(plan, i)]
                    signals.append(grad * kept_ref[i, there, :])
                    out[here, lanes_of(plan, i)] = signals[i].astype(BF16)
                for i in range(plan.channels):
                    local_out_ref[i, there, :] = mixed_with(plan, mixing_ref, signals, i, True)

        run_blocks(plan, inner_ref, third_t_ref, [field_a, field_b, signal_a, signal_b], work, third_ref, sums_ref,
                   leaving)
        finish(plan, sums_ref, lambda k: second_ref[half, k], total_ref, wire_ref)
        wait_pieces(plan, leaving)

    @pl.when(segment >= active)
    def _():
        if turn == 0:
            def work(rows):
                signals = [kept_ref[o, rows, :] for o in range(plan.channels)]
                for i in range(plan.channels):
                    local_out_ref[i, rows, :] = mixed_with(plan, mixing_ref, signals, i, True)

            each_chunk(plan.rows, 32, work)
            waits(starts([(local_out_ref, local_out_hbm)], sems))
        else:
            waits(starts([(local_ref, local_out_hbm)], sems))


def side_grads(plan, segments, y, flags, local_ref, third_t_ref, second_t_ref, wire_in_ref, kept_wire_ref, grad_ref,
               spectrum_ref, inner_ref, field_ref):
    half, segment = flags[0], flags[1]
    last = (segments - 1) * plan.devices

    def load(device, lanes):
        return jnp.where(segment == 0, wire_in_ref[device, :, lanes], kept_wire_ref[last + device, :, lanes])

    synthesise(plan, load, lambda p: second_t_ref[half, p, side(plan, y), :], spectrum_ref, inner_ref)
    inner = inner_ref[...]
    field_ref[...] = dot(join([inner, inner], 1), join([third_t_ref[0], third_t_ref[1]], 0))

    def work(rows):
        there = shifted(rows, y * plan.side)
        for i in range(plan.channels):
            grad_ref[i, rows, :] = (local_ref[i, there, :] + field_ref[rows, lanes_of(plan, i)]).astype(BF16)

    each_chunk(plan.side, 64, work)


def last_other_kernel(
    plan, segments, flags, local_ref, third_t_ref, second_t_ref, wire_in_ref, kept_wire_ref, input_modes_ref,
    modes_ref, kept_modes_ref, grad_ref, weight_hbm, spectrum_ref, inner_ref, field_ref, sems, weight_ref,
):
    modes = jnp.where(flags[1] == 0, modes_ref[...], kept_modes_ref[...])
    for i in range(plan.channels):
        weight_ref[:, i] = input_modes_ref[:, i : i + 1, :] * modes
    copies = starts([(weight_ref, weight_hbm)], sems)
    side_grads(plan, segments, 1, flags, local_ref, third_t_ref, second_t_ref, wire_in_ref, kept_wire_ref, grad_ref,
               spectrum_ref, inner_ref, field_ref)
    waits(copies)


def last_own_kernel(
    plan, segments, flags, local_ref, third_t_ref, second_t_ref, wire_in_ref, kept_wire_ref, out_hbm,
    spectrum_ref, inner_ref, field_ref, sems, grad_ref,
):
    side_grads(plan, segments, 0, flags, local_ref, third_t_ref, second_t_ref, wire_in_ref, kept_wire_ref, grad_ref,
               spectrum_ref, inner_ref, field_ref)
    waits(starts([(grad_ref, out_hbm.at[:, own_side(plan, flags)])], sems))


def place_kernel(plan, flags, part_hbm, received_ref, out_hbm, sems):
    waits(starts([(received_ref, out_hbm.at[:, own_side(plan, flags, 1)])], sems))


def nothing_kernel(unused, out_hbm):
    pass


def mode_sums(plan, wire_ref, first_ref):
    received = wire_ref[...].reshape(plan.devices * plan.slot, plan.lanes)
    sums = dot(first_ref[0], received) + dot(first_ref[1], received)
    modes = join([sums[p * MODES : (p + 1) * MODES].T for p in range(plan.parts)], 0)
    return modes.reshape(plan.modes, plan.channels, MODES)


def flatten(plan, mixed):
    rows = mixed.reshape(plan.parts, plan.lanes, MODES)
    return join([rows[p].T for p in range(plan.parts)], 0).astype(BF16)


def mix_modes(plan, modes, weights_ref, backward):
    if not backward:
        mixed = weights_ref[:, 0] * modes[:, 0:1, :]
        for i in range(1, plan.channels):
            mixed = mixed + weights_ref[:, i] * modes[:, i : i + 1, :]
        return mixed
    row = lax.broadcasted_iota(jnp.int32, modes.shape, 1)
    mixed = jnp.zeros_like(modes)
    for i in range(plan.channels):
        mixed = jnp.where(row == i, jnp.sum(weights_ref[:, i] * modes, axis=1, keepdims=True), mixed)
    return mixed


def spread_modes(plan, mixed, first_t_ref):
    flat = flatten(plan, mixed)
    return (dot(first_t_ref[0], flat) + dot(first_t_ref[1], flat)).astype(BF16).reshape(plan.wire)


def spectral_kernel(plan, backward, wire_ref, weights_ref, first_ref, first_t_ref, modes_ref, wire_out_ref):
    modes = mode_sums(plan, wire_ref, first_ref)
    modes_ref[...] = modes
    spread = spread_modes(plan, mix_modes(plan, modes, weights_ref, backward), first_t_ref)
    copies = wire_out_ref.shape[0] // plan.devices
    for k in range(copies):
        wire_out_ref[pl.ds(k * plan.devices, plan.devices)] = spread


VMEM = pl.BlockSpec(memory_space=pltpu.VMEM)
SMEM = pl.BlockSpec(memory_space=pltpu.SMEM)
HBM = pl.BlockSpec(memory_space=pltpu.HBM)


def call(kernel, name, args, out_shape, scratch=(), scalars=0, far=0, aliases={}):
    specs = [SMEM] * scalars + [HBM] * far + [VMEM] * (len(args) - scalars - far)
    args = [
        pltpu.with_memory_space_constraint(arg, pltpu.HBM) if spec is HBM else arg for arg, spec in zip(args, specs)
    ]
    outs = out_shape if isinstance(out_shape, tuple) else (out_shape,)
    out_specs = tuple(VMEM if isinstance(out, jax.ShapeDtypeStruct) else HBM for out in outs)
    result = pl.pallas_call(
        kernel, in_specs=specs, out_specs=out_specs, out_shape=outs, scratch_shapes=scratch,
        input_output_aliases=aliases,
        compiler_params=pltpu.CompilerParams(vmem_limit_bytes=VMEM_LIMIT), name=name,
    )(*args)
    return result if isinstance(out_shape, tuple) else result[0]


def exchange(wire, axes=PLANE):
    return lax.all_to_all(wire, axes, split_axis=0, concat_axis=0, tiled=True)


def from_behind(block, distance):
    devices = range(lax.axis_size("segment"))
    route = [(i - distance, i) for i in devices if i - distance in devices]
    return lax.ppermute(block, "segment", route)


def other_core(block):
    return lax.ppermute(block, "gy", [(0, 1), (1, 0)])


def body(activations, cotangent, spectral_weights, pointwise, channel_bias):
    _, channels, rows_x, rows_y, length_z = activations.shape
    plan = Plan(channels, rows_x, rows_y, length_z, lax.axis_size("gx"), lax.axis_size("gy"))
    act = activations.reshape(plan.field)
    cot = cotangent.reshape(plan.field)
    weights = spectral_weights.reshape(plan.modes, channels, channels, MODES)
    mixing = jnp.concatenate([pointwise[0], channel_bias[0][:, None]], axis=1)
    third, third_t = jnp.asarray(plan.third), jnp.asarray(plan.third_t)
    second, second_t = jnp.asarray(plan.second), jnp.asarray(plan.second_t)
    first, first_t = jnp.asarray(plan.first), jnp.asarray(plan.first_t)
    segment = lax.axis_index("segment")
    segments = lax.axis_size("segment")
    half = lax.axis_index("gy")

    wire_shape = jax.ShapeDtypeStruct(plan.wire, BF16)
    wires_shape = jax.ShapeDtypeStruct((segments * plan.devices,) + plan.wire[1:], BF16)
    modes_shape = jax.ShapeDtypeStruct((plan.modes, channels, MODES), F32)
    part_shape = (channels, plan.side, length_z)
    wide = pltpu.HBM(plan.field, F32)
    wide_scratch = pltpu.VMEM(plan.field, F32)
    sums = pltpu.VMEM((plan.rows, MODES * channels), F32)
    inner = pltpu.VMEM((plan.rows, MODES * channels), BF16)
    total = pltpu.VMEM(plan.spectrum, F32)
    spectrum = pltpu.VMEM(plan.spectrum, BF16)
    field = pltpu.VMEM((plan.block, channels * length_z), F32)
    signal = pltpu.VMEM((plan.block, channels * length_z), BF16)
    flags = jnp.stack([half, segment])

    def sems(count):
        return pltpu.SemaphoreType.DMA((count,))

    both_ways = [total, spectrum, inner, sums, field, field, signal, signal, sems(plan.pieces)]

    def part_of(block, at):
        return lax.dynamic_slice_in_dim(block, at * plan.side, plan.side, 1)

    act_other = other_core(part_of(act, 1 - half))
    if segments > 1:
        next_own, mixing_next = from_behind(part_of(act, half), -1), from_behind(mixing, -1)
        next_other = from_behind(act_other, -1)
    wire = call(
        functools.partial(input_kernel, plan), "input_modes", (flags, act, third, second, act_other), wire_shape,
        [pltpu.VMEM(part_shape, BF16), pltpu.VMEM(plan.third.shape, BF16), pltpu.VMEM(plan.second.shape[1:], BF16),
         sums, total, sems(3)], 1, 3,
    )
    cot_later, wire = lax.optimization_barrier((cot, wire))
    cot_other = other_core(part_of(cot_later, 1 - half))
    input_modes, wire = call(
        functools.partial(spectral_kernel, plan, False), "mix_inputs", (exchange(wire), weights, first, first_t),
        (modes_shape, wire_shape),
    )
    wire_in = exchange(wire)
    wire, kept = call(
        functools.partial(first_kernel, plan, segments), "first_signal",
        (flags, mixing, act, cot, act_other, cot_other, wire_in, third, third_t, second, second_t),
        (wire_shape, wide), [wide_scratch] + both_ways, 2,
    )

    def mix_signal(wire, count):
        return call(
            functools.partial(spectral_kernel, plan, True), "mix_signal", (exchange(wire), weights, first, first_t),
            (modes_shape, jax.ShapeDtypeStruct((count * plan.devices,) + plan.wire[1:], BF16)),
        )

    def of_last():
        local = call(nothing_kernel, "no_local", (flags,), wide, scalars=1)
        return *mix_signal(wire, segments), local

    def of_others():
        local = call(
            functools.partial(shared_kernel, plan), "shared",
            (flags, mixing_next, next_own, next_other, cot, cot_other, wire_next, third_t, second_t), wide,
            [wide_scratch, spectrum, inner, field, field, sems(plan.pieces)], 2,
        )
        no_wires = call(nothing_kernel, "no_wires", (flags,), wires_shape, scalars=1)
        return input_modes, no_wires, local

    kept_wire = kept_modes = None
    local = kept
    for turn in range(segments - 1):
        active = segment == segments - 1 - turn
        if turn == 0:
            wire_next = from_behind(wire_in, -1)
            modes, wire, local = lax.cond(active, of_last, of_others)
        else:
            ahead = from_behind(local.astype(BF16), -1).astype(F32)
            local = jnp.where(segment == segments - 2 - turn, ahead, local)
            modes, wire = mix_signal(wire, segments)
        kept_modes = modes if kept_modes is None else jnp.where(active, modes, kept_modes)
        wires = exchange(wire, WHOLE)
        if kept_wire is None:
            kept_wire = wires
        else:
            here = lax.slice_in_dim(wires, (segments - 1 - turn) * plan.devices, (segments - turn) * plan.devices)
            old = lax.slice_in_dim(kept_wire, (segments - 1) * plan.devices, segments * plan.devices)
            kept_wire = jnp.concatenate(
                [kept_wire[: (segments - 1) * plan.devices], jnp.where(active, here, old)], axis=0
            )
        wire, local = call(
            functools.partial(middle_kernel, plan, segments, turn), "next_signal",
            (flags, mixing, local, kept, wires, third, third_t, second, second_t), (wire_shape, wide),
            [wide_scratch] + both_ways, 2,
        )
    if segments == 1:
        local = jnp.einsum("oi,oyz->iyz", pointwise[0], kept, precision=lax.Precision.HIGHEST)
    modes, wire = mix_signal(wire, 1)
    wire = exchange(wire)
    args = (flags, local, third_t, second_t, wire, wire if kept_wire is None else kept_wire)
    scratch = [spectrum, pltpu.VMEM((plan.side, MODES * channels), BF16),
               pltpu.VMEM((plan.side, channels * length_z), F32), sems(1)]
    weight_shape = (plan.modes, channels, channels, MODES)
    other_grads, weight_grad = call(
        functools.partial(last_other_kernel, plan, segments), "last_other",
        args + (input_modes, modes, modes if kept_modes is None else kept_modes),
        (jax.ShapeDtypeStruct(part_shape, BF16), pltpu.HBM(weight_shape, F32)),
        scratch + [pltpu.VMEM(weight_shape, F32)], 1,
    )
    received = other_core(other_grads)
    grad = call(
        functools.partial(last_own_kernel, plan, segments), "last_own", args, pltpu.HBM(plan.field, BF16),
        scratch + [pltpu.VMEM(part_shape, BF16)], 1,
    )
    grad = call(
        functools.partial(place_kernel, plan), "place", (flags, grad, received), pltpu.HBM(plan.field, BF16),
        [sems(1)], 1, 1, {1: 0},
    )
    return grad.reshape(activations.shape), weight_grad.reshape(spectral_weights.shape)


def solution(mesh):
    return jax.shard_map(
        body,
        mesh=mesh,
        in_specs=(
            P("segment", "groups", "gx", "gy", None),
            P("groups", "gx", "gy", None),
            P("segment", "gy", "gx", None, None, None),
            P("segment", None, None),
            P("segment", None),
        ),
        out_specs=(
            P("segment", "groups", "gx", "gy", None),
            P("segment", "gy", "gx", "groups", None, None),
        ),
        check_vma=False,
    )
```

time: 450 us -> 143 us (0.32); the launches traced: 441 us -> 143 us
  waiting for transfers between devices: 144 us -> 7.82 us
  matrix products: 79.5 us -> 0 us
  other arithmetic: 53.9 us -> 0.15 us
  Pallas kernels: 0 us -> 52.5 us
  local copies, waits for them, and re-layouts: 55.7 us -> 11.8 us
  starting transfers between devices: 26.8 us -> 6.03 us
  between operations: 14.6 us -> 1.14 us
    dot_general x18 -> x0, matrix products: 79.5 us -> none  [the longest x3 30.1 us: analyse(): third = jnp.einsum('ixyz,cz->cixy', field, along_z, precision=highest)]
    all_to_all x4 -> x0, waiting for transfers between devices: 76.7 us -> none  [the longest x3 51 us: synthesise(): lax.all_to_all(spread, 'gx', split_axis=2, concat_axis=0, tiled=True)]
    pallas_call x0 -> x10, Pallas kernels: none -> 52.5 us  [call(): pl.pallas_call(kernel, in_specs=specs, out_specs=out_specs, out_shape=out...]
    ppermute x1 -> x7, waiting for transfers between devices: 47.1 us -> 7.82 us  [the longest x4 5.61 us: from_behind(): return lax.ppermute(block, 'segment', route)]
    unnamed x39 -> x46, local copies, waits for them, and re-layouts: 32.2 us -> 7.28 us
    all_to_all x4 -> x0, starting transfers between devices: 24.8 us -> none  [the longest x3 17.5 us: synthesise(): lax.all_to_all(spread, 'gx', split_axis=2, concat_axis=0, tiled=True)]
    all_to_all x6 -> x0, other arithmetic: 23.5 us -> none  [the longest x3 11.8 us: synthesise(): lax.all_to_all(spread, 'gx', split_axis=2, concat_axis=0, tiled=True)]
    reduce_sum x3 -> x0, other arithmetic: 21.6 us -> none  [channel_mix(): return jnp.sum(matrix[:, :, None, None, None] * field[None], axis=1)]
  transfers between devices with their start and end apart: 8 -> 7, of which waited for: 8 -> 2; matrix products, arithmetic and copies ran while one was open for 6% -> 0% of each run, Pallas kernels for 0% -> 12%
where the time goes in v2:
time: 143 us
  blocking collectives  63.3 us (44%)
  Pallas kernels  52.5 us (37%)
  local copies, waits for them, and re-layouts  11.8 us (8%)
  waiting for transfers between devices  7.82 us (5%)
  starting transfers between devices  6.03 us (4%)
    all_to_all x5, blocking collectives, exchange(): return lax.all_to_all(wire, axes, split_axis=0, concat_axis=0, tiled=True)  63.3 us
    pallas_call x10, Pallas kernels, call(): pl.pallas_call(kernel, in_specs=specs, out_specs=out_specs, out_shape=out...  52.5 us
    unnamed x46, local copies, waits for them, and re-layouts  7.28 us
    ppermute x4, waiting for transfers between devices, from_behind(): return lax.ppermute(block, 'segment', route)  5.61 us
    ppermute x4, starting transfers between devices, from_behind(): return lax.ppermute(block, 'segment', route)  5.13 us
    dynamic_slice x2, local copies, waits for them, and re-layouts, part_of(): return lax.dynamic_slice_in_dim(block, at * plan.side, plan.side, 1)  3.76 us
  transfers between devices with their start and end apart: 7, of which 2 were waited for; matrix products, arithmetic and copies ran while one was open for 0% of the time, Pallas kernels for 12%

profile of v2, /device:TPU:0, one launch (start us, length us, event | category | flops | bytes accessed | tf_op | source)
XLA Modules:
  0.0 142.7 jit_solution(6368495992290399063)
XLA Ops:
  0.6 2.7 %constant_dynamic-slice_fusion.1 = (bf16[8,512,128]{2,1,0:T(8,128)(2,1)S(1)}, bf16[8,512,128]{2,1,0:T(8,128)(2,1)}) fusion(bf16[8,1024,128]{2,1,0:T(8,128)(2,1)} %bitcast.9, s32[]{:T(128)S(6)} %select_n.8, s32[]{:T(128)S(6)} %select_n.7), kind=kLoop, calls=%fused_computation.2 | loop fusion | bytes 4194312 | tf_op jit(solution)/shard_map/dynamic_slice | solution.py:571
  3.9 2.2 %collective-permute-done.2.other_ref.act_other_ref = bf16[8,512,128]{2,1,0:T(8,128)(2,1)S(1)} collective-permute-done((bf16[8,512,128]{2,1,0:T(8,128)(2,1)S(1)}, bf16[8,512,128]{2,1,0:T(8,128)(2,1)S(1)}, u32[]{:S(2)}, u32[]{:S(2)}) %collective-permute-start.2) | collective-permute-done | bytes 1048608 | tf_op jit(solution)/shard_map/ppermute | solution.py:534
  6.1 5.3 %input_modes.1 = bf16[16,16,256]{2,1,0:T(8,128)(2,1)S(1)} custom-call(s32[2]{0:T(128)S(1)} %pad_add_fusion.flags, bf16[8,1024,128]{2,1,0:T(8,128)(2,1)} %bitcast.10, bf16[2,1024,256]{2,1,0:T(8,128)(2,1)} %constant.26.clone.third_hbm.third_ref, bf16[2,2,256,1024]{3,2,1,0:T(8,128)(2,1)} %constant.28.clone.second_hbm.second_ref, ...), custom_call_target="tpu_custom_call" | custom-call | tf_op jit(solution)/shard_map/input_modes/pallas_call | solution.py:515
  12.9 1.3 collective-permute-start.1
  14.2 1.3 collective-permute-start.3
  15.5 14.9 %all_to_all.29.wire_ref = bf16[16,16,256]{2,1,0:T(8,128)(2,1)S(1)} all-to-all(bf16[16,16,256]{2,1,0:T(8,128)(2,1)S(1)} %input_modes.1), channel_id=1, replica_groups=mesh['groups'=1,'gx'=8,'gy'=2,'segment'=2] {'gx','gy'}, dimensions={0} | all-to-all | bytes 262144 | tf_op jit(solution)/shard_map/all_to_all | solution.py:524
  31.6 10.5 %all_to_all.30.wire_in_ref = bf16[16,16,256]{2,1,0:T(8,128)(2,1)S(1)} all-to-all(bf16[16,16,256]{2,1,0:T(8,128)(2,1)S(1)} %get-tuple-element.66), channel_id=1, replica_groups=mesh['groups'=1,'gx'=8,'gy'=2,'segment'=2] {'gx','gy'}, dimensions={0} | all-to-all | bytes 262144 | tf_op jit(solution)/shard_map/all_to_all | solution.py:524
  42.1 1.3 collective-permute-start.5
  43.6 1.3 collective-permute-start
  44.9 1.6 %copy-done.1 = bf16[2,2,256,1024]{3,2,1,0:T(8,128)(2,1)S(1)} copy-done((bf16[2,2,256,1024]{3,2,1,0:T(8,128)(2,1)S(1)}, bf16[2,2,256,1024]{3,2,1,0:T(8,128)(2,1)}, u32[]{:S(2)}) %copy-start.1) | copy-done | bytes 2097176
  46.5 1.2 copy-done.7
  47.7 12.8 %first_signal.1 = (bf16[16,16,256]{2,1,0:T(8,128)(2,1)}, f32[8,1024,128]{2,1,0:T(8,128)}) custom-call(s32[2]{0:T(128)S(1)} %pad_add_fusion.flags, f32[8,9]{1,0:T(8,128)S(1)} %pad_maximum_fusion.mixing_ref, bf16[8,1024,128]{2,1,0:T(8,128)(2,1)S(1)} %bitcast.11, bf16[8,1024,128]{2,1,0:T(8,128)(2,1)} %bitcast.15, bf16[8,512,128]{2,1,0:T(8,128)(2,1)S(1)} %copy-done.7, ...), custom_call_target="tpu_custom_call" | custom-call | tf_op jit(solution)/shard_map/first_signal/pallas_call | solution.py:515
  60.6 5.6 %collective-permute-done = f32[8,9]{1,0:T(8,128)S(1)} collective-permute-done((f32[8,9]{1,0:T(8,128)S(1)}, f32[8,9]{1,0:T(8,128)S(1)}, u32[]{:S(2)}, u32[]{:S(2)}) %collective-permute-start) | collective-permute-done | bytes 320 | tf_op jit(solution)/shard_map/ppermute | solution.py:530
  66.2 14.6 %conditional.1 = (f32[64,8,32]{2,1,0:T(8,128)}, bf16[32,16,256]{2,1,0:T(8,128)(2,1)S(1)}, f32[8,1024,128]{2,1,0:T(8,128)}) conditional(s32[]{:T(128)} %convert_element_type.3, (s32[2]{0:T(128)S(1)}, f32[8,9]{1,0:T(8,128)S(1)}, bf16[8,512,128]{2,1,0:T(8,128)(2,1)}, bf16[8,512,128]{2,1,0:T(8,128)(2,1)}, bf16[8,1024,128]{2,1,0:T(8,128)(2,1)S(1)}, ...), branch_computations={%region_0.0_spmd, %region_1.0_spmd} | conditional | bytes 393272 | solution.py:620
  67.5 13.3 %shared.1 = f32[8,1024,128]{2,1,0:T(8,128)} custom-call(s32[2]{0:T(128)S(1)} %get-tuple-element.31.unused.flags, f32[8,9]{1,0:T(8,128)S(1)} %get-tuple-element.32.mixing_ref, bf16[8,512,128]{2,1,0:T(8,128)(2,1)} %get-tuple-element.33.act_own_ref, bf16[8,512,128]{2,1,0:T(8,128)(2,1)} %get-tuple-element.34.act_other_ref, ...), custom_call_target="tpu_custom_call" | custom-call | tf_op jit(solution)/shard_map/cond/branch_0_fun/shared/pallas_call | solution.py:515
  80.9 15.9 %all_to_all.31.wire_in_ref.kept_wire_ref = bf16[32,16,256]{2,1,0:T(8,128)(2,1)S(1)} all-to-all(bf16[32,16,256]{2,1,0:T(8,128)(2,1)S(1)} %get-tuple-element.71), channel_id=1, replica_groups=mesh['groups'=1,'gx'=8,'gy'=2,'segment'=2] {'segment','gx','gy'}, dimensions={0} | all-to-all | bytes 524288 | tf_op jit(solution)/shard_map/all_to_all | solution.py:524
  96.7 2.2 %copy-done.5 = f32[8,1024,128]{2,1,0:T(8,128)S(1)} copy-done((f32[8,1024,128]{2,1,0:T(8,128)S(1)}, f32[8,1024,128]{2,1,0:T(8,128)}, u32[]{:S(2)}) %copy-start.5) | copy-done | bytes 4194328
  98.9 10.7 %next_signal.1 = (bf16[16,16,256]{2,1,0:T(8,128)(2,1)S(1)}, f32[8,1024,128]{2,1,0:T(8,128)}) custom-call(s32[2]{0:T(128)S(1)} %pad_add_fusion.flags, f32[8,9]{1,0:T(8,128)S(1)} %pad_maximum_fusion.mixing_ref, f32[8,1024,128]{2,1,0:T(8,128)} %get-tuple-element.69.local_ref, f32[8,1024,128]{2,1,0:T(8,128)S(1)} %copy-done.5, ...), custom_call_target="tpu_custom_call" | custom-call | tf_op jit(solution)/shard_map/next_signal/pallas_call | solution.py:515
  109.7 11.4 %all_to_all.32.wire_ref = bf16[16,16,256]{2,1,0:T(8,128)(2,1)S(1)} all-to-all(bf16[16,16,256]{2,1,0:T(8,128)(2,1)S(1)} %get-tuple-element.73), channel_id=1, replica_groups=mesh['groups'=1,'gx'=8,'gy'=2,'segment'=2] {'gx','gy'}, dimensions={0} | all-to-all | bytes 262144 | tf_op jit(solution)/shard_map/all_to_all | solution.py:524
  122.3 10.5 %all_to_all.33.wire_in_ref = bf16[16,16,256]{2,1,0:T(8,128)(2,1)S(1)} all-to-all(bf16[16,16,256]{2,1,0:T(8,128)(2,1)S(1)} %get-tuple-element.74), channel_id=1, replica_groups=mesh['groups'=1,'gx'=8,'gy'=2,'segment'=2] {'gx','gy'}, dimensions={0} | all-to-all | bytes 262144 | tf_op jit(solution)/shard_map/all_to_all | solution.py:524
  132.8 2.2 %copy-done.3 = f32[8,1024,128]{2,1,0:T(8,128)S(1)} copy-done((f32[8,1024,128]{2,1,0:T(8,128)S(1)}, f32[8,1024,128]{2,1,0:T(8,128)}, u32[]{:S(2)}) %copy-start.3) | copy-done | bytes 4194328
  135.0 3.1 %last_other.1 = (bf16[8,512,128]{2,1,0:T(8,128)(2,1)S(1)}, f32[64,8,8,32]{3,2,1,0:T(8,128)}) custom-call(s32[2]{0:T(128)S(1)} %pad_add_fusion.flags, f32[8,1024,128]{2,1,0:T(8,128)S(1)} %copy-done.3, bf16[2,256,1024]{2,1,0:T(8,128)(2,1)S(1)} %copy-done.11, bf16[2,2,1024,256]{3,2,1,0:T(8,128)(2,1)S(1)} %copy-done.9, ...), custom_call_target="tpu_custom_call" | custom-call | tf_op jit(solution)/shard_map/last_other/pallas_call | solution.py:515
  138.2 2.8 %last_own.1.part_hbm = bf16[8,1024,128]{2,1,0:T(8,128)(2,1)} custom-call(s32[2]{0:T(128)S(1)} %pad_add_fusion.flags, f32[8,1024,128]{2,1,0:T(8,128)S(1)} %copy-done.3, bf16[2,256,1024]{2,1,0:T(8,128)(2,1)S(1)} %copy-done.11, bf16[2,2,1024,256]{3,2,1,0:T(8,128)(2,1)S(1)} %copy-done.9, bf16[16,16,256]{2,1,0:T(8,128)(2,1)S(1)} %all_to_all.33.wire_in_ref, ...), custom_call_target="tpu_custom_call" | custom-call | tf_op jit(solution)/shard_map/last_own/pallas_call | solution.py:515
  141.0 1.5 %place.1 = bf16[8,1024,128]{2,1,0:T(8,128)(2,1)} custom-call(s32[2]{0:T(128)S(1)} %pad_add_fusion.flags, bf16[8,1024,128]{2,1,0:T(8,128)(2,1)} %last_own.1.part_hbm, bf16[8,512,128]{2,1,0:T(8,128)(2,1)S(1)} %collective-permute-done.6.received_ref), custom_call_target="tpu_custom_call", output_to_operand_aliasing={{}: (1, {})} | custom-call | tf_op jit(solution)/shard_map/place/pallas_call | solution.py:515
  (58 shorter events, 5.8 us)
Async XLA Ops:
  3.3 2.7 %collective-permute-start.2 = (bf16[8,512,128]{2,1,0:T(8,128)(2,1)S(1)}, bf16[8,512,128]{2,1,0:T(8,128)(2,1)S(1)}, u32[]{:S(2)}, u32[]{:S(2)}) collective-permute-start(bf16[8,512,128]{2,1,0:T(8,128)(2,1)S(1)} %get-tuple-element.79), channel_id=1, source_target_pairs={{0,2},{2,0},{1,3},{3,1},{4,6},{6,4},{5,7},{7,5},{8,10},{10,8},{9,1... | collective-permute-start | bytes 3145736 | tf_op jit(solution)/shard_map/ppermute | solution.py:534
  6.1 24.4 %copy-start.12 = (f32[1,16,4,8,8,32]{5,4,3,2,1,0:T(8,128)S(1)}, f32[1,16,4,8,8,32]{5,4,3,2,1,0:T(8,128)}, u32[]{:S(2)}) copy-start(f32[1,16,4,8,8,32]{5,4,3,2,1,0:T(8,128)} %param.15) | copy-start | bytes 1572868
  11.4 19.1 %copy-start.16 = (bf16[2,256,64]{2,1,0:T(8,128)(2,1)S(1)}, bf16[2,256,64]{2,1,0:T(8,128)(2,1)}, u32[]{:S(2)}) copy-start(bf16[2,256,64]{2,1,0:T(8,128)(2,1)} %constant.31.clone.first_t_ref) | copy-start | bytes 196612
  11.4 19.0 %copy-start.20 = (bf16[2,64,256]{2,1,0:T(8,128)(2,1)S(1)}, bf16[2,64,256]{2,1,0:T(8,128)(2,1)}, u32[]{:S(2)}) copy-start(bf16[2,64,256]{2,1,0:T(8,128)(2,1)} %constant.30.clone.first_ref) | copy-start | bytes 196612
  11.4 32.0 %copy-start.22 = (f32[1,8]{1,0:T(1,128)S(1)}, f32[1,8]{1,0:T(1,128)}, u32[]{:S(2)}) copy-start(f32[1,8]{1,0:T(1,128)} %param.17) | copy-start | bytes 100
  11.5 32.1 %copy-start.21 = (f32[1,8,8]{2,1,0:T(8,128)S(1)}, f32[1,8,8]{2,1,0:T(8,128)}, u32[]{:S(2)}) copy-start(f32[1,8,8]{2,1,0:T(8,128)} %param.16) | copy-start | bytes 772
  11.5 33.4 %copy-start = (bf16[1,8,16,64,128]{4,3,2,1,0:T(8,128)(2,1)S(1)}, bf16[1,8,16,64,128]{4,3,2,1,0:T(8,128)(2,1)}, u32[]{:S(2)}) copy-start(bf16[1,8,16,64,128]{4,3,2,1,0:T(8,128)(2,1)} %param.13) | copy-start | bytes 6291460
  11.5 33.4 %copy-start.4 = (bf16[2,1024,256]{2,1,0:T(8,128)(2,1)S(1)}, bf16[2,1024,256]{2,1,0:T(8,128)(2,1)}, u32[]{:S(2)}) copy-start(bf16[2,1024,256]{2,1,0:T(8,128)(2,1)} %constant.26.clone.third_hbm.third_ref) | copy-start | bytes 3145732
  12.6 32.3 %collective-permute-start.4 = (bf16[8,512,128]{2,1,0:T(8,128)(2,1)}, bf16[8,512,128]{2,1,0:T(8,128)(2,1)}, u32[]{:S(2)}, u32[]{:S(2)}) collective-permute-start(bf16[8,512,128]{2,1,0:T(8,128)(2,1)} %constant_dynamic-slice_fusion), channel_id=1, source_target_pairs={{0,2},{2,0},{1,3},{3,1},{4,6},{6,4},{5,7},{7,5},{8,10},{10,8},{9,1... | collective-permute-start | bytes 3145736 | tf_op jit(solution)/shard_map/ppermute | solution.py:534
  12.9 53.2 %collective-permute-start.1 = (bf16[8,512,128]{2,1,0:T(8,128)(2,1)}, bf16[8,512,128]{2,1,0:T(8,128)(2,1)}, u32[]{:S(2)}, u32[]{:S(2)}) collective-permute-start(bf16[8,512,128]{2,1,0:T(8,128)(2,1)} %get-tuple-element.80), channel_id=1, source_target_pairs={{1,0},{3,2},{5,4},{7,6},{9,8},{11,10},{13,12},{15,14},{17,16},{19,... | collective-permute-start | bytes 3145736 | tf_op jit(solution)/shard_map/ppermute | solution.py:530
  14.2 51.9 %collective-permute-start.3 = (bf16[8,512,128]{2,1,0:T(8,128)(2,1)}, bf16[8,512,128]{2,1,0:T(8,128)(2,1)}, u32[]{:S(2)}, u32[]{:S(2)}) collective-permute-start(bf16[8,512,128]{2,1,0:T(8,128)(2,1)} %copy-done.6), channel_id=1, source_target_pairs={{1,0},{3,2},{5,4},{7,6},{9,8},{11,10},{13,12},{15,14},{17,16},{19,... | collective-permute-start | bytes 3145736 | tf_op jit(solution)/shard_map/ppermute | solution.py:530
  42.1 24.0 %collective-permute-start.5 = (bf16[16,16,256]{2,1,0:T(8,128)(2,1)S(1)}, bf16[16,16,256]{2,1,0:T(8,128)(2,1)}, u32[]{:S(2)}, u32[]{:S(2)}) collective-permute-start(bf16[16,16,256]{2,1,0:T(8,128)(2,1)S(1)} %all_to_all.30.wire_in_ref), channel_id=1, source_target_pairs={{1,0},{3,2},{5,4},{7,6},{9,8},{11,10},{13,12},{15,14},{17,16},{19,... | collective-permute-start | bytes 393224 | tf_op jit(solution)/shard_map/ppermute | solution.py:530
  43.6 22.6 %collective-permute-start = (f32[8,9]{1,0:T(8,128)S(1)}, f32[8,9]{1,0:T(8,128)S(1)}, u32[]{:S(2)}, u32[]{:S(2)}) collective-permute-start(f32[8,9]{1,0:T(8,128)S(1)} %pad_maximum_fusion.mixing_ref), channel_id=1, source_target_pairs={{1,0},{3,2},{5,4},{7,6},{9,8},{11,10},{13,12},{15,14},{17,16},{19,... | collective-permute-start | bytes 872 | tf_op jit(solution)/shard_map/ppermute | solution.py:530
  47.7 18.4 %copy-start.8 = (bf16[2,2,1024,256]{3,2,1,0:T(8,128)(2,1)S(1)}, bf16[2,2,1024,256]{3,2,1,0:T(8,128)(2,1)}, u32[]{:S(2)}) copy-start(bf16[2,2,1024,256]{3,2,1,0:T(8,128)(2,1)} %constant.29.clone.second_t_ref) | copy-start | bytes 6291460
  47.7 18.5 %copy-start.10 = (bf16[2,256,1024]{2,1,0:T(8,128)(2,1)S(1)}, bf16[2,256,1024]{2,1,0:T(8,128)(2,1)}, u32[]{:S(2)}) copy-start(bf16[2,256,1024]{2,1,0:T(8,128)(2,1)} %constant.27.clone.third_t_ref) | copy-start | bytes 3145732
  47.7 18.5 %copy-start.15 = (bf16[8,16,64,128]{3,2,1,0:T(8,128)(2,1)S(1)}, bf16[8,16,64,128]{3,2,1,0:T(8,128)(2,1)}, u32[]{:S(2)}) copy-start(bf16[8,16,64,128]{3,2,1,0:T(8,128)(2,1)} %param.14) | copy-start | bytes 6291460
  47.7 18.5 %copy-start.17 = (f32[64,8,32]{2,1,0:T(8,128)S(1)}, f32[64,8,32]{2,1,0:T(8,128)}, u32[]{:S(2)}) copy-start(f32[64,8,32]{2,1,0:T(8,128)} %get-tuple-element.67.input_modes_ref) | copy-start | bytes 196612
  66.2 30.5 %copy-start.2 = (bf16[2,2,256,1024]{3,2,1,0:T(8,128)(2,1)S(1)}, bf16[2,2,256,1024]{3,2,1,0:T(8,128)(2,1)}, u32[]{:S(2)}) copy-start(bf16[2,2,256,1024]{3,2,1,0:T(8,128)(2,1)} %constant.28.clone.second_hbm.second_ref) | copy-start | bytes 6291460
  98.9 22.2 %copy-start.13 = (f32[1,16,4,8,8,32]{5,4,3,2,1,0:T(8,128)S(1)}, f32[1,16,4,8,8,32]{5,4,3,2,1,0:T(8,128)}, u32[]{:S(2)}) copy-start(f32[1,16,4,8,8,32]{5,4,3,2,1,0:T(8,128)} %param.15) | copy-start | bytes 1572868
  98.9 33.9 %copy-start.11 = (bf16[2,256,1024]{2,1,0:T(8,128)(2,1)S(1)}, bf16[2,256,1024]{2,1,0:T(8,128)(2,1)}, u32[]{:S(2)}) copy-start(bf16[2,256,1024]{2,1,0:T(8,128)(2,1)} %constant.27.clone.third_t_ref) | copy-start | bytes 3145732
  109.7 23.1 %copy-start.9 = (bf16[2,2,1024,256]{3,2,1,0:T(8,128)(2,1)S(1)}, bf16[2,2,1024,256]{3,2,1,0:T(8,128)(2,1)}, u32[]{:S(2)}) copy-start(bf16[2,2,1024,256]{3,2,1,0:T(8,128)(2,1)} %constant.29.clone.second_t_ref) | copy-start | bytes 6291460
  109.7 23.1 %copy-start.18 = (f32[64,8,32]{2,1,0:T(8,128)S(1)}, f32[64,8,32]{2,1,0:T(8,128)}, u32[]{:S(2)}) copy-start(f32[64,8,32]{2,1,0:T(8,128)} %get-tuple-element.67.input_modes_ref) | copy-start | bytes 196612
  109.7 23.1 %copy-start.19 = (f32[64,8,32]{2,1,0:T(8,128)S(1)}, f32[64,8,32]{2,1,0:T(8,128)}, u32[]{:S(2)}) copy-start(f32[64,8,32]{2,1,0:T(8,128)} %get-tuple-element.76.kept_modes_ref) | copy-start | bytes 196612
  138.2 2.9 %collective-permute-start.6 = (bf16[8,512,128]{2,1,0:T(8,128)(2,1)S(1)}, bf16[8,512,128]{2,1,0:T(8,128)(2,1)S(1)}, u32[]{:S(2)}, u32[]{:S(2)}) collective-permute-start(bf16[8,512,128]{2,1,0:T(8,128)(2,1)S(1)} %get-tuple-element.77), channel_id=1, source_target_pairs={{0,2},{2,0},{1,3},{3,1},{4,6},{6,4},{5,7},{7,5},{8,10},{10,8},{9,1... | collective-permute-start | bytes 3145736 | tf_op jit(solution)/shard_map/ppermute | solution.py:534
  (6 other events, 20.1 us)

commit v3 on v2

v3 whole, which is shorter than its diff:
```python
import functools
import math

import jax
import jax.numpy as jnp
import ml_dtypes
import numpy as np
from jax import lax
from jax.experimental import pallas as pl
from jax.experimental.pallas import tpu as pltpu
from jax.sharding import PartitionSpec as P

MODES = 32
LANES = 128
PLANE = ("gx", "gy")
WHOLE = ("segment",) + PLANE
F32 = jnp.float32
BF16 = jnp.bfloat16
VMEM_LIMIT = 22 * 1024 * 1024
CHUNK = 64


def trig_basis(length):
    half = MODES // 2
    points = np.arange(length)[None, :]
    freqs = np.arange(half)[:, None]
    angle = 2.0 * math.pi / length
    rows = np.concatenate(
        [np.cos((freqs * points % length) * angle), np.sin(((freqs + 1) * points % length) * angle)], axis=0
    )
    scales = np.where(np.arange(MODES) == 0, 1.0 / math.sqrt(length), math.sqrt(2.0 / length))
    return rows * scales[:, None]


def high_low(values):
    high = values.astype(np.float32).astype(ml_dtypes.bfloat16)
    low = (values - high.astype(np.float64)).astype(np.float32).astype(ml_dtypes.bfloat16)
    return np.stack([high, low])


class Plan:
    def __init__(self, channels, rows_x, rows_y, length_z, count_x, count_y):
        self.channels, self.length_z = channels, length_z
        self.count_x, self.count_y = count_x, count_y
        self.devices = count_x * count_y
        share = rows_x // count_y
        self.side = share * rows_y
        self.rows = self.side * count_y
        self.pieces = 2 * count_y
        self.piece = self.rows // self.pieces
        self.own_third = MODES // count_x
        self.own_second = MODES // count_y
        self.width = self.own_third * channels
        self.parts = 2 if share <= 8 and self.own_second // 2 * self.width >= LANES else 1
        padded = 8 if self.parts == 2 else -(-share // 16) * 16
        self.in_part = self.own_second // self.parts
        self.slot = self.parts * padded
        self.per_tile = LANES // self.width
        self.tiles = self.in_part // self.per_tile
        self.groups = MODES // self.parts // self.per_tile
        self.halves = MODES * channels // LANES
        self.lanes = self.in_part * self.width
        self.wire = (self.devices, self.slot, self.lanes)
        self.modes = self.own_second * self.own_third
        self.spectrum = (MODES * padded, MODES * channels)
        self.field = (channels, self.rows, length_z)
        along_x = trig_basis(rows_x * count_x).reshape(MODES, self.devices, share)
        along_y = trig_basis(rows_y * count_y).reshape(MODES, count_y, rows_y)
        along_z = trig_basis(length_z)
        third = np.einsum("ik,cz->izck", np.eye(channels), along_z)
        third = third.reshape(channels * length_z, MODES * channels)
        self.third = high_low(third)
        self.third_t = high_low(third.T)[0]
        slabs = along_y.reshape(count_y, self.parts, self.in_part, count_y, rows_y)
        second = np.einsum("opqsy,xk->oqpxsky", slabs, np.eye(padded, share))
        second = second.reshape(MODES * padded, self.rows)
        self.second = high_low(second)
        self.second_t = high_low(second.T)[0]
        spread = np.zeros((MODES, self.devices, padded))
        spread[:, :, :share] = along_x
        first = np.einsum("pq,adx->padqx", np.eye(self.parts), spread)
        first = first.reshape(self.parts * MODES, self.devices * self.slot)
        self.first = high_low(first)
        self.first_t = high_low(first.T)


def dot(a, b):
    return jnp.dot(a, b, preferred_element_type=F32)


def join(arrays, axis):
    return jnp.concatenate(arrays, axis=axis)


def split(value):
    high = value.astype(BF16)
    return high, (value - high.astype(F32)).astype(BF16)


def swap_groups(parts, width):
    parts = list(parts)
    lane = lax.broadcasted_iota(jnp.int32, parts[0].shape, 1)
    bit = len(parts) // 2
    while bit:
        shift = bit * width
        low = (lane // shift) % 2 == 0
        for at in range(len(parts)):
            if at & bit:
                continue
            a, b = parts[at], parts[at | bit]
            parts[at] = jnp.where(low, a, pltpu.roll(b, shift, 1))
            parts[at | bit] = jnp.where(low, pltpu.roll(a, LANES - shift, 1), b)
        bit //= 2
    return parts


def pack_wire(plan, total_ref, wire_ref):
    slot, group = plan.slot, plan.per_tile
    for half in range(plan.halves):
        for block in range(plan.groups):
            parts = [
                total_ref[pl.ds((block * group + j) * slot, slot), pl.ds(half * LANES, LANES)] for j in range(group)
            ]
            parts = swap_groups(parts, plan.width)
            owner_y, tile = block // plan.tiles, block % plan.tiles
            for g in range(group):
                target = (half * group + g) * plan.count_y + owner_y
                wire_ref[target, :, pl.ds(tile * LANES, LANES)] = parts[g].astype(BF16)


def unpack_wire(plan, load, spectrum_ref):
    slot, group = plan.slot, plan.per_tile
    for half in range(plan.halves):
        for block in range(plan.groups):
            owner_y, tile = block // plan.tiles, block % plan.tiles
            parts = [
                load((half * group + g) * plan.count_y + owner_y, pl.ds(tile * LANES, LANES)).astype(F32)
                for g in range(group)
            ]
            parts = swap_groups(parts, plan.width)
            for j in range(group):
                spectrum_ref[pl.ds((block * group + j) * slot, slot), pl.ds(half * LANES, LANES)] = parts[j].astype(BF16)


def blocks_of(wire_ref):
    return lambda device, lanes: wire_ref[device, :, lanes]


def synthesise(plan, load, second_t, third_t_ref, spectrum_ref, cells_ref):
    unpack_wire(plan, load, spectrum_ref)
    spectrum = spectrum_ref[...]
    inner = dot(second_t, spectrum).astype(BF16)
    cells_ref[...] = dot(inner, third_t_ref[...])


def piece_rows(plan, k):
    return pl.ds(pl.multiple_of(k * plan.piece, 16), plan.piece)


def each_piece(plan, flags, works, arriving=(), leaving=()):
    per_side = plan.pieces // plan.count_y
    for which in range(plan.count_y):
        for k in range(per_side):
            piece = (1 - flags[0] if which else flags[0]) * per_side + k
            rows = piece_rows(plan, piece)
            for ref, source, sems in arriving:
                pltpu.make_async_copy(source.at[:, rows], ref.at[:, rows], sems.at[piece]).wait()
            for work in works:

                def step(c, carry):
                    in_side = pl.ds(pl.multiple_of(k * plan.piece + c * CHUNK, 16), CHUNK)
                    work(which, in_side, pl.ds(pl.multiple_of(piece * plan.piece + c * CHUNK, 16), CHUNK))
                    return carry

                lax.fori_loop(0, plan.piece // CHUNK, step, 0)
            for ref, target, sems in leaving:
                pltpu.make_async_copy(ref.at[:, rows], target.at[:, rows], sems.at[piece]).start()


def start_pieces(plan, arriving):
    for k in range(plan.pieces):
        rows = piece_rows(plan, k)
        for ref, source, sems in arriving:
            pltpu.make_async_copy(source.at[:, rows], ref.at[:, rows], sems.at[k]).start()


def start_sides(plan, flags, own, other, target, sems):
    per_side = plan.pieces // plan.count_y
    for k in range(per_side):
        at = k * plan.piece
        there = pl.ds(pl.multiple_of(flags[0] * plan.side + at, 16), plan.piece)
        other_there = there if other.shape == own.shape else pl.ds(at, plan.piece)
        for half, source in [(flags[0], own.at[:, there]), (1 - flags[0], other.at[:, other_there])]:
            piece = half * per_side + k
            pltpu.make_async_copy(source, target.at[:, piece_rows(plan, piece)], sems.at[piece]).start()


def wait_pieces(plan, leaving):
    for ref, target, sems in leaving:
        for p in range(plan.pieces):
            rows = piece_rows(plan, p)
            pltpu.make_async_copy(ref.at[:, rows], target.at[:, rows], sems.at[p]).wait()


def sums_over_z(fields, third_ref):
    return dot(join([fields, fields], 1), join([third_ref[0], third_ref[1]], 0))


def finish(plan, sums, second_ref, total_ref, wire_ref):
    high, low = split(sums)
    total_ref[...] = dot(join([second_ref[0], second_ref[0], second_ref[1]], 1), join([high, low, high], 0))
    pack_wire(plan, total_ref, wire_ref)


def gelu_slope(value):
    size = jnp.abs(value)
    t = 1.0 / (1.0 + (0.3275911 * 0.7071067811865476) * size)
    poly = 0.5 * 1.061405429
    for c in (-1.453152027, 1.421413741, -0.284496736, 0.254829592):
        poly = poly * t + 0.5 * c
    bell = jnp.exp(-0.5 * value * value)
    tail = bell * (poly * t - 0.3989422804014327 * size)
    return jnp.where(value >= 0, 1.0 - tail, tail)


def each_chunk(total, chunk, work):
    def step(k, carry):
        work(pl.ds(pl.multiple_of(k * chunk, chunk), chunk))
        return carry

    lax.fori_loop(0, total // chunk, step, 0)


def lanes_of(plan, channel):
    return pl.ds(channel * plan.length_z, plan.length_z)


def mixed_with(plan, mixing_ref, values, out, transposed):
    total = None
    for k, value in enumerate(values):
        term = (mixing_ref[k, out] if transposed else mixing_ref[out, k]) * value
        total = term if total is None else total + term
    return total


def starts(copies, sems):
    copies = [pltpu.make_async_copy(source, target, sems.at[k]) for k, (source, target) in enumerate(copies)]
    for copy in copies:
        copy.start()
    return copies


def waits(copies):
    for copy in copies:
        copy.wait()


def own_side(plan, flags, k=0):
    at = flags[0] if k == 0 else 1 - flags[0]
    return pl.ds(pl.multiple_of(at * plan.side, 16), plan.side)


def position():
    return lax.axis_index("gy"), lax.axis_index("segment")


def input_own_kernel(
    plan, act_hbm, third_hbm, second_hbm, third_ref, second_ref, sums_ref, own_ref, sems
):
    flags = position()
    copies = starts(
        [(third_hbm, third_ref), (act_hbm.at[:, own_side(plan, flags)], own_ref), (second_hbm, second_ref)], sems
    )
    waits(copies[:2])
    sums_ref[...] = sums_over_z(join([own_ref[i] for i in range(plan.channels)], 1), third_ref)
    waits(copies[2:])


def input_kernel(
    plan, third_ref, second_ref, own_sums_ref, other_ref, mixing_ref, wire_ref, other_hbm, three_ref,
    sums_ref, total_ref, sems,
):
    flags = position()
    values = mixing_ref[...]
    three_ref[...] = jnp.zeros_like(three_ref)
    for k in range(3):
        part = values.astype(BF16)
        three_ref[0, :, pl.ds(k * values.shape[1], values.shape[1])] = part
        values = values - part.astype(F32)
    halves = [own_side(plan, flags, k) for k in range(2)]
    copies = starts([(other_ref, other_hbm)], sems)
    sums_ref[halves[0], :] = own_sums_ref[...]
    sums_ref[halves[1], :] = sums_over_z(join([other_ref[i] for i in range(plan.channels)], 1), third_ref)
    finish(plan, sums_ref[...], second_ref, total_ref, wire_ref)
    waits(copies)


def mix_inputs(plan, mixing_ref, act_ref, mixed_ref):
    def work(which, in_side, rows):
        inputs = [act_ref[i, rows, :].astype(F32) for i in range(plan.channels)]
        for o in range(plan.channels):
            mixed = mixed_with(plan, mixing_ref, inputs, o, False) + mixing_ref[o, plan.channels]
            mixed_ref[o, rows, :] = mixed

    return work


def first_kernel(
    plan, segments, flags, mixing_ref, act_hbm, act_other_hbm, cot_hbm, cot_other_hbm, third_hbm, second_hbm,
    wire_in_ref, third_t_ref, second_t_ref, wire_ref, kept_hbm,
    act_ref, cot_ref, kept_ref, third_ref, second_ref, total_ref, spectrum_ref, cells_ref, signals_ref, sems, piece_sems,
):
    last = flags[1] == segments - 1
    start_sides(plan, flags, act_hbm, act_other_hbm, act_ref, piece_sems.at[0])
    start_sides(plan, flags, cot_hbm, cot_other_hbm, cot_ref, piece_sems.at[1])
    copies = starts([(third_hbm, third_ref), (second_hbm, second_ref)], sems)
    synthesise(plan, blocks_of(wire_in_ref), second_t_ref[...], third_t_ref, spectrum_ref, cells_ref)
    arriving = [(act_ref, act_hbm, piece_sems.at[0]), (cot_ref, act_hbm, piece_sems.at[1])]
    leaving = [(kept_ref, kept_hbm, piece_sems.at[2])]
    mix = mix_inputs(plan, mixing_ref, act_ref, kept_ref)

    @pl.when(last)
    def _():
        def work(which, in_side, rows):
            for o in range(plan.channels):
                slope = gelu_slope(kept_ref[o, rows, :] + cells_ref[rows, lanes_of(plan, o)])
                signal = cot_ref[o, rows, :].astype(F32) * slope
                kept_ref[o, rows, :] = signal
                signals_ref[rows, lanes_of(plan, o)] = signal.astype(BF16)

        each_piece(plan, flags, [mix, work], arriving, leaving)
        waits(copies)
        finish(plan, sums_over_z(signals_ref[...], third_ref), second_ref, total_ref, wire_ref)

    @pl.when(jnp.logical_not(last))
    def _():
        def work(which, in_side, rows):
            for o in range(plan.channels):
                pre = kept_ref[o, rows, :] + cells_ref[rows, lanes_of(plan, o)]
                kept_ref[o, rows, :] = gelu_slope(pre)

        each_piece(plan, flags, [mix, work], arriving, leaving)
        waits(copies)

    wait_pieces(plan, leaving)


def shared_kernel(
    plan, segments, columns, flags, act_hbm, act_other_hbm, cot_hbm, cot_other_hbm, wire_hbm, third_t_ref,
    second_t_ref, local_ref, act_ref, cot_ref, wire_ref, spectrum_ref, cells_ref, values_ref, mixing_ref, sems,
    piece_sems,
):
    @pl.when(flags[1] == segments - 2)
    def _():
        copies = starts([(wire_hbm, wire_ref)], sems)
        start_sides(plan, flags, act_hbm, act_other_hbm, act_ref, piece_sems.at[0])
        start_sides(plan, flags, cot_hbm, cot_other_hbm, cot_ref, piece_sems.at[1])
        waits(copies)
        parts = [
            wire_ref[plan.devices, :, pl.ds(k * columns, columns)].astype(F32) for k in range(3)
        ]
        values_ref[:, pl.ds(0, columns)] = parts[0] + parts[1] + parts[2]
        copies = starts([(values_ref, mixing_ref)], sems)
        synthesise(plan, blocks_of(wire_ref), second_t_ref[...], third_t_ref, spectrum_ref, cells_ref)
        waits(copies)

        def slope(which, in_side, rows):
            for o in range(plan.channels):
                pre = local_ref[o, rows, :] + cells_ref[rows, lanes_of(plan, o)]
                local_ref[o, rows, :] = cot_ref[o, rows, :].astype(F32) * gelu_slope(pre)

        def back(which, in_side, rows):
            signals = [local_ref[o, rows, :] for o in range(plan.channels)]
            for i in range(plan.channels):
                local_ref[i, rows, :] = mixed_with(plan, mixing_ref, signals, i, True)

        arriving = [(act_ref, act_hbm, piece_sems.at[0]), (cot_ref, act_hbm, piece_sems.at[1])]
        each_piece(plan, flags, [mix_inputs(plan, mixing_ref, act_ref, local_ref), slope, back], arriving)


def middle_kernel(
    plan, segments, turn, flags, mixing_ref, kept_hbm, local_ref, wire_in_ref, third_ref, third_t_ref, second_ref,
    second_t_ref, wire_ref, local_out_ref,
    kept_ref, total_ref, spectrum_ref, cells_ref, signals_ref, sems, piece_sems,
):
    segment = flags[1]
    active = segments - 1 - turn
    kept = (kept_ref, kept_hbm, piece_sems.at[0])

    @pl.when(segment < active)
    def _():
        start_pieces(plan, [kept])
        synthesise(plan, lambda device, lanes: wire_in_ref[active * plan.devices + device, :, lanes],
                   second_t_ref[...], third_t_ref, spectrum_ref, cells_ref)

        def work(which, in_side, rows):
            signals = []
            for i in range(plan.channels):
                grad = local_ref[i, rows, :] + cells_ref[rows, lanes_of(plan, i)]
                signals.append(grad * kept_ref[i, rows, :])
                signals_ref[rows, lanes_of(plan, i)] = signals[i].astype(BF16)
            for i in range(plan.channels):
                local_out_ref[i, rows, :] = mixed_with(plan, mixing_ref, signals, i, True)

        each_piece(plan, flags, [work], [kept])
        finish(plan, sums_over_z(signals_ref[...], third_ref), second_ref, total_ref, wire_ref)

    @pl.when(segment >= active)
    def _():
        if turn == 0:
            start_pieces(plan, [kept])

            def work(which, in_side, rows):
                signals = [kept_ref[o, rows, :] for o in range(plan.channels)]
                for i in range(plan.channels):
                    local_out_ref[i, rows, :] = mixed_with(plan, mixing_ref, signals, i, True)

            each_piece(plan, flags, [work], [kept])
        else:
            waits(starts([(local_ref, local_out_ref)], sems))


def side_grads(plan, segments, which, flags, local_ref, third_t_ref, second_t_ref, wire_in_ref, kept_wire_ref,
               grad_ref, spectrum_ref, cells_ref):
    segment = flags[1]
    last = (segments - 1) * plan.devices
    here = own_side(plan, flags, which)

    def load(device, lanes):
        return jnp.where(segment == 0, wire_in_ref[device, :, lanes], kept_wire_ref[last + device, :, lanes])

    synthesise(plan, load, second_t_ref[here, :], third_t_ref, spectrum_ref, cells_ref)

    def work(rows):
        there = pl.ds(pl.multiple_of(rows.start + here.start, 16), rows.size)
        for i in range(plan.channels):
            grad_ref[i, rows, :] = (local_ref[i, there, :] + cells_ref[rows, lanes_of(plan, i)]).astype(BF16)

    each_chunk(plan.side, 64, work)


def last_other_kernel(
    plan, segments, local_ref, third_t_ref, second_t_ref, wire_in_ref, kept_wire_ref, grad_ref,
    spectrum_ref, cells_ref,
):
    flags = position()
    side_grads(plan, segments, 1, flags, local_ref, third_t_ref, second_t_ref, wire_in_ref, kept_wire_ref, grad_ref,
               spectrum_ref, cells_ref)


def last_own_kernel(
    plan, segments, local_ref, third_t_ref, second_t_ref, wire_in_ref, kept_wire_ref, input_modes_ref,
    modes_ref, kept_modes_ref, out_hbm, weight_hbm, spectrum_ref, cells_ref, weight_ref, grad_ref, sems,
):
    flags = position()
    modes = jnp.where(flags[1] == 0, modes_ref[...], kept_modes_ref[...])
    for i in range(plan.channels):
        weight_ref[:, i] = input_modes_ref[:, i : i + 1, :] * modes
    copies = starts([(weight_ref, weight_hbm)], sems)
    side_grads(plan, segments, 0, flags, local_ref, third_t_ref, second_t_ref, wire_in_ref, kept_wire_ref, grad_ref,
               spectrum_ref, cells_ref)
    waits(copies + starts([(grad_ref, out_hbm.at[:, own_side(plan, flags)])], sems.at[pl.ds(1, 1)]))


def nothing_kernel(unused, out_hbm):
    pass


def mode_sums(plan, wire_ref, first_ref):
    received = wire_ref[...].reshape(plan.devices * plan.slot, plan.lanes)
    sums = dot(first_ref[0], received) + dot(first_ref[1], received)
    modes = join([sums[p * MODES : (p + 1) * MODES].T for p in range(plan.parts)], 0)
    return modes.reshape(plan.modes, plan.channels, MODES)


def flatten(plan, mixed):
    rows = mixed.reshape(plan.parts, plan.lanes, MODES)
    return join([rows[p].T for p in range(plan.parts)], 0)


def mix_modes(plan, modes, weights_ref, backward):
    if not backward:
        mixed = weights_ref[:, 0] * modes[:, 0:1, :]
        for i in range(1, plan.channels):
            mixed = mixed + weights_ref[:, i] * modes[:, i : i + 1, :]
        return mixed
    row = lax.broadcasted_iota(jnp.int32, modes.shape, 1)
    mixed = jnp.zeros_like(modes)
    for i in range(plan.channels):
        mixed = jnp.where(row == i, jnp.sum(weights_ref[:, i] * modes, axis=1, keepdims=True), mixed)
    return mixed


def spread_modes(plan, mixed, first_t_ref):
    high, low = split(flatten(plan, mixed))
    spread = dot(first_t_ref[0], high) + dot(first_t_ref[0], low) + dot(first_t_ref[1], high)
    return spread.astype(BF16).reshape(plan.wire)


def spectral_kernel(plan, backward, wire_ref, weights_ref, first_ref, first_t_ref, modes_ref, wire_out_ref):
    modes = mode_sums(plan, wire_ref, first_ref)
    modes_ref[...] = modes
    spread = spread_modes(plan, mix_modes(plan, modes, weights_ref, backward), first_t_ref)
    copies = wire_out_ref.shape[0] // plan.devices
    for k in range(copies):
        wire_out_ref[pl.ds(k * plan.devices, plan.devices)] = spread


VMEM = pl.BlockSpec(memory_space=pltpu.VMEM)
SMEM = pl.BlockSpec(memory_space=pltpu.SMEM)
HBM = pl.BlockSpec(memory_space=pltpu.HBM)


def call(kernel, name, args, out_shape, scratch=(), scalars=0, far=0, aliases={}):
    specs = [SMEM] * scalars + [HBM] * far + [VMEM] * (len(args) - scalars - far)
    args = [
        pltpu.with_memory_space_constraint(arg, pltpu.HBM) if spec is HBM else arg for arg, spec in zip(args, specs)
    ]
    outs = out_shape if isinstance(out_shape, tuple) else (out_shape,)
    out_specs = tuple(HBM if getattr(out, "memory_space", None) is pltpu.HBM else VMEM for out in outs)
    result = pl.pallas_call(
        kernel, in_specs=specs, out_specs=out_specs, out_shape=outs, scratch_shapes=scratch,
        input_output_aliases=aliases,
        compiler_params=pltpu.CompilerParams(vmem_limit_bytes=VMEM_LIMIT), name=name,
    )(*args)
    return result if isinstance(out_shape, tuple) else result[0]


def exchange(wire, axes=PLANE):
    return lax.all_to_all(wire, axes, split_axis=0, concat_axis=0, tiled=True)


def from_behind(block, distance):
    devices = range(lax.axis_size("segment"))
    route = [(i - distance, i) for i in devices if i - distance in devices]
    return lax.ppermute(block, "segment", route)


def other_core(block):
    return lax.ppermute(block, "gy", [(0, 1), (1, 0)])


def body(activations, cotangent, spectral_weights, pointwise, channel_bias):
    _, channels, rows_x, rows_y, length_z = activations.shape
    plan = Plan(channels, rows_x, rows_y, length_z, lax.axis_size("gx"), lax.axis_size("gy"))
    act = activations.reshape(plan.field)
    cot = cotangent.reshape(plan.field)
    weights = spectral_weights.reshape(plan.modes, channels, channels, MODES)
    mixing = jnp.concatenate([pointwise[0], channel_bias[0][:, None]], axis=1)
    third, third_t = jnp.asarray(plan.third), jnp.asarray(plan.third_t)
    second, second_t = jnp.asarray(plan.second), jnp.asarray(plan.second_t)
    first, first_t = jnp.asarray(plan.first), jnp.asarray(plan.first_t)
    segment = lax.axis_index("segment")
    segments = lax.axis_size("segment")
    half = lax.axis_index("gy")

    wire_shape = jax.ShapeDtypeStruct(plan.wire, BF16)
    wires_shape = jax.ShapeDtypeStruct((segments * plan.devices,) + plan.wire[1:], BF16)
    modes_shape = jax.ShapeDtypeStruct((plan.modes, channels, MODES), F32)
    part_shape = (channels, plan.side, length_z)
    part = jax.ShapeDtypeStruct(part_shape, BF16)
    wide = pltpu.HBM(plan.field, F32)
    wide_scratch, narrow_scratch = pltpu.VMEM(plan.field, F32), pltpu.VMEM(plan.field, BF16)
    piece_sems = pltpu.SemaphoreType.DMA((3, plan.pieces))
    total = pltpu.VMEM(plan.spectrum, F32)
    spectrum = pltpu.VMEM(plan.spectrum, BF16)
    cells = pltpu.VMEM((plan.rows, channels * length_z), F32)
    half_cells = pltpu.VMEM((plan.side, channels * length_z), F32)
    signals = pltpu.VMEM((plan.rows, channels * length_z), BF16)
    flags = jnp.stack([half, segment])

    def sems(count):
        return pltpu.SemaphoreType.DMA((count,))

    def part_of(block, at):
        return lax.dynamic_slice_in_dim(block, at * plan.side, plan.side, 1)

    act_other = other_core(part_of(act, 1 - half))
    if segments > 1:
        act_next = from_behind(act, -1)
    parts = call(
        functools.partial(input_own_kernel, plan), "own_inputs", (act, third, second),
        (jax.ShapeDtypeStruct(third.shape, BF16), jax.ShapeDtypeStruct(second.shape, BF16),
         jax.ShapeDtypeStruct((plan.side, MODES * channels), F32)),
        [pltpu.VMEM(part_shape, BF16), sems(3)], 0, 3,
    )
    wire, act_other, in_three = call(
        functools.partial(input_kernel, plan), "input_modes",
        (*parts, act_other, jnp.pad(mixing, [(0, plan.slot - channels), (0, 0)])),
        (wire_shape, pltpu.HBM(part_shape, BF16), jax.ShapeDtypeStruct((1,) + plan.wire[1:], BF16)),
        [pltpu.VMEM((plan.rows, MODES * channels), F32), total, sems(2)],
    )
    cot_other = other_core(cot)
    input_modes, wire = call(
        functools.partial(spectral_kernel, plan, False), "mix_inputs", (exchange(wire), weights, first, first_t),
        (modes_shape, wire_shape),
    )
    wire_in = exchange(wire)
    if segments > 1:
        next_block = from_behind(jnp.concatenate([wire_in, in_three], axis=0), -1)
    wire, kept = call(
        functools.partial(first_kernel, plan, segments), "first_signal",
        (flags, mixing, act, act_other, cot, cot_other, third, second, wire_in, third_t, second_t), (wire_shape, wide),
        [narrow_scratch, narrow_scratch, wide_scratch, pltpu.VMEM(third.shape, BF16), pltpu.VMEM(second.shape, BF16),
         total, spectrum, cells, signals, sems(2), piece_sems], 2, 6,
    )

    def mix_signal(wire, count):
        return call(
            functools.partial(spectral_kernel, plan, True), "mix_signal", (wire, weights, first, first_t),
            (modes_shape, jax.ShapeDtypeStruct((count * plan.devices,) + plan.wire[1:], BF16)),
        )

    def of_last():
        return exchange(wire), call(nothing_kernel, "no_inputs", (flags,), pltpu.HBM(plan.field, BF16), scalars=1)

    def of_others():
        return wire, other_core(act_next)

    kept_wire = kept_modes = None
    for turn in range(segments - 1):
        active = segment == segments - 1 - turn
        if turn == 0:
            wire, next_other = lax.cond(active, of_last, of_others)
            wire, next_block = lax.optimization_barrier((wire, next_block))
            local = call(
                functools.partial(shared_kernel, plan, segments, mixing.shape[1]), "shared",
                (flags, act_next, next_other, cot, cot_other, next_block, third_t, second_t),
                jax.ShapeDtypeStruct(plan.field, F32),
                [narrow_scratch, narrow_scratch, pltpu.VMEM(next_block.shape, BF16), spectrum, cells,
                 pltpu.VMEM((plan.slot, LANES), F32), pltpu.SMEM((plan.slot, LANES), F32), sems(1), piece_sems], 1, 5,
            )
            wire, local = lax.optimization_barrier((wire, local))
        else:
            ahead = from_behind(local.astype(BF16), -1).astype(F32)
            local = jnp.where(segment == segments - 2 - turn, ahead, local)
            wire = exchange(wire)
        modes, wire = mix_signal(wire, segments)
        kept_modes = modes if kept_modes is None else jnp.where(active, modes, kept_modes)
        wires = exchange(wire, WHOLE)
        if kept_wire is None:
            kept_wire = wires
        else:
            here = lax.slice_in_dim(wires, (segments - 1 - turn) * plan.devices, (segments - turn) * plan.devices)
            old = lax.slice_in_dim(kept_wire, (segments - 1) * plan.devices, segments * plan.devices)
            kept_wire = jnp.concatenate(
                [kept_wire[: (segments - 1) * plan.devices], jnp.where(active, here, old)], axis=0
            )
        wire, local = call(
            functools.partial(middle_kernel, plan, segments, turn), "next_signal",
            (flags, mixing, kept, local, wires, third, third_t, second, second_t),
            (wire_shape, jax.ShapeDtypeStruct(plan.field, F32)),
            [wide_scratch, total, spectrum, cells, signals, sems(2), piece_sems], 2, 1,
        )
    if segments == 1:
        local = jnp.einsum("oi,oyz->iyz", pointwise[0], kept, precision=lax.Precision.HIGHEST)
    modes, wire = mix_signal(exchange(wire), 1)
    wire = exchange(wire)
    args = (local, third_t, second_t, wire, wire if kept_wire is None else kept_wire)
    weight_shape = (plan.modes, channels, channels, MODES)
    other_grads = call(
        functools.partial(last_other_kernel, plan, segments), "last_other", args, part, [spectrum, half_cells]
    )
    received = other_core(other_grads)
    grad, weight_grad = call(
        functools.partial(last_own_kernel, plan, segments), "last_own",
        args + (input_modes, modes, modes if kept_modes is None else kept_modes),
        (pltpu.HBM(plan.field, BF16), pltpu.HBM(weight_shape, F32)),
        [spectrum, half_cells, pltpu.VMEM(weight_shape, F32), pltpu.VMEM(part_shape, BF16), sems(2)],
    )
    grad = lax.dynamic_update_slice_in_dim(grad, received, (1 - half) * plan.side, 1)
    return grad.reshape(activations.shape), weight_grad.reshape(spectral_weights.shape)


def solution(mesh):
    return jax.shard_map(
        body,
        mesh=mesh,
        in_specs=(
            P("segment", "groups", "gx", "gy", None),
            P("groups", "gx", "gy", None),
            P("segment", "gy", "gx", None, None, None),
            P("segment", None, None),
            P("segment", None),
        ),
        out_specs=(
            P("segment", "groups", "gx", "gy", None),
            P("segment", "gy", "gx", "groups", None, None),
        ),
        check_vma=False,
    )
```

time: 143 us -> 122 us (0.85)
  Pallas kernels: 52.5 us -> 42.5 us
  local copies, waits for them, and re-layouts: 11.8 us -> 4.29 us
  starting transfers between devices: 6.03 us -> 3.21 us
    pallas_call x10, Pallas kernels: 52.5 us -> 42.5 us  [call(): pl.pallas_call(kernel, in_specs=specs, out_specs=out_specs, out_shape=out...]
    unnamed x46 -> x24, local copies, waits for them, and re-layouts: 7.28 us -> 0.76 us
    ppermute x4 -> x2, waiting for transfers between devices: 5.61 us -> 2.16 us  [from_behind(): return lax.ppermute(block, 'segment', route)]
    ppermute x3 -> x4, waiting for transfers between devices: 2.21 us -> 4.82 us  [other_core(): return lax.ppermute(block, 'gy', [(0, 1), (1, 0)])]
    ppermute x4 -> x2, starting transfers between devices: 5.13 us -> 2.56 us  [from_behind(): return lax.ppermute(block, 'segment', route)]
    dynamic_slice x2 -> x1, local copies, waits for them, and re-layouts: 3.76 us -> 2.28 us  [part_of(): return lax.dynamic_slice_in_dim(block, at * plan.side, plan.side, 1)]
  transfers between devices with their start and end apart: 7 -> 6, of which waited for: 2 -> 3; matrix products, arithmetic and copies ran while one was open for 0% -> 3% of each run, Pallas kernels for 12% -> 15%
where the time goes in v3:
time: 122 us
  blocking collectives  63.3 us (52%)
  Pallas kernels  42.5 us (35%)
  waiting for transfers between devices  6.98 us (6%)
  local copies, waits for them, and re-layouts  4.29 us (4%)
  starting transfers between devices  3.21 us (3%)
    all_to_all x5, blocking collectives, exchange(): return lax.all_to_all(wire, axes, split_axis=0, concat_axis=0, tiled=True)  63.3 us
    pallas_call x10, Pallas kernels, call(): pl.pallas_call(kernel, in_specs=specs, out_specs=out_specs, out_shape=out...  42.5 us
    ppermute x4, waiting for transfers between devices, other_core(): return lax.ppermute(block, 'gy', [(0, 1), (1, 0)])  4.82 us
    ppermute x2, starting transfers between devices, from_behind(): return lax.ppermute(block, 'segment', route)  2.56 us
  transfers between devices with their start and end apart: 6, of which 3 were waited for; matrix products, arithmetic and copies ran while one was open for 3% of the time, Pallas kernels for 15%

profile of v3, /device:TPU:0, one launch (start us, length us, event | category | flops | bytes accessed | tf_op | source)
XLA Modules:
  0.0 121.9 jit_solution(14829523155705464722)
XLA Ops:
  1.2 1.3 %collective-permute-start.3 = (bf16[8,1024,128]{2,1,0:T(8,128)(2,1)}, bf16[8,1024,128]{2,1,0:T(8,128)(2,1)}, u32[]{:S(2)}, u32[]{:S(2)}) collective-permute-start(bf16[8,1024,128]{2,1,0:T(8,128)(2,1)} %bitcast.12), channel_id=1, source_target_pairs={{1,0},{3,2},{5,4},{7,6},{9,8},{11,10},{13,12},{15,14},{17,16},{19,... | collective-permute-start | bytes 6291464 | tf_op jit(solution)/shard_map/ppermute | solution.py:536
  2.5 2.3 %constant_dynamic-slice_fusion = bf16[8,512,128]{2,1,0:T(8,128)(2,1)} fusion(bf16[8,1024,128]{2,1,0:T(8,128)(2,1)} %bitcast.13, s32[]{:T(128)S(6)} %select_n.4), kind=kLoop, calls=%fused_computation.4 | loop fusion | bytes 2097156 | tf_op jit(solution)/shard_map/dynamic_slice | solution.py:576
  5.0 2.3 %own_inputs.1 = (bf16[2,1024,256]{2,1,0:T(8,128)(2,1)S(1)}, bf16[2,256,1024]{2,1,0:T(8,128)(2,1)S(1)}, f32[512,256]{1,0:T(8,128)S(1)}) custom-call(bf16[8,1024,128]{2,1,0:T(8,128)(2,1)} %bitcast.14, bf16[2,1024,256]{2,1,0:T(8,128)(2,1)} %constant.28.clone.third_hbm.third_ref, bf16[2,256,1024]{2,1,0:T(8,128)(2,1)} %constant.30.clone.second_hbm.second_ref), custom_call_target="tpu_custom_call" | custom-call | tf_op jit(solution)/shard_map/own_inputs/pallas_call | solution.py:521
  7.6 2.5 %input_modes.1 = (bf16[16,16,256]{2,1,0:T(8,128)(2,1)S(1)}, bf16[8,512,128]{2,1,0:T(8,128)(2,1)}, bf16[1,16,256]{2,1,0:T(8,128)(2,1)S(1)}) custom-call(bf16[2,1024,256]{2,1,0:T(8,128)(2,1)S(1)} %get-tuple-element.38.third_ref, bf16[2,256,1024]{2,1,0:T(8,128)(2,1)S(1)} %get-tuple-element.39.second_ref, f32[512,256]{1,0:T(8,128)S(1)} %get-tuple-element.40.own_sums_ref, ...), custom_call_target="tpu_custom_call" | custom-call | tf_op jit(solution)/shard_map/input_modes/pallas_call | solution.py:521
  10.1 15.0 %all_to_all.29.wire_ref = bf16[16,16,256]{2,1,0:T(8,128)(2,1)S(1)} all-to-all(bf16[16,16,256]{2,1,0:T(8,128)(2,1)S(1)} %get-tuple-element.42), channel_id=1, replica_groups=mesh['groups'=1,'gx'=8,'gy'=2,'segment'=2] {'gx','gy'}, dimensions={0} | all-to-all | bytes 262144 | tf_op jit(solution)/shard_map/all_to_all | solution.py:530
  25.1 0.8 mix_inputs.1
  25.9 0.7 copy-done.7
  26.6 10.5 %all_to_all.30.wire_in_ref = bf16[16,16,256]{2,1,0:T(8,128)(2,1)S(1)} all-to-all(bf16[16,16,256]{2,1,0:T(8,128)(2,1)S(1)} %get-tuple-element.43), channel_id=1, replica_groups=mesh['groups'=1,'gx'=8,'gy'=2,'segment'=2] {'gx','gy'}, dimensions={0} | all-to-all | bytes 262144 | tf_op jit(solution)/shard_map/all_to_all | solution.py:530
  37.1 0.7 pad_maximum_fusion
  37.7 1.3 %collective-permute-start.4 = (bf16[17,16,256]{2,1,0:T(8,128)(2,1)}, bf16[17,16,256]{2,1,0:T(8,128)(2,1)}, u32[]{:S(2)}, u32[]{:S(2)}) collective-permute-start(bf16[17,16,256]{2,1,0:T(8,128)(2,1)} %pad_maximum_fusion), channel_id=1, source_target_pairs={{1,0},{3,2},{5,4},{7,6},{9,8},{11,10},{13,12},{15,14},{17,16},{19,... | collective-permute-start | bytes 417800 | tf_op jit(solution)/shard_map/ppermute | solution.py:536
  39.1 10.6 %first_signal.1 = (bf16[16,16,256]{2,1,0:T(8,128)(2,1)}, f32[8,1024,128]{2,1,0:T(8,128)}) custom-call(s32[2]{0:T(128)S(1)} %pad_add_fusion.flags, f32[8,9]{1,0:T(8,128)S(1)} %pad_maximum_fusion.1.mixing_ref, bf16[8,1024,128]{2,1,0:T(8,128)(2,1)} %bitcast.15, bf16[8,512,128]{2,1,0:T(8,128)(2,1)} %get-tuple-element.41.act_other_hbm, ...), custom_call_target="tpu_custom_call" | custom-call | tf_op jit(solution)/shard_map/first_signal/pallas_call | solution.py:521
  49.7 2.2 %collective-permute-done.3.act_hbm = bf16[8,1024,128]{2,1,0:T(8,128)(2,1)} collective-permute-done((bf16[8,1024,128]{2,1,0:T(8,128)(2,1)}, bf16[8,1024,128]{2,1,0:T(8,128)(2,1)}, u32[]{:S(2)}, u32[]{:S(2)}) %collective-permute-start.3) | collective-permute-done | bytes 2097184 | tf_op jit(solution)/shard_map/ppermute | solution.py:536
  51.9 4.5 %conditional.1 = (bf16[16,16,256]{2,1,0:T(8,128)(2,1)}, bf16[8,1024,128]{2,1,0:T(8,128)(2,1)}) conditional(s32[]{:T(128)} %convert_element_type.5, (bf16[8,1024,128]{2,1,0:T(8,128)(2,1)}, bf16[16,16,256]{2,1,0:T(8,128)(2,1)}) %tuple.18, (bf16[16,16,256]{2,1,0:T(8,128)(2,1)}, s32[2]{0:T(128)S(1)}) %tuple.19), branch_computations={%region_0.1_spmd, %region_1.2_spmd} | conditional | bytes 8388664 | solution.py:624
  51.9 4.5 %collective-permute-done = bf16[8,1024,128]{2,1,0:T(8,128)(2,1)} collective-permute-done((bf16[8,1024,128]{2,1,0:T(8,128)(2,1)}, bf16[8,1024,128]{2,1,0:T(8,128)(2,1)}, u32[]{:S(2)}, u32[]{:S(2)}) %collective-permute-start) | collective-permute-done | bytes 2097184 | tf_op jit(solution)/shard_map/cond/branch_0_fun/ppermute | solution.py:540
  56.4 12.0 %shared.1.local_ref = f32[8,1024,128]{2,1,0:T(8,128)S(1)} custom-call(s32[2]{0:T(128)S(1)} %pad_add_fusion.flags, bf16[8,1024,128]{2,1,0:T(8,128)(2,1)} %collective-permute-done.3.act_hbm, bf16[8,1024,128]{2,1,0:T(8,128)(2,1)} %get-tuple-element.49.act_other_hbm, bf16[8,1024,128]{2,1,0:T(8,128)(2,1)} %bitcast.18, ...), custom_call_target="tpu_custom_call" | custom-call | tf_op jit(solution)/shard_map/shared/pallas_call | solution.py:521
  68.4 1.2 mix_signal.2
  69.6 16.0 %all_to_all.31.wire_in_ref.kept_wire_ref = bf16[32,16,256]{2,1,0:T(8,128)(2,1)S(1)} all-to-all(bf16[32,16,256]{2,1,0:T(8,128)(2,1)S(1)} %get-tuple-element.53), channel_id=1, replica_groups=mesh['groups'=1,'gx'=8,'gy'=2,'segment'=2] {'segment','gx','gy'}, dimensions={0} | all-to-all | bytes 524288 | tf_op jit(solution)/shard_map/all_to_all | solution.py:530
  85.6 8.4 %next_signal.1 = (bf16[16,16,256]{2,1,0:T(8,128)(2,1)S(1)}, f32[8,1024,128]{2,1,0:T(8,128)S(1)}) custom-call(s32[2]{0:T(128)S(1)} %pad_add_fusion.flags, f32[8,9]{1,0:T(8,128)S(1)} %pad_maximum_fusion.1.mixing_ref, f32[8,1024,128]{2,1,0:T(8,128)} %get-tuple-element.44.kept_hbm, f32[8,1024,128]{2,1,0:T(8,128)S(1)} %shared.1.local_ref, ...), custom_call_target="tpu_custom_call" | custom-call | tf_op jit(solution)/shard_map/next_signal/pallas_call | solution.py:521
  94.0 11.3 %all_to_all.32.wire_ref = bf16[16,16,256]{2,1,0:T(8,128)(2,1)S(1)} all-to-all(bf16[16,16,256]{2,1,0:T(8,128)(2,1)S(1)} %get-tuple-element.55), channel_id=1, replica_groups=mesh['groups'=1,'gx'=8,'gy'=2,'segment'=2] {'gx','gy'}, dimensions={0} | all-to-all | bytes 262144 | tf_op jit(solution)/shard_map/all_to_all | solution.py:530
  105.3 1.2 mix_signal.3
  106.4 10.5 %all_to_all.33.wire_in_ref = bf16[16,16,256]{2,1,0:T(8,128)(2,1)S(1)} all-to-all(bf16[16,16,256]{2,1,0:T(8,128)(2,1)S(1)} %get-tuple-element.56), channel_id=1, replica_groups=mesh['groups'=1,'gx'=8,'gy'=2,'segment'=2] {'gx','gy'}, dimensions={0} | all-to-all | bytes 262144 | tf_op jit(solution)/shard_map/all_to_all | solution.py:530
  117.0 1.0 last_other.1
  118.0 2.7 %last_own.1 = (bf16[8,1024,128]{2,1,0:T(8,128)(2,1)}, f32[64,8,8,32]{3,2,1,0:T(8,128)}) custom-call(f32[8,1024,128]{2,1,0:T(8,128)S(1)} %get-tuple-element.54.local_ref, bf16[256,1024]{1,0:T(8,128)(2,1)S(1)} %copy-done.2, bf16[1024,256]{1,0:T(8,128)(2,1)S(1)} %copy-done.1, bf16[16,16,256]{2,1,0:T(8,128)(2,1)S(1)} %all_to_all.33.wire_in_ref, ...), custom_call_target="tpu_custom_call" | custom-call | tf_op jit(solution)/shard_map/last_own/pallas_call | solution.py:521
  120.8 1.2 constant_dynamic-update-slice_fusion
  (35 shorter events, 1.3 us)
Async XLA Ops:
  0.6 4.2 %copy-start.11 = (f32[1,8]{1,0:T(1,128)S(1)}, f32[1,8]{1,0:T(1,128)}, u32[]{:S(2)}) copy-start(f32[1,8]{1,0:T(1,128)} %param.17) | copy-start | bytes 100
  0.6 4.2 %copy-start.10 = (f32[1,8,8]{2,1,0:T(8,128)S(1)}, f32[1,8,8]{2,1,0:T(8,128)}, u32[]{:S(2)}) copy-start(f32[1,8,8]{2,1,0:T(8,128)} %param.16) | copy-start | bytes 772
  0.6 38.5 %collective-permute-start.2 = (bf16[8,1024,128]{2,1,0:T(8,128)(2,1)}, bf16[8,1024,128]{2,1,0:T(8,128)(2,1)}, u32[]{:S(2)}, u32[]{:S(2)}) collective-permute-start(bf16[8,1024,128]{2,1,0:T(8,128)(2,1)} %bitcast.16), channel_id=1, source_target_pairs={{0,2},{2,0},{1,3},{3,1},{4,6},{6,4},{5,7},{7,5},{8,10},{10,8},{9,1... | collective-permute-start | bytes 6291464 | tf_op jit(solution)/shard_map/ppermute | solution.py:540
  1.2 50.7 %collective-permute-start.3 = (bf16[8,1024,128]{2,1,0:T(8,128)(2,1)}, bf16[8,1024,128]{2,1,0:T(8,128)(2,1)}, u32[]{:S(2)}, u32[]{:S(2)}) collective-permute-start(bf16[8,1024,128]{2,1,0:T(8,128)(2,1)} %bitcast.12), channel_id=1, source_target_pairs={{1,0},{3,2},{5,4},{7,6},{9,8},{11,10},{13,12},{15,14},{17,16},{19,... | collective-permute-start | bytes 6291464 | tf_op jit(solution)/shard_map/ppermute | solution.py:536
  4.7 2.9 %collective-permute-start.1 = (bf16[8,512,128]{2,1,0:T(8,128)(2,1)}, bf16[8,512,128]{2,1,0:T(8,128)(2,1)S(1)}, u32[]{:S(2)}, u32[]{:S(2)}) collective-permute-start(bf16[8,512,128]{2,1,0:T(8,128)(2,1)} %constant_dynamic-slice_fusion), channel_id=1, source_target_pairs={{0,2},{2,0},{1,3},{3,1},{4,6},{6,4},{5,7},{7,5},{8,10},{10,8},{9,1... | collective-permute-start | bytes 3145736 | tf_op jit(solution)/shard_map/ppermute | solution.py:540
  7.3 17.8 %copy-start = (f32[1,16,4,8,8,32]{5,4,3,2,1,0:T(8,128)S(1)}, f32[1,16,4,8,8,32]{5,4,3,2,1,0:T(8,128)}, u32[]{:S(2)}) copy-start(f32[1,16,4,8,8,32]{5,4,3,2,1,0:T(8,128)} %param.15) | copy-start | bytes 1572868
  7.3 17.8 %copy-start.5 = (bf16[2,256,64]{2,1,0:T(8,128)(2,1)S(1)}, bf16[2,256,64]{2,1,0:T(8,128)(2,1)}, u32[]{:S(2)}) copy-start(bf16[2,256,64]{2,1,0:T(8,128)(2,1)} %constant.33.clone.first_t_ref) | copy-start | bytes 196612
  7.3 17.8 %copy-start.6 = (bf16[2,64,256]{2,1,0:T(8,128)(2,1)S(1)}, bf16[2,64,256]{2,1,0:T(8,128)(2,1)}, u32[]{:S(2)}) copy-start(bf16[2,64,256]{2,1,0:T(8,128)(2,1)} %constant.32.clone.first_ref) | copy-start | bytes 196612
  10.1 29.0 %copy-start.1 = (bf16[1024,256]{1,0:T(8,128)(2,1)S(1)}, bf16[1024,256]{1,0:T(8,128)(2,1)}, u32[]{:S(2)}) copy-start(bf16[1024,256]{1,0:T(8,128)(2,1)} %constant.31.clone.second_t_ref) | copy-start | bytes 1572868
  10.1 29.0 %copy-start.2 = (bf16[256,1024]{1,0:T(8,128)(2,1)S(1)}, bf16[256,1024]{1,0:T(8,128)(2,1)}, u32[]{:S(2)}) copy-start(bf16[256,1024]{1,0:T(8,128)(2,1)} %constant.29.clone.third_t_ref) | copy-start | bytes 1572868
  25.8 0.7 copy-start.7
  37.7 18.6 %collective-permute-start.4 = (bf16[17,16,256]{2,1,0:T(8,128)(2,1)}, bf16[17,16,256]{2,1,0:T(8,128)(2,1)}, u32[]{:S(2)}, u32[]{:S(2)}) collective-permute-start(bf16[17,16,256]{2,1,0:T(8,128)(2,1)} %pad_maximum_fusion), channel_id=1, source_target_pairs={{1,0},{3,2},{5,4},{7,6},{9,8},{11,10},{13,12},{15,14},{17,16},{19,... | collective-permute-start | bytes 417800 | tf_op jit(solution)/shard_map/ppermute | solution.py:536
  51.9 4.5 %collective-permute-start = (bf16[8,1024,128]{2,1,0:T(8,128)(2,1)}, bf16[8,1024,128]{2,1,0:T(8,128)(2,1)}, u32[]{:S(2)}, u32[]{:S(2)}) collective-permute-start(bf16[8,1024,128]{2,1,0:T(8,128)(2,1)} %get-tuple-element.9), channel_id=1, source_target_pairs={{0,2},{2,0},{1,3},{3,1},{4,6},{6,4},{5,7},{7,5},{8,10},{10,8},{9,1... | collective-permute-start | bytes 6291464 | tf_op jit(solution)/shard_map/cond/branch_0_fun/ppermute | solution.py:540
  56.4 12.0 %copy-start.9 = (bf16[16,16,256]{2,1,0:T(8,128)(2,1)S(1)}, bf16[16,16,256]{2,1,0:T(8,128)(2,1)}, u32[]{:S(2)}) copy-start(bf16[16,16,256]{2,1,0:T(8,128)(2,1)} %get-tuple-element.52.wire_ref) | copy-start | bytes 393220
  68.4 17.2 %copy-start.3 = (bf16[2,256,1024]{2,1,0:T(8,128)(2,1)S(1)}, bf16[2,256,1024]{2,1,0:T(8,128)(2,1)}, u32[]{:S(2)}) copy-start(bf16[2,256,1024]{2,1,0:T(8,128)(2,1)} %constant.30.clone.second_hbm.second_ref) | copy-start | bytes 3145732
  68.4 17.2 %copy-start.4 = (bf16[2,1024,256]{2,1,0:T(8,128)(2,1)S(1)}, bf16[2,1024,256]{2,1,0:T(8,128)(2,1)}, u32[]{:S(2)}) copy-start(bf16[2,1024,256]{2,1,0:T(8,128)(2,1)} %constant.28.clone.third_hbm.third_ref) | copy-start | bytes 3145732
  117.0 1.1 copy-start.8
  117.9 2.8 %collective-permute-start.5 = (bf16[8,512,128]{2,1,0:T(8,128)(2,1)S(1)}, bf16[8,512,128]{2,1,0:T(8,128)(2,1)S(1)}, u32[]{:S(2)}, u32[]{:S(2)}) collective-permute-start(bf16[8,512,128]{2,1,0:T(8,128)(2,1)S(1)} %last_other.1), channel_id=1, source_target_pairs={{0,2},{2,0},{1,3},{3,1},{4,6},{6,4},{5,7},{7,5},{8,10},{10,8},{9,1... | collective-permute-start | bytes 3145736 | tf_op jit(solution)/shard_map/ppermute | solution.py:540

commit v4 on v3

--- a/solution.py
+++ b/solution.py
@@ -12,7 +12,7 @@
 
 MODES = 32
 LANES = 128
-PLANE = ("gx", "gy")
+PLANE = ("gy", "gx")
 WHOLE = ("segment",) + PLANE
 F32 = jnp.float32
 BF16 = jnp.bfloat16
@@ -64,7 +64,8 @@
         self.modes = self.own_second * self.own_third
         self.spectrum = (MODES * padded, MODES * channels)
         self.field = (channels, self.rows, length_z)
-        along_x = trig_basis(rows_x * count_x).reshape(MODES, self.devices, share)
+        along_x = trig_basis(rows_x * count_x).reshape(MODES, count_x, count_y, share)
+        along_x = np.swapaxes(along_x, 1, 2).reshape(MODES, self.devices, share)
         along_y = trig_basis(rows_y * count_y).reshape(MODES, count_y, rows_y)
         along_z = trig_basis(length_z)
         third = np.einsum("ik,cz->izck", np.eye(channels), along_z)
@@ -124,7 +125,7 @@
             parts = swap_groups(parts, plan.width)
             owner_y, tile = block // plan.tiles, block % plan.tiles
             for g in range(group):
-                target = (half * group + g) * plan.count_y + owner_y
+                target = owner_y * plan.count_x + half * group + g
                 wire_ref[target, :, pl.ds(tile * LANES, LANES)] = parts[g].astype(BF16)
 
 
@@ -134,7 +135,7 @@
         for block in range(plan.groups):
             owner_y, tile = block // plan.tiles, block % plan.tiles
             parts = [
-                load((half * group + g) * plan.count_y + owner_y, pl.ds(tile * LANES, LANES)).astype(F32)
+                load(owner_y * plan.count_x + half * group + g, pl.ds(tile * LANES, LANES)).astype(F32)
                 for g in range(group)
             ]
             parts = swap_groups(parts, plan.width)
@@ -184,15 +185,20 @@
             pltpu.make_async_copy(source.at[:, rows], ref.at[:, rows], sems.at[k]).start()
 
 
-def start_sides(plan, flags, own, other, target, sems):
+def start_sides(plan, flags, arrays):
     per_side = plan.pieces // plan.count_y
-    for k in range(per_side):
-        at = k * plan.piece
-        there = pl.ds(pl.multiple_of(flags[0] * plan.side + at, 16), plan.piece)
-        other_there = there if other.shape == own.shape else pl.ds(at, plan.piece)
-        for half, source in [(flags[0], own.at[:, there]), (1 - flags[0], other.at[:, other_there])]:
-            piece = half * per_side + k
-            pltpu.make_async_copy(source, target.at[:, piece_rows(plan, piece)], sems.at[piece]).start()
+    for which in range(plan.count_y):
+        for k in range(per_side):
+            at = k * plan.piece
+            there = pl.ds(pl.multiple_of(flags[0] * plan.side + at, 16), plan.piece)
+            piece = (1 - flags[0] if which else flags[0]) * per_side + k
+            for own, other, target, sems in arrays:
+                source = other if which else own
+                if source.shape[1] == plan.side:
+                    source = source.at[:, pl.ds(at, plan.piece)]
+                else:
+                    source = source.at[:, there]
+                pltpu.make_async_copy(source, target.at[:, piece_rows(plan, piece)], sems.at[piece]).start()
 
 
 def wait_pieces(plan, leaving):
@@ -311,8 +317,8 @@
     act_ref, cot_ref, kept_ref, third_ref, second_ref, total_ref, spectrum_ref, cells_ref, signals_ref, sems, piece_sems,
 ):
     last = flags[1] == segments - 1
-    start_sides(plan, flags, act_hbm, act_other_hbm, act_ref, piece_sems.at[0])
-    start_sides(plan, flags, cot_hbm, cot_other_hbm, cot_ref, piece_sems.at[1])
+    start_sides(plan, flags, [(act_hbm, act_other_hbm, act_ref, piece_sems.at[0]),
+                              (cot_hbm, cot_other_hbm, cot_ref, piece_sems.at[1])])
     copies = starts([(third_hbm, third_ref), (second_hbm, second_ref)], sems)
     synthesise(plan, blocks_of(wire_in_ref), second_t_ref[...], third_t_ref, spectrum_ref, cells_ref)
     arriving = [(act_ref, act_hbm, piece_sems.at[0]), (cot_ref, act_hbm, piece_sems.at[1])]
@@ -353,8 +359,8 @@
     @pl.when(flags[1] == segments - 2)
     def _():
         copies = starts([(wire_hbm, wire_ref)], sems)
-        start_sides(plan, flags, act_hbm, act_other_hbm, act_ref, piece_sems.at[0])
-        start_sides(plan, flags, cot_hbm, cot_other_hbm, cot_ref, piece_sems.at[1])
+        start_sides(plan, flags, [(act_hbm, act_other_hbm, act_ref, piece_sems.at[0]),
+                                  (cot_hbm, cot_other_hbm, cot_ref, piece_sems.at[1])])
         waits(copies)
         parts = [
             wire_ref[plan.devices, :, pl.ds(k * columns, columns)].astype(F32) for k in range(3)
@@ -497,10 +503,18 @@
     return spread.astype(BF16).reshape(plan.wire)
 
 
-def spectral_kernel(plan, backward, wire_ref, weights_ref, first_ref, first_t_ref, modes_ref, wire_out_ref):
+def inputs_kernel(plan, wire_ref, weights_ref, first_ref, first_t_ref, modes_hbm, wire_out_ref, modes_ref, sems):
     modes = mode_sums(plan, wire_ref, first_ref)
     modes_ref[...] = modes
-    spread = spread_modes(plan, mix_modes(plan, modes, weights_ref, backward), first_t_ref)
+    copies = starts([(modes_ref, modes_hbm)], sems)
+    wire_out_ref[...] = spread_modes(plan, mix_modes(plan, modes, weights_ref, False), first_t_ref)
+    waits(copies)
+
+
+def spectral_kernel(plan, wire_ref, weights_ref, first_ref, first_t_ref, modes_ref, wire_out_ref):
+    modes = mode_sums(plan, wire_ref, first_ref)
+    modes_ref[...] = modes
+    spread = spread_modes(plan, mix_modes(plan, modes, weights_ref, True), first_t_ref)
     copies = wire_out_ref.shape[0] // plan.devices
     for k in range(copies):
         wire_out_ref[pl.ds(k * plan.devices, plan.devices)] = spread
@@ -592,8 +606,8 @@
     )
     cot_other = other_core(cot)
     input_modes, wire = call(
-        functools.partial(spectral_kernel, plan, False), "mix_inputs", (exchange(wire), weights, first, first_t),
-        (modes_shape, wire_shape),
+        functools.partial(inputs_kernel, plan), "mix_inputs", (exchange(wire), weights, first, first_t),
+        (pltpu.HBM(modes_shape.shape, F32), wire_shape), [pltpu.VMEM(modes_shape.shape, F32), sems(1)],
     )
     wire_in = exchange(wire)
     if segments > 1:
@@ -607,7 +621,7 @@
 
     def mix_signal(wire, count):
         return call(
-            functools.partial(spectral_kernel, plan, True), "mix_signal", (wire, weights, first, first_t),
+            functools.partial(spectral_kernel, plan), "mix_signal", (wire, weights, first, first_t),
             (modes_shape, jax.ShapeDtypeStruct((count * plan.devices,) + plan.wire[1:], BF16)),
         )
 

time: 122 us -> 122 us (level)
  waiting for transfers between devices: 6.98 us -> 8.43 us
    ppermute x2, waiting for transfers between devices: 2.16 us -> 3.61 us  [from_behind(): return lax.ppermute(block, 'segment', route)]
where the time goes in v4:
time: 122 us; the launch traced here: 121 us
  blocking collectives  62.2 us (51%)
  Pallas kernels  42.3 us (35%)
  waiting for transfers between devices  8.43 us (7%)
  local copies, waits for them, and re-layouts  3.59 us (3%)
  starting transfers between devices  3.21 us (3%)
    all_to_all x5, blocking collectives, exchange(): return lax.all_to_all(wire, axes, split_axis=0, concat_axis=0, tiled=True)  62.2 us
    pallas_call x10, Pallas kernels, call(): pl.pallas_call(kernel, in_specs=specs, out_specs=out_specs, out_shape=out...  42.3 us
    ppermute x4, waiting for transfers between devices, other_core(): return lax.ppermute(block, 'gy', [(0, 1), (1, 0)])  4.82 us
    ppermute x2, waiting for transfers between devices, from_behind(): return lax.ppermute(block, 'segment', route)  3.61 us
    ppermute x2, starting transfers between devices, from_behind(): return lax.ppermute(block, 'segment', route)  2.56 us
  transfers between devices with their start and end apart: 6, of which 3 were waited for; matrix products, arithmetic and copies ran while one was open for 3% of the time, Pallas kernels for 15%

profile of v4, /device:TPU:0, one launch (start us, length us, event | category | flops | bytes accessed | tf_op | source)
XLA Modules:
  0.0 121.4 jit_solution(895407059734814880)
XLA Ops:
  0.6 0.5 collective-permute-start.2
  1.2 1.3 %collective-permute-start.3 = (bf16[8,1024,128]{2,1,0:T(8,128)(2,1)}, bf16[8,1024,128]{2,1,0:T(8,128)(2,1)}, u32[]{:S(2)}, u32[]{:S(2)}) collective-permute-start(bf16[8,1024,128]{2,1,0:T(8,128)(2,1)} %bitcast.12), channel_id=1, source_target_pairs={{1,0},{3,2},{5,4},{7,6},{9,8},{11,10},{13,12},{15,14},{17,16},{19,... | collective-permute-start | bytes 6291464 | tf_op jit(solution)/shard_map/ppermute | solution.py:550
  2.5 2.3 %constant_dynamic-slice_fusion = bf16[8,512,128]{2,1,0:T(8,128)(2,1)} fusion(bf16[8,1024,128]{2,1,0:T(8,128)(2,1)} %bitcast.13, s32[]{:T(128)S(6)} %select_n.4), kind=kLoop, calls=%fused_computation.4 | loop fusion | bytes 2097156 | tf_op jit(solution)/shard_map/dynamic_slice | solution.py:590
  5.0 2.3 %own_inputs.1 = (bf16[2,1024,256]{2,1,0:T(8,128)(2,1)S(1)}, bf16[2,256,1024]{2,1,0:T(8,128)(2,1)S(1)}, f32[512,256]{1,0:T(8,128)S(1)}) custom-call(bf16[8,1024,128]{2,1,0:T(8,128)(2,1)} %bitcast.14, bf16[2,1024,256]{2,1,0:T(8,128)(2,1)} %constant.28.clone.third_hbm.third_ref, bf16[2,256,1024]{2,1,0:T(8,128)(2,1)} %constant.30.clone.second_hbm.second_ref), custom_call_target="tpu_custom_call" | custom-call | tf_op jit(solution)/shard_map/own_inputs/pallas_call | solution.py:535
  7.6 2.5 %input_modes.1 = (bf16[16,16,256]{2,1,0:T(8,128)(2,1)S(1)}, bf16[8,512,128]{2,1,0:T(8,128)(2,1)}, bf16[1,16,256]{2,1,0:T(8,128)(2,1)S(1)}) custom-call(bf16[2,1024,256]{2,1,0:T(8,128)(2,1)S(1)} %get-tuple-element.38.third_ref, bf16[2,256,1024]{2,1,0:T(8,128)(2,1)S(1)} %get-tuple-element.39.second_ref, f32[512,256]{1,0:T(8,128)S(1)} %get-tuple-element.40.own_sums_ref, ...), custom_call_target="tpu_custom_call" | custom-call | tf_op jit(solution)/shard_map/input_modes/pallas_call | solution.py:535
  10.1 14.7 %all_to_all.29.wire_ref = bf16[16,16,256]{2,1,0:T(8,128)(2,1)S(1)} all-to-all(bf16[16,16,256]{2,1,0:T(8,128)(2,1)S(1)} %get-tuple-element.42), channel_id=1, replica_groups=mesh['groups'=1,'gx'=8,'gy'=2,'segment'=2] {'gy','gx'}, dimensions={0} | all-to-all | bytes 262144 | tf_op jit(solution)/shard_map/all_to_all | solution.py:544
  24.8 1.1 mix_inputs.1
  25.9 10.2 %all_to_all.30.wire_in_ref = bf16[16,16,256]{2,1,0:T(8,128)(2,1)S(1)} all-to-all(bf16[16,16,256]{2,1,0:T(8,128)(2,1)S(1)} %get-tuple-element.43), channel_id=1, replica_groups=mesh['groups'=1,'gx'=8,'gy'=2,'segment'=2] {'gy','gx'}, dimensions={0} | all-to-all | bytes 262144 | tf_op jit(solution)/shard_map/all_to_all | solution.py:544
  36.1 0.7 pad_maximum_fusion
  36.8 1.3 %collective-permute-start.4 = (bf16[17,16,256]{2,1,0:T(8,128)(2,1)}, bf16[17,16,256]{2,1,0:T(8,128)(2,1)}, u32[]{:S(2)}, u32[]{:S(2)}) collective-permute-start(bf16[17,16,256]{2,1,0:T(8,128)(2,1)} %pad_maximum_fusion), channel_id=1, source_target_pairs={{1,0},{3,2},{5,4},{7,6},{9,8},{11,10},{13,12},{15,14},{17,16},{19,... | collective-permute-start | bytes 417800 | tf_op jit(solution)/shard_map/ppermute | solution.py:550
  38.2 10.1 %first_signal.1 = (bf16[16,16,256]{2,1,0:T(8,128)(2,1)}, f32[8,1024,128]{2,1,0:T(8,128)}) custom-call(s32[2]{0:T(128)S(1)} %pad_add_fusion.flags, f32[8,9]{1,0:T(8,128)S(1)} %pad_maximum_fusion.1.mixing_ref, bf16[8,1024,128]{2,1,0:T(8,128)(2,1)} %bitcast.15, bf16[8,512,128]{2,1,0:T(8,128)(2,1)} %get-tuple-element.41.act_other_hbm, ...), custom_call_target="tpu_custom_call" | custom-call | tf_op jit(solution)/shard_map/first_signal/pallas_call | solution.py:535
  48.3 3.6 %collective-permute-done.3.act_hbm = bf16[8,1024,128]{2,1,0:T(8,128)(2,1)} collective-permute-done((bf16[8,1024,128]{2,1,0:T(8,128)(2,1)}, bf16[8,1024,128]{2,1,0:T(8,128)(2,1)}, u32[]{:S(2)}, u32[]{:S(2)}) %collective-permute-start.3) | collective-permute-done | bytes 2097184 | tf_op jit(solution)/shard_map/ppermute | solution.py:550
  51.9 4.5 %conditional.1 = (bf16[16,16,256]{2,1,0:T(8,128)(2,1)}, bf16[8,1024,128]{2,1,0:T(8,128)(2,1)}) conditional(s32[]{:T(128)} %convert_element_type.5, (bf16[8,1024,128]{2,1,0:T(8,128)(2,1)}, bf16[16,16,256]{2,1,0:T(8,128)(2,1)}) %tuple.18, (bf16[16,16,256]{2,1,0:T(8,128)(2,1)}, s32[2]{0:T(128)S(1)}) %tuple.19), branch_computations={%region_0.1_spmd, %region_1.2_spmd} | conditional | bytes 8388664 | solution.py:638
  51.9 4.5 %collective-permute-done = bf16[8,1024,128]{2,1,0:T(8,128)(2,1)} collective-permute-done((bf16[8,1024,128]{2,1,0:T(8,128)(2,1)}, bf16[8,1024,128]{2,1,0:T(8,128)(2,1)}, u32[]{:S(2)}, u32[]{:S(2)}) %collective-permute-start) | collective-permute-done | bytes 2097184 | tf_op jit(solution)/shard_map/cond/branch_0_fun/ppermute | solution.py:554
  56.4 12.0 %shared.1.local_ref = f32[8,1024,128]{2,1,0:T(8,128)S(1)} custom-call(s32[2]{0:T(128)S(1)} %pad_add_fusion.flags, bf16[8,1024,128]{2,1,0:T(8,128)(2,1)} %collective-permute-done.3.act_hbm, bf16[8,1024,128]{2,1,0:T(8,128)(2,1)} %get-tuple-element.49.act_other_hbm, bf16[8,1024,128]{2,1,0:T(8,128)(2,1)} %bitcast.18, ...), custom_call_target="tpu_custom_call" | custom-call | tf_op jit(solution)/shard_map/shared/pallas_call | solution.py:535
  68.4 1.2 mix_signal.2
  69.6 16.3 %all_to_all.31.wire_in_ref.kept_wire_ref = bf16[32,16,256]{2,1,0:T(8,128)(2,1)S(1)} all-to-all(bf16[32,16,256]{2,1,0:T(8,128)(2,1)S(1)} %get-tuple-element.53), channel_id=1, replica_groups=mesh['groups'=1,'gx'=8,'gy'=2,'segment'=2] {'segment','gy','gx'}, dimensions={0} | all-to-all | bytes 524288 | tf_op jit(solution)/shard_map/all_to_all | solution.py:544
  85.9 8.4 %next_signal.1 = (bf16[16,16,256]{2,1,0:T(8,128)(2,1)S(1)}, f32[8,1024,128]{2,1,0:T(8,128)S(1)}) custom-call(s32[2]{0:T(128)S(1)} %pad_add_fusion.flags, f32[8,9]{1,0:T(8,128)S(1)} %pad_maximum_fusion.1.mixing_ref, f32[8,1024,128]{2,1,0:T(8,128)} %get-tuple-element.44.kept_hbm, f32[8,1024,128]{2,1,0:T(8,128)S(1)} %shared.1.local_ref, ...), custom_call_target="tpu_custom_call" | custom-call | tf_op jit(solution)/shard_map/next_signal/pallas_call | solution.py:535
  94.3 10.8 %all_to_all.32.wire_ref = bf16[16,16,256]{2,1,0:T(8,128)(2,1)S(1)} all-to-all(bf16[16,16,256]{2,1,0:T(8,128)(2,1)S(1)} %get-tuple-element.55), channel_id=1, replica_groups=mesh['groups'=1,'gx'=8,'gy'=2,'segment'=2] {'gy','gx'}, dimensions={0} | all-to-all | bytes 262144 | tf_op jit(solution)/shard_map/all_to_all | solution.py:544
  105.1 1.2 mix_signal.3
  106.3 10.2 %all_to_all.33.wire_in_ref = bf16[16,16,256]{2,1,0:T(8,128)(2,1)S(1)} all-to-all(bf16[16,16,256]{2,1,0:T(8,128)(2,1)S(1)} %get-tuple-element.56), channel_id=1, replica_groups=mesh['groups'=1,'gx'=8,'gy'=2,'segment'=2] {'gy','gx'}, dimensions={0} | all-to-all | bytes 262144 | tf_op jit(solution)/shard_map/all_to_all | solution.py:544
  116.5 1.0 last_other.1
  117.6 2.7 %last_own.1 = (bf16[8,1024,128]{2,1,0:T(8,128)(2,1)}, f32[64,8,8,32]{3,2,1,0:T(8,128)}) custom-call(f32[8,1024,128]{2,1,0:T(8,128)S(1)} %get-tuple-element.54.local_ref, bf16[256,1024]{1,0:T(8,128)(2,1)S(1)} %copy-done.2, bf16[1024,256]{1,0:T(8,128)(2,1)S(1)} %copy-done.1, bf16[16,16,256]{2,1,0:T(8,128)(2,1)S(1)} %all_to_all.33.wire_in_ref, ...), custom_call_target="tpu_custom_call" | custom-call | tf_op jit(solution)/shard_map/last_own/pallas_call | solution.py:535
  120.3 1.2 constant_dynamic-update-slice_fusion
  (33 shorter events, 0.8 us)
Async XLA Ops:
  0.6 4.2 %copy-start.10 = (f32[1,8]{1,0:T(1,128)S(1)}, f32[1,8]{1,0:T(1,128)}, u32[]{:S(2)}) copy-start(f32[1,8]{1,0:T(1,128)} %param.17) | copy-start | bytes 100
  0.6 4.2 %copy-start.9 = (f32[1,8,8]{2,1,0:T(8,128)S(1)}, f32[1,8,8]{2,1,0:T(8,128)}, u32[]{:S(2)}) copy-start(f32[1,8,8]{2,1,0:T(8,128)} %param.16) | copy-start | bytes 772
  0.6 37.5 %collective-permute-start.2 = (bf16[8,1024,128]{2,1,0:T(8,128)(2,1)}, bf16[8,1024,128]{2,1,0:T(8,128)(2,1)}, u32[]{:S(2)}, u32[]{:S(2)}) collective-permute-start(bf16[8,1024,128]{2,1,0:T(8,128)(2,1)} %bitcast.16), channel_id=1, source_target_pairs={{0,2},{2,0},{1,3},{3,1},{4,6},{6,4},{5,7},{7,5},{8,10},{10,8},{9,1... | collective-permute-start | bytes 6291464 | tf_op jit(solution)/shard_map/ppermute | solution.py:554
  1.2 50.7 %collective-permute-start.3 = (bf16[8,1024,128]{2,1,0:T(8,128)(2,1)}, bf16[8,1024,128]{2,1,0:T(8,128)(2,1)}, u32[]{:S(2)}, u32[]{:S(2)}) collective-permute-start(bf16[8,1024,128]{2,1,0:T(8,128)(2,1)} %bitcast.12), channel_id=1, source_target_pairs={{1,0},{3,2},{5,4},{7,6},{9,8},{11,10},{13,12},{15,14},{17,16},{19,... | collective-permute-start | bytes 6291464 | tf_op jit(solution)/shard_map/ppermute | solution.py:550
  4.7 2.9 %collective-permute-start.1 = (bf16[8,512,128]{2,1,0:T(8,128)(2,1)}, bf16[8,512,128]{2,1,0:T(8,128)(2,1)S(1)}, u32[]{:S(2)}, u32[]{:S(2)}) collective-permute-start(bf16[8,512,128]{2,1,0:T(8,128)(2,1)} %constant_dynamic-slice_fusion), channel_id=1, source_target_pairs={{0,2},{2,0},{1,3},{3,1},{4,6},{6,4},{5,7},{7,5},{8,10},{10,8},{9,1... | collective-permute-start | bytes 3145736 | tf_op jit(solution)/shard_map/ppermute | solution.py:554
  7.3 17.5 %copy-start = (f32[1,16,4,8,8,32]{5,4,3,2,1,0:T(8,128)S(1)}, f32[1,16,4,8,8,32]{5,4,3,2,1,0:T(8,128)}, u32[]{:S(2)}) copy-start(f32[1,16,4,8,8,32]{5,4,3,2,1,0:T(8,128)} %param.15) | copy-start | bytes 1572868
  7.3 17.5 %copy-start.5 = (bf16[2,256,64]{2,1,0:T(8,128)(2,1)S(1)}, bf16[2,256,64]{2,1,0:T(8,128)(2,1)}, u32[]{:S(2)}) copy-start(bf16[2,256,64]{2,1,0:T(8,128)(2,1)} %constant.33.clone.first_t_ref) | copy-start | bytes 196612
  7.3 17.5 %copy-start.6 = (bf16[2,64,256]{2,1,0:T(8,128)(2,1)S(1)}, bf16[2,64,256]{2,1,0:T(8,128)(2,1)}, u32[]{:S(2)}) copy-start(bf16[2,64,256]{2,1,0:T(8,128)(2,1)} %constant.32.clone.first_ref) | copy-start | bytes 196612
  10.1 28.1 %copy-start.1 = (bf16[1024,256]{1,0:T(8,128)(2,1)S(1)}, bf16[1024,256]{1,0:T(8,128)(2,1)}, u32[]{:S(2)}) copy-start(bf16[1024,256]{1,0:T(8,128)(2,1)} %constant.31.clone.second_t_ref) | copy-start | bytes 1572868
  10.1 28.1 %copy-start.2 = (bf16[256,1024]{1,0:T(8,128)(2,1)S(1)}, bf16[256,1024]{1,0:T(8,128)(2,1)}, u32[]{:S(2)}) copy-start(bf16[256,1024]{1,0:T(8,128)(2,1)} %constant.29.clone.third_t_ref) | copy-start | bytes 1572868
  36.8 19.6 %collective-permute-start.4 = (bf16[17,16,256]{2,1,0:T(8,128)(2,1)}, bf16[17,16,256]{2,1,0:T(8,128)(2,1)}, u32[]{:S(2)}, u32[]{:S(2)}) collective-permute-start(bf16[17,16,256]{2,1,0:T(8,128)(2,1)} %pad_maximum_fusion), channel_id=1, source_target_pairs={{1,0},{3,2},{5,4},{7,6},{9,8},{11,10},{13,12},{15,14},{17,16},{19,... | collective-permute-start | bytes 417800 | tf_op jit(solution)/shard_map/ppermute | solution.py:550
  51.9 4.5 %collective-permute-start = (bf16[8,1024,128]{2,1,0:T(8,128)(2,1)}, bf16[8,1024,128]{2,1,0:T(8,128)(2,1)}, u32[]{:S(2)}, u32[]{:S(2)}) collective-permute-start(bf16[8,1024,128]{2,1,0:T(8,128)(2,1)} %get-tuple-element.9), channel_id=1, source_target_pairs={{0,2},{2,0},{1,3},{3,1},{4,6},{6,4},{5,7},{7,5},{8,10},{10,8},{9,1... | collective-permute-start | bytes 6291464 | tf_op jit(solution)/shard_map/cond/branch_0_fun/ppermute | solution.py:554
  56.4 12.0 %copy-start.8 = (bf16[16,16,256]{2,1,0:T(8,128)(2,1)S(1)}, bf16[16,16,256]{2,1,0:T(8,128)(2,1)}, u32[]{:S(2)}) copy-start(bf16[16,16,256]{2,1,0:T(8,128)(2,1)} %get-tuple-element.52.wire_ref) | copy-start | bytes 393220
  68.4 17.5 %copy-start.3 = (bf16[2,256,1024]{2,1,0:T(8,128)(2,1)S(1)}, bf16[2,256,1024]{2,1,0:T(8,128)(2,1)}, u32[]{:S(2)}) copy-start(bf16[2,256,1024]{2,1,0:T(8,128)(2,1)} %constant.30.clone.second_hbm.second_ref) | copy-start | bytes 3145732
  68.4 17.5 %copy-start.4 = (bf16[2,1024,256]{2,1,0:T(8,128)(2,1)S(1)}, bf16[2,1024,256]{2,1,0:T(8,128)(2,1)}, u32[]{:S(2)}) copy-start(bf16[2,1024,256]{2,1,0:T(8,128)(2,1)} %constant.28.clone.third_hbm.third_ref) | copy-start | bytes 3145732
  116.5 1.1 copy-start.7
  117.5 2.8 %collective-permute-start.5 = (bf16[8,512,128]{2,1,0:T(8,128)(2,1)S(1)}, bf16[8,512,128]{2,1,0:T(8,128)(2,1)S(1)}, u32[]{:S(2)}, u32[]{:S(2)}) collective-permute-start(bf16[8,512,128]{2,1,0:T(8,128)(2,1)S(1)} %last_other.1), channel_id=1, source_target_pairs={{0,2},{2,0},{1,3},{3,1},{4,6},{6,4},{5,7},{7,5},{8,10},{10,8},{9,1... | collective-permute-start | bytes 3145736 | tf_op jit(solution)/shard_map/ppermute | solution.py:554

commit v5 on v4

--- a/solution.py
+++ b/solution.py
@@ -178,13 +178,6 @@
                 pltpu.make_async_copy(ref.at[:, rows], target.at[:, rows], sems.at[piece]).start()
 
 
-def start_pieces(plan, arriving):
-    for k in range(plan.pieces):
-        rows = piece_rows(plan, k)
-        for ref, source, sems in arriving:
-            pltpu.make_async_copy(source.at[:, rows], ref.at[:, rows], sems.at[k]).start()
-
-
 def start_sides(plan, flags, arrays):
     per_side = plan.pieces // plan.count_y
     for which in range(plan.count_y):
@@ -385,21 +378,19 @@
 
 
 def middle_kernel(
-    plan, segments, turn, flags, mixing_ref, kept_hbm, local_ref, wire_in_ref, third_ref, third_t_ref, second_ref,
+    plan, segments, turn, flags, mixing_ref, kept_ref, local_ref, wire_in_ref, third_ref, third_t_ref, second_ref,
     second_t_ref, wire_ref, local_out_ref,
-    kept_ref, total_ref, spectrum_ref, cells_ref, signals_ref, sems, piece_sems,
+    total_ref, spectrum_ref, cells_ref, signals_ref, sems,
 ):
     segment = flags[1]
     active = segments - 1 - turn
-    kept = (kept_ref, kept_hbm, piece_sems.at[0])
 
     @pl.when(segment < active)
     def _():
-        start_pieces(plan, [kept])
         synthesise(plan, lambda device, lanes: wire_in_ref[active * plan.devices + device, :, lanes],
                    second_t_ref[...], third_t_ref, spectrum_ref, cells_ref)
 
-        def work(which, in_side, rows):
+        def work(rows):
             signals = []
             for i in range(plan.channels):
                 grad = local_ref[i, rows, :] + cells_ref[rows, lanes_of(plan, i)]
@@ -408,20 +399,18 @@
             for i in range(plan.channels):
                 local_out_ref[i, rows, :] = mixed_with(plan, mixing_ref, signals, i, True)
 
-        each_piece(plan, flags, [work], [kept])
+        each_chunk(plan.rows, CHUNK, work)
         finish(plan, sums_over_z(signals_ref[...], third_ref), second_ref, total_ref, wire_ref)
 
     @pl.when(segment >= active)
     def _():
         if turn == 0:
-            start_pieces(plan, [kept])
-
-            def work(which, in_side, rows):
+            def work(rows):
                 signals = [kept_ref[o, rows, :] for o in range(plan.channels)]
                 for i in range(plan.channels):
                     local_out_ref[i, rows, :] = mixed_with(plan, mixing_ref, signals, i, True)
 
-            each_piece(plan, flags, [work], [kept])
+            each_chunk(plan.rows, CHUNK, work)
         else:
             waits(starts([(local_ref, local_out_ref)], sems))
 
@@ -664,7 +653,7 @@
             functools.partial(middle_kernel, plan, segments, turn), "next_signal",
             (flags, mixing, kept, local, wires, third, third_t, second, second_t),
             (wire_shape, jax.ShapeDtypeStruct(plan.field, F32)),
-            [wide_scratch, total, spectrum, cells, signals, sems(2), piece_sems], 2, 1,
+            [total, spectrum, cells, signals, sems(2)], 2,
         )
     if segments == 1:
         local = jnp.einsum("oi,oyz->iyz", pointwise[0], kept, precision=lax.Precision.HIGHEST)

time: 122 us -> 122 us (level)
  no operation moved by 1% of the time
where the time goes in v5:
time: 122 us
  blocking collectives  62.3 us (51%)
  Pallas kernels  42.6 us (35%)
  waiting for transfers between devices  8.4 us (7%)
  local copies, waits for them, and re-layouts  3.59 us (3%)
  starting transfers between devices  3.21 us (3%)
    all_to_all x5, blocking collectives, exchange(): return lax.all_to_all(wire, axes, split_axis=0, concat_axis=0, tiled=True)  62.3 us
    pallas_call x10, Pallas kernels, call(): pl.pallas_call(kernel, in_specs=specs, out_specs=out_specs, out_shape=out...  42.6 us
    ppermute x4, waiting for transfers between devices, other_core(): return lax.ppermute(block, 'gy', [(0, 1), (1, 0)])  4.82 us
    ppermute x2, waiting for transfers between devices, from_behind(): return lax.ppermute(block, 'segment', route)  3.58 us
    ppermute x2, starting transfers between devices, from_behind(): return lax.ppermute(block, 'segment', route)  2.56 us
  transfers between devices with their start and end apart: 6, of which 3 were waited for; matrix products, arithmetic and copies ran while one was open for 3% of the time, Pallas kernels for 15%

profile of v5, /device:TPU:0, one launch (start us, length us, event | category | flops | bytes accessed | tf_op | source)
XLA Modules:
  0.0 121.7 jit_solution(159025471814650601)
XLA Ops:
  0.6 0.5 collective-permute-start.2
  1.2 1.3 %collective-permute-start.3 = (bf16[8,1024,128]{2,1,0:T(8,128)(2,1)}, bf16[8,1024,128]{2,1,0:T(8,128)(2,1)}, u32[]{:S(2)}, u32[]{:S(2)}) collective-permute-start(bf16[8,1024,128]{2,1,0:T(8,128)(2,1)} %bitcast.12), channel_id=1, source_target_pairs={{1,0},{3,2},{5,4},{7,6},{9,8},{11,10},{13,12},{15,14},{17,16},{19,... | collective-permute-start | bytes 6291464 | tf_op jit(solution)/shard_map/ppermute | solution.py:539
  2.5 2.3 %constant_dynamic-slice_fusion = bf16[8,512,128]{2,1,0:T(8,128)(2,1)} fusion(bf16[8,1024,128]{2,1,0:T(8,128)(2,1)} %bitcast.13, s32[]{:T(128)S(6)} %select_n.4), kind=kLoop, calls=%fused_computation.4 | loop fusion | bytes 2097156 | tf_op jit(solution)/shard_map/dynamic_slice | solution.py:579
  5.0 2.3 %own_inputs.1 = (bf16[2,1024,256]{2,1,0:T(8,128)(2,1)S(1)}, bf16[2,256,1024]{2,1,0:T(8,128)(2,1)S(1)}, f32[512,256]{1,0:T(8,128)S(1)}) custom-call(bf16[8,1024,128]{2,1,0:T(8,128)(2,1)} %bitcast.14, bf16[2,1024,256]{2,1,0:T(8,128)(2,1)} %constant.28.clone.third_hbm.third_ref, bf16[2,256,1024]{2,1,0:T(8,128)(2,1)} %constant.30.clone.second_hbm.second_ref), custom_call_target="tpu_custom_call" | custom-call | tf_op jit(solution)/shard_map/own_inputs/pallas_call | solution.py:524
  7.6 2.5 %input_modes.1 = (bf16[16,16,256]{2,1,0:T(8,128)(2,1)S(1)}, bf16[8,512,128]{2,1,0:T(8,128)(2,1)}, bf16[1,16,256]{2,1,0:T(8,128)(2,1)S(1)}) custom-call(bf16[2,1024,256]{2,1,0:T(8,128)(2,1)S(1)} %get-tuple-element.38.third_ref, bf16[2,256,1024]{2,1,0:T(8,128)(2,1)S(1)} %get-tuple-element.39.second_ref, f32[512,256]{1,0:T(8,128)S(1)} %get-tuple-element.40.own_sums_ref, ...), custom_call_target="tpu_custom_call" | custom-call | tf_op jit(solution)/shard_map/input_modes/pallas_call | solution.py:524
  10.1 14.7 %all_to_all.29.wire_ref = bf16[16,16,256]{2,1,0:T(8,128)(2,1)S(1)} all-to-all(bf16[16,16,256]{2,1,0:T(8,128)(2,1)S(1)} %get-tuple-element.42), channel_id=1, replica_groups=mesh['groups'=1,'gx'=8,'gy'=2,'segment'=2] {'gy','gx'}, dimensions={0} | all-to-all | bytes 262144 | tf_op jit(solution)/shard_map/all_to_all | solution.py:533
  24.8 1.1 mix_inputs.1
  25.9 10.2 %all_to_all.30.wire_in_ref = bf16[16,16,256]{2,1,0:T(8,128)(2,1)S(1)} all-to-all(bf16[16,16,256]{2,1,0:T(8,128)(2,1)S(1)} %get-tuple-element.43), channel_id=1, replica_groups=mesh['groups'=1,'gx'=8,'gy'=2,'segment'=2] {'gy','gx'}, dimensions={0} | all-to-all | bytes 262144 | tf_op jit(solution)/shard_map/all_to_all | solution.py:533
  36.1 0.7 pad_maximum_fusion
  36.8 1.3 %collective-permute-start.4 = (bf16[17,16,256]{2,1,0:T(8,128)(2,1)}, bf16[17,16,256]{2,1,0:T(8,128)(2,1)}, u32[]{:S(2)}, u32[]{:S(2)}) collective-permute-start(bf16[17,16,256]{2,1,0:T(8,128)(2,1)} %pad_maximum_fusion), channel_id=1, source_target_pairs={{1,0},{3,2},{5,4},{7,6},{9,8},{11,10},{13,12},{15,14},{17,16},{19,... | collective-permute-start | bytes 417800 | tf_op jit(solution)/shard_map/ppermute | solution.py:539
  38.2 10.1 %first_signal.1 = (bf16[16,16,256]{2,1,0:T(8,128)(2,1)}, f32[8,1024,128]{2,1,0:T(8,128)}) custom-call(s32[2]{0:T(128)S(1)} %pad_add_fusion.flags, f32[8,9]{1,0:T(8,128)S(1)} %pad_maximum_fusion.1.mixing_ref, bf16[8,1024,128]{2,1,0:T(8,128)(2,1)} %bitcast.15, bf16[8,512,128]{2,1,0:T(8,128)(2,1)} %get-tuple-element.41.act_other_hbm, ...), custom_call_target="tpu_custom_call" | custom-call | tf_op jit(solution)/shard_map/first_signal/pallas_call | solution.py:524
  48.3 3.6 %collective-permute-done.3.act_hbm = bf16[8,1024,128]{2,1,0:T(8,128)(2,1)} collective-permute-done((bf16[8,1024,128]{2,1,0:T(8,128)(2,1)}, bf16[8,1024,128]{2,1,0:T(8,128)(2,1)}, u32[]{:S(2)}, u32[]{:S(2)}) %collective-permute-start.3) | collective-permute-done | bytes 2097184 | tf_op jit(solution)/shard_map/ppermute | solution.py:539
  51.9 4.5 %conditional.1 = (bf16[16,16,256]{2,1,0:T(8,128)(2,1)}, bf16[8,1024,128]{2,1,0:T(8,128)(2,1)}) conditional(s32[]{:T(128)} %convert_element_type.5, (bf16[8,1024,128]{2,1,0:T(8,128)(2,1)}, bf16[16,16,256]{2,1,0:T(8,128)(2,1)}) %tuple.18, (bf16[16,16,256]{2,1,0:T(8,128)(2,1)}, s32[2]{0:T(128)S(1)}) %tuple.19), branch_computations={%region_0.1_spmd, %region_1.2_spmd} | conditional | bytes 8388664 | solution.py:627
  51.9 4.5 %collective-permute-done = bf16[8,1024,128]{2,1,0:T(8,128)(2,1)} collective-permute-done((bf16[8,1024,128]{2,1,0:T(8,128)(2,1)}, bf16[8,1024,128]{2,1,0:T(8,128)(2,1)}, u32[]{:S(2)}, u32[]{:S(2)}) %collective-permute-start) | collective-permute-done | bytes 2097184 | tf_op jit(solution)/shard_map/cond/branch_0_fun/ppermute | solution.py:543
  56.4 12.4 %shared.1.local_ref = f32[8,1024,128]{2,1,0:T(8,128)S(1)} custom-call(s32[2]{0:T(128)S(1)} %pad_add_fusion.flags, bf16[8,1024,128]{2,1,0:T(8,128)(2,1)} %collective-permute-done.3.act_hbm, bf16[8,1024,128]{2,1,0:T(8,128)(2,1)} %get-tuple-element.49.act_other_hbm, bf16[8,1024,128]{2,1,0:T(8,128)(2,1)} %bitcast.18, ...), custom_call_target="tpu_custom_call" | custom-call | tf_op jit(solution)/shard_map/shared/pallas_call | solution.py:524
  68.8 1.2 mix_signal.2
  70.0 16.3 %all_to_all.31.wire_in_ref.kept_wire_ref = bf16[32,16,256]{2,1,0:T(8,128)(2,1)S(1)} all-to-all(bf16[32,16,256]{2,1,0:T(8,128)(2,1)S(1)} %get-tuple-element.53), channel_id=1, replica_groups=mesh['groups'=1,'gx'=8,'gy'=2,'segment'=2] {'segment','gy','gx'}, dimensions={0} | all-to-all | bytes 524288 | tf_op jit(solution)/shard_map/all_to_all | solution.py:533
  86.3 8.3 %next_signal.1 = (bf16[16,16,256]{2,1,0:T(8,128)(2,1)S(1)}, f32[8,1024,128]{2,1,0:T(8,128)S(1)}) custom-call(s32[2]{0:T(128)S(1)} %pad_add_fusion.flags, f32[8,9]{1,0:T(8,128)S(1)} %pad_maximum_fusion.1.mixing_ref, f32[8,1024,128]{2,1,0:T(8,128)S(1)} %copy-done.5, f32[8,1024,128]{2,1,0:T(8,128)S(1)} %shared.1.local_ref, ...), custom_call_target="tpu_custom_call" | custom-call | tf_op jit(solution)/shard_map/next_signal/pallas_call | solution.py:524
  94.6 10.8 %all_to_all.32.wire_ref = bf16[16,16,256]{2,1,0:T(8,128)(2,1)S(1)} all-to-all(bf16[16,16,256]{2,1,0:T(8,128)(2,1)S(1)} %get-tuple-element.55), channel_id=1, replica_groups=mesh['groups'=1,'gx'=8,'gy'=2,'segment'=2] {'gy','gx'}, dimensions={0} | all-to-all | bytes 262144 | tf_op jit(solution)/shard_map/all_to_all | solution.py:533
  105.4 1.2 mix_signal.3
  106.6 10.2 %all_to_all.33.wire_in_ref = bf16[16,16,256]{2,1,0:T(8,128)(2,1)S(1)} all-to-all(bf16[16,16,256]{2,1,0:T(8,128)(2,1)S(1)} %get-tuple-element.56), channel_id=1, replica_groups=mesh['groups'=1,'gx'=8,'gy'=2,'segment'=2] {'gy','gx'}, dimensions={0} | all-to-all | bytes 262144 | tf_op jit(solution)/shard_map/all_to_all | solution.py:533
  116.8 1.0 last_other.1
  117.9 2.7 %last_own.1 = (bf16[8,1024,128]{2,1,0:T(8,128)(2,1)}, f32[64,8,8,32]{3,2,1,0:T(8,128)}) custom-call(f32[8,1024,128]{2,1,0:T(8,128)S(1)} %get-tuple-element.54.local_ref, bf16[256,1024]{1,0:T(8,128)(2,1)S(1)} %copy-done.2, bf16[1024,256]{1,0:T(8,128)(2,1)S(1)} %copy-done.1, bf16[16,16,256]{2,1,0:T(8,128)(2,1)S(1)} %all_to_all.33.wire_in_ref, ...), custom_call_target="tpu_custom_call" | custom-call | tf_op jit(solution)/shard_map/last_own/pallas_call | solution.py:524
  120.6 1.2 constant_dynamic-update-slice_fusion
  (35 shorter events, 0.8 us)
Async XLA Ops:
  0.6 4.2 %copy-start.11 = (f32[1,8]{1,0:T(1,128)S(1)}, f32[1,8]{1,0:T(1,128)}, u32[]{:S(2)}) copy-start(f32[1,8]{1,0:T(1,128)} %param.17) | copy-start | bytes 100
  0.6 4.2 %copy-start.10 = (f32[1,8,8]{2,1,0:T(8,128)S(1)}, f32[1,8,8]{2,1,0:T(8,128)}, u32[]{:S(2)}) copy-start(f32[1,8,8]{2,1,0:T(8,128)} %param.16) | copy-start | bytes 772
  0.6 37.5 %collective-permute-start.2 = (bf16[8,1024,128]{2,1,0:T(8,128)(2,1)}, bf16[8,1024,128]{2,1,0:T(8,128)(2,1)}, u32[]{:S(2)}, u32[]{:S(2)}) collective-permute-start(bf16[8,1024,128]{2,1,0:T(8,128)(2,1)} %bitcast.16), channel_id=1, source_target_pairs={{0,2},{2,0},{1,3},{3,1},{4,6},{6,4},{5,7},{7,5},{8,10},{10,8},{9,1... | collective-permute-start | bytes 6291464 | tf_op jit(solution)/shard_map/ppermute | solution.py:543
  1.2 50.7 %collective-permute-start.3 = (bf16[8,1024,128]{2,1,0:T(8,128)(2,1)}, bf16[8,1024,128]{2,1,0:T(8,128)(2,1)}, u32[]{:S(2)}, u32[]{:S(2)}) collective-permute-start(bf16[8,1024,128]{2,1,0:T(8,128)(2,1)} %bitcast.12), channel_id=1, source_target_pairs={{1,0},{3,2},{5,4},{7,6},{9,8},{11,10},{13,12},{15,14},{17,16},{19,... | collective-permute-start | bytes 6291464 | tf_op jit(solution)/shard_map/ppermute | solution.py:539
  4.7 2.9 %collective-permute-start.1 = (bf16[8,512,128]{2,1,0:T(8,128)(2,1)}, bf16[8,512,128]{2,1,0:T(8,128)(2,1)S(1)}, u32[]{:S(2)}, u32[]{:S(2)}) collective-permute-start(bf16[8,512,128]{2,1,0:T(8,128)(2,1)} %constant_dynamic-slice_fusion), channel_id=1, source_target_pairs={{0,2},{2,0},{1,3},{3,1},{4,6},{6,4},{5,7},{7,5},{8,10},{10,8},{9,1... | collective-permute-start | bytes 3145736 | tf_op jit(solution)/shard_map/ppermute | solution.py:543
  7.3 17.5 %copy-start = (f32[1,16,4,8,8,32]{5,4,3,2,1,0:T(8,128)S(1)}, f32[1,16,4,8,8,32]{5,4,3,2,1,0:T(8,128)}, u32[]{:S(2)}) copy-start(f32[1,16,4,8,8,32]{5,4,3,2,1,0:T(8,128)} %param.15) | copy-start | bytes 1572868
  7.3 17.5 %copy-start.6 = (bf16[2,256,64]{2,1,0:T(8,128)(2,1)S(1)}, bf16[2,256,64]{2,1,0:T(8,128)(2,1)}, u32[]{:S(2)}) copy-start(bf16[2,256,64]{2,1,0:T(8,128)(2,1)} %constant.33.clone.first_t_ref) | copy-start | bytes 196612
  7.3 17.5 %copy-start.7 = (bf16[2,64,256]{2,1,0:T(8,128)(2,1)S(1)}, bf16[2,64,256]{2,1,0:T(8,128)(2,1)}, u32[]{:S(2)}) copy-start(bf16[2,64,256]{2,1,0:T(8,128)(2,1)} %constant.32.clone.first_ref) | copy-start | bytes 196612
  10.1 28.1 %copy-start.1 = (bf16[1024,256]{1,0:T(8,128)(2,1)S(1)}, bf16[1024,256]{1,0:T(8,128)(2,1)}, u32[]{:S(2)}) copy-start(bf16[1024,256]{1,0:T(8,128)(2,1)} %constant.31.clone.second_t_ref) | copy-start | bytes 1572868
  10.1 28.1 %copy-start.2 = (bf16[256,1024]{1,0:T(8,128)(2,1)S(1)}, bf16[256,1024]{1,0:T(8,128)(2,1)}, u32[]{:S(2)}) copy-start(bf16[256,1024]{1,0:T(8,128)(2,1)} %constant.29.clone.third_t_ref) | copy-start | bytes 1572868
  36.8 19.6 %collective-permute-start.4 = (bf16[17,16,256]{2,1,0:T(8,128)(2,1)}, bf16[17,16,256]{2,1,0:T(8,128)(2,1)}, u32[]{:S(2)}, u32[]{:S(2)}) collective-permute-start(bf16[17,16,256]{2,1,0:T(8,128)(2,1)} %pad_maximum_fusion), channel_id=1, source_target_pairs={{1,0},{3,2},{5,4},{7,6},{9,8},{11,10},{13,12},{15,14},{17,16},{19,... | collective-permute-start | bytes 417800 | tf_op jit(solution)/shard_map/ppermute | solution.py:539
  51.9 4.5 %collective-permute-start = (bf16[8,1024,128]{2,1,0:T(8,128)(2,1)}, bf16[8,1024,128]{2,1,0:T(8,128)(2,1)}, u32[]{:S(2)}, u32[]{:S(2)}) collective-permute-start(bf16[8,1024,128]{2,1,0:T(8,128)(2,1)} %get-tuple-element.9), channel_id=1, source_target_pairs={{0,2},{2,0},{1,3},{3,1},{4,6},{6,4},{5,7},{7,5},{8,10},{10,8},{9,1... | collective-permute-start | bytes 6291464 | tf_op jit(solution)/shard_map/cond/branch_0_fun/ppermute | solution.py:543
  56.4 12.4 %copy-start.9 = (bf16[16,16,256]{2,1,0:T(8,128)(2,1)S(1)}, bf16[16,16,256]{2,1,0:T(8,128)(2,1)}, u32[]{:S(2)}) copy-start(bf16[16,16,256]{2,1,0:T(8,128)(2,1)} %get-tuple-element.52.wire_ref) | copy-start | bytes 393220
  56.4 30.0 %copy-start.5 = (f32[8,1024,128]{2,1,0:T(8,128)S(1)}, f32[8,1024,128]{2,1,0:T(8,128)}, u32[]{:S(2)}) copy-start(f32[8,1024,128]{2,1,0:T(8,128)} %get-tuple-element.44.kept_ref) | copy-start | bytes 12582916
  68.8 17.5 %copy-start.3 = (bf16[2,256,1024]{2,1,0:T(8,128)(2,1)S(1)}, bf16[2,256,1024]{2,1,0:T(8,128)(2,1)}, u32[]{:S(2)}) copy-start(bf16[2,256,1024]{2,1,0:T(8,128)(2,1)} %constant.30.clone.second_hbm.second_ref) | copy-start | bytes 3145732
  68.8 17.5 %copy-start.4 = (bf16[2,1024,256]{2,1,0:T(8,128)(2,1)S(1)}, bf16[2,1024,256]{2,1,0:T(8,128)(2,1)}, u32[]{:S(2)}) copy-start(bf16[2,1024,256]{2,1,0:T(8,128)(2,1)} %constant.28.clone.third_hbm.third_ref) | copy-start | bytes 3145732
  116.8 1.1 copy-start.8
  117.8 2.8 %collective-permute-start.5 = (bf16[8,512,128]{2,1,0:T(8,128)(2,1)S(1)}, bf16[8,512,128]{2,1,0:T(8,128)(2,1)S(1)}, u32[]{:S(2)}, u32[]{:S(2)}) collective-permute-start(bf16[8,512,128]{2,1,0:T(8,128)(2,1)S(1)} %last_other.1), channel_id=1, source_target_pairs={{0,2},{2,0},{1,3},{3,1},{4,6},{6,4},{5,7},{7,5},{8,10},{10,8},{9,1... | collective-permute-start | bytes 3145736 | tf_op jit(solution)/shard_map/ppermute | solution.py:543

commit v6 on v4

--- a/solution.py
+++ b/solution.py
@@ -491,10 +491,17 @@
             mixed = mixed + weights_ref[:, i] * modes[:, i : i + 1, :]
         return mixed
     row = lax.broadcasted_iota(jnp.int32, modes.shape, 1)
-    mixed = jnp.zeros_like(modes)
-    for i in range(plan.channels):
-        mixed = jnp.where(row == i, jnp.sum(weights_ref[:, i] * modes, axis=1, keepdims=True), mixed)
-    return mixed
+    count = plan.channels
+    terms = [weights_ref[:, i] * modes for i in range(count)]
+    while len(terms) > 1:
+        half = len(terms) // 2
+        low = row // half % 2 == 0
+        pairs = []
+        for a, b in zip(terms[:half], terms[half:]):
+            kept, moved = jnp.where(low, a, b), jnp.where(low, b, a)
+            pairs.append(kept + jnp.where(low, pltpu.roll(moved, count - half, 1), pltpu.roll(moved, half, 1)))
+        terms = pairs
+    return terms[0]
 
 
 def spread_modes(plan, mixed, first_t_ref):

time: 122 us -> 121 us (level)
  no operation moved by 1% of the time
where the time goes in v6:
time: 121 us
  blocking collectives  62.2 us (51%)
  Pallas kernels  41.8 us (35%)
  waiting for transfers between devices  8.43 us (7%)
  local copies, waits for them, and re-layouts  3.59 us (3%)
  starting transfers between devices  3.21 us (3%)
    all_to_all x5, blocking collectives, exchange(): return lax.all_to_all(wire, axes, split_axis=0, concat_axis=0, tiled=True)  62.2 us
    pallas_call x10, Pallas kernels, call(): pl.pallas_call(kernel, in_specs=specs, out_specs=out_specs, out_shape=out...  41.8 us
    ppermute x4, waiting for transfers between devices, other_core(): return lax.ppermute(block, 'gy', [(0, 1), (1, 0)])  4.82 us
    ppermute x2, waiting for transfers between devices, from_behind(): return lax.ppermute(block, 'segment', route)  3.61 us
    ppermute x2, starting transfers between devices, from_behind(): return lax.ppermute(block, 'segment', route)  2.56 us
  transfers between devices with their start and end apart: 6, of which 3 were waited for; matrix products, arithmetic and copies ran while one was open for 3% of the time, Pallas kernels for 15%

profile of v6, /device:TPU:0, one launch (start us, length us, event | category | flops | bytes accessed | tf_op | source)
XLA Modules:
  0.0 120.9 jit_solution(12817772563514972387)
XLA Ops:
  0.6 0.5 collective-permute-start.2
  1.2 1.3 %collective-permute-start.3 = (bf16[8,1024,128]{2,1,0:T(8,128)(2,1)}, bf16[8,1024,128]{2,1,0:T(8,128)(2,1)}, u32[]{:S(2)}, u32[]{:S(2)}) collective-permute-start(bf16[8,1024,128]{2,1,0:T(8,128)(2,1)} %bitcast.12), channel_id=1, source_target_pairs={{1,0},{3,2},{5,4},{7,6},{9,8},{11,10},{13,12},{15,14},{17,16},{19,... | collective-permute-start | bytes 6291464 | tf_op jit(solution)/shard_map/ppermute | solution.py:557
  2.5 2.3 %constant_dynamic-slice_fusion = bf16[8,512,128]{2,1,0:T(8,128)(2,1)} fusion(bf16[8,1024,128]{2,1,0:T(8,128)(2,1)} %bitcast.13, s32[]{:T(128)S(6)} %select_n.4), kind=kLoop, calls=%fused_computation.4 | loop fusion | bytes 2097156 | tf_op jit(solution)/shard_map/dynamic_slice | solution.py:597
  5.0 2.3 %own_inputs.1 = (bf16[2,1024,256]{2,1,0:T(8,128)(2,1)S(1)}, bf16[2,256,1024]{2,1,0:T(8,128)(2,1)S(1)}, f32[512,256]{1,0:T(8,128)S(1)}) custom-call(bf16[8,1024,128]{2,1,0:T(8,128)(2,1)} %bitcast.14, bf16[2,1024,256]{2,1,0:T(8,128)(2,1)} %constant.28.clone.third_hbm.third_ref, bf16[2,256,1024]{2,1,0:T(8,128)(2,1)} %constant.30.clone.second_hbm.second_ref), custom_call_target="tpu_custom_call" | custom-call | tf_op jit(solution)/shard_map/own_inputs/pallas_call | solution.py:542
  7.6 2.5 %input_modes.1 = (bf16[16,16,256]{2,1,0:T(8,128)(2,1)S(1)}, bf16[8,512,128]{2,1,0:T(8,128)(2,1)}, bf16[1,16,256]{2,1,0:T(8,128)(2,1)S(1)}) custom-call(bf16[2,1024,256]{2,1,0:T(8,128)(2,1)S(1)} %get-tuple-element.38.third_ref, bf16[2,256,1024]{2,1,0:T(8,128)(2,1)S(1)} %get-tuple-element.39.second_ref, f32[512,256]{1,0:T(8,128)S(1)} %get-tuple-element.40.own_sums_ref, ...), custom_call_target="tpu_custom_call" | custom-call | tf_op jit(solution)/shard_map/input_modes/pallas_call | solution.py:542
  10.1 14.7 %all_to_all.29.wire_ref = bf16[16,16,256]{2,1,0:T(8,128)(2,1)S(1)} all-to-all(bf16[16,16,256]{2,1,0:T(8,128)(2,1)S(1)} %get-tuple-element.42), channel_id=1, replica_groups=mesh['groups'=1,'gx'=8,'gy'=2,'segment'=2] {'gy','gx'}, dimensions={0} | all-to-all | bytes 262144 | tf_op jit(solution)/shard_map/all_to_all | solution.py:551
  24.8 1.1 mix_inputs.1
  25.9 10.2 %all_to_all.30.wire_in_ref = bf16[16,16,256]{2,1,0:T(8,128)(2,1)S(1)} all-to-all(bf16[16,16,256]{2,1,0:T(8,128)(2,1)S(1)} %get-tuple-element.43), channel_id=1, replica_groups=mesh['groups'=1,'gx'=8,'gy'=2,'segment'=2] {'gy','gx'}, dimensions={0} | all-to-all | bytes 262144 | tf_op jit(solution)/shard_map/all_to_all | solution.py:551
  36.1 0.7 pad_maximum_fusion
  36.8 1.3 %collective-permute-start.4 = (bf16[17,16,256]{2,1,0:T(8,128)(2,1)}, bf16[17,16,256]{2,1,0:T(8,128)(2,1)}, u32[]{:S(2)}, u32[]{:S(2)}) collective-permute-start(bf16[17,16,256]{2,1,0:T(8,128)(2,1)} %pad_maximum_fusion), channel_id=1, source_target_pairs={{1,0},{3,2},{5,4},{7,6},{9,8},{11,10},{13,12},{15,14},{17,16},{19,... | collective-permute-start | bytes 417800 | tf_op jit(solution)/shard_map/ppermute | solution.py:557
  38.2 10.1 %first_signal.1 = (bf16[16,16,256]{2,1,0:T(8,128)(2,1)}, f32[8,1024,128]{2,1,0:T(8,128)}) custom-call(s32[2]{0:T(128)S(1)} %pad_add_fusion.flags, f32[8,9]{1,0:T(8,128)S(1)} %pad_maximum_fusion.1.mixing_ref, bf16[8,1024,128]{2,1,0:T(8,128)(2,1)} %bitcast.15, bf16[8,512,128]{2,1,0:T(8,128)(2,1)} %get-tuple-element.41.act_other_hbm, ...), custom_call_target="tpu_custom_call" | custom-call | tf_op jit(solution)/shard_map/first_signal/pallas_call | solution.py:542
  48.3 3.6 %collective-permute-done.3.act_hbm = bf16[8,1024,128]{2,1,0:T(8,128)(2,1)} collective-permute-done((bf16[8,1024,128]{2,1,0:T(8,128)(2,1)}, bf16[8,1024,128]{2,1,0:T(8,128)(2,1)}, u32[]{:S(2)}, u32[]{:S(2)}) %collective-permute-start.3) | collective-permute-done | bytes 2097184 | tf_op jit(solution)/shard_map/ppermute | solution.py:557
  51.9 4.5 %conditional.1 = (bf16[16,16,256]{2,1,0:T(8,128)(2,1)}, bf16[8,1024,128]{2,1,0:T(8,128)(2,1)}) conditional(s32[]{:T(128)} %convert_element_type.5, (bf16[8,1024,128]{2,1,0:T(8,128)(2,1)}, bf16[16,16,256]{2,1,0:T(8,128)(2,1)}) %tuple.18, (bf16[16,16,256]{2,1,0:T(8,128)(2,1)}, s32[2]{0:T(128)S(1)}) %tuple.19), branch_computations={%region_0.1_spmd, %region_1.2_spmd} | conditional | bytes 8388664 | solution.py:645
  51.9 4.5 %collective-permute-done = bf16[8,1024,128]{2,1,0:T(8,128)(2,1)} collective-permute-done((bf16[8,1024,128]{2,1,0:T(8,128)(2,1)}, bf16[8,1024,128]{2,1,0:T(8,128)(2,1)}, u32[]{:S(2)}, u32[]{:S(2)}) %collective-permute-start) | collective-permute-done | bytes 2097184 | tf_op jit(solution)/shard_map/cond/branch_0_fun/ppermute | solution.py:561
  56.4 12.0 %shared.1.local_ref = f32[8,1024,128]{2,1,0:T(8,128)S(1)} custom-call(s32[2]{0:T(128)S(1)} %pad_add_fusion.flags, bf16[8,1024,128]{2,1,0:T(8,128)(2,1)} %collective-permute-done.3.act_hbm, bf16[8,1024,128]{2,1,0:T(8,128)(2,1)} %get-tuple-element.49.act_other_hbm, bf16[8,1024,128]{2,1,0:T(8,128)(2,1)} %bitcast.18, ...), custom_call_target="tpu_custom_call" | custom-call | tf_op jit(solution)/shard_map/shared/pallas_call | solution.py:542
  68.4 0.9 mix_signal.2
  69.4 16.3 %all_to_all.31.wire_in_ref.kept_wire_ref = bf16[32,16,256]{2,1,0:T(8,128)(2,1)S(1)} all-to-all(bf16[32,16,256]{2,1,0:T(8,128)(2,1)S(1)} %get-tuple-element.53), channel_id=1, replica_groups=mesh['groups'=1,'gx'=8,'gy'=2,'segment'=2] {'segment','gy','gx'}, dimensions={0} | all-to-all | bytes 524288 | tf_op jit(solution)/shard_map/all_to_all | solution.py:551
  85.7 8.4 %next_signal.1 = (bf16[16,16,256]{2,1,0:T(8,128)(2,1)S(1)}, f32[8,1024,128]{2,1,0:T(8,128)S(1)}) custom-call(s32[2]{0:T(128)S(1)} %pad_add_fusion.flags, f32[8,9]{1,0:T(8,128)S(1)} %pad_maximum_fusion.1.mixing_ref, f32[8,1024,128]{2,1,0:T(8,128)} %get-tuple-element.44.kept_hbm, f32[8,1024,128]{2,1,0:T(8,128)S(1)} %shared.1.local_ref, ...), custom_call_target="tpu_custom_call" | custom-call | tf_op jit(solution)/shard_map/next_signal/pallas_call | solution.py:542
  94.1 10.8 %all_to_all.32.wire_ref = bf16[16,16,256]{2,1,0:T(8,128)(2,1)S(1)} all-to-all(bf16[16,16,256]{2,1,0:T(8,128)(2,1)S(1)} %get-tuple-element.55), channel_id=1, replica_groups=mesh['groups'=1,'gx'=8,'gy'=2,'segment'=2] {'gy','gx'}, dimensions={0} | all-to-all | bytes 262144 | tf_op jit(solution)/shard_map/all_to_all | solution.py:551
  104.8 0.9 mix_signal.3
  105.8 10.2 %all_to_all.33.wire_in_ref = bf16[16,16,256]{2,1,0:T(8,128)(2,1)S(1)} all-to-all(bf16[16,16,256]{2,1,0:T(8,128)(2,1)S(1)} %get-tuple-element.56), channel_id=1, replica_groups=mesh['groups'=1,'gx'=8,'gy'=2,'segment'=2] {'gy','gx'}, dimensions={0} | all-to-all | bytes 262144 | tf_op jit(solution)/shard_map/all_to_all | solution.py:551
  116.0 1.0 last_other.1
  117.1 2.7 %last_own.1 = (bf16[8,1024,128]{2,1,0:T(8,128)(2,1)}, f32[64,8,8,32]{3,2,1,0:T(8,128)}) custom-call(f32[8,1024,128]{2,1,0:T(8,128)S(1)} %get-tuple-element.54.local_ref, bf16[256,1024]{1,0:T(8,128)(2,1)S(1)} %copy-done.2, bf16[1024,256]{1,0:T(8,128)(2,1)S(1)} %copy-done.1, bf16[16,16,256]{2,1,0:T(8,128)(2,1)S(1)} %all_to_all.33.wire_in_ref, ...), custom_call_target="tpu_custom_call" | custom-call | tf_op jit(solution)/shard_map/last_own/pallas_call | solution.py:542
  119.8 1.2 constant_dynamic-update-slice_fusion
  (33 shorter events, 0.8 us)
Async XLA Ops:
  0.6 4.2 %copy-start.10 = (f32[1,8]{1,0:T(1,128)S(1)}, f32[1,8]{1,0:T(1,128)}, u32[]{:S(2)}) copy-start(f32[1,8]{1,0:T(1,128)} %param.17) | copy-start | bytes 100
  0.6 4.2 %copy-start.9 = (f32[1,8,8]{2,1,0:T(8,128)S(1)}, f32[1,8,8]{2,1,0:T(8,128)}, u32[]{:S(2)}) copy-start(f32[1,8,8]{2,1,0:T(8,128)} %param.16) | copy-start | bytes 772
  0.6 37.5 %collective-permute-start.2 = (bf16[8,1024,128]{2,1,0:T(8,128)(2,1)}, bf16[8,1024,128]{2,1,0:T(8,128)(2,1)}, u32[]{:S(2)}, u32[]{:S(2)}) collective-permute-start(bf16[8,1024,128]{2,1,0:T(8,128)(2,1)} %bitcast.16), channel_id=1, source_target_pairs={{0,2},{2,0},{1,3},{3,1},{4,6},{6,4},{5,7},{7,5},{8,10},{10,8},{9,1... | collective-permute-start | bytes 6291464 | tf_op jit(solution)/shard_map/ppermute | solution.py:561
  1.2 50.7 %collective-permute-start.3 = (bf16[8,1024,128]{2,1,0:T(8,128)(2,1)}, bf16[8,1024,128]{2,1,0:T(8,128)(2,1)}, u32[]{:S(2)}, u32[]{:S(2)}) collective-permute-start(bf16[8,1024,128]{2,1,0:T(8,128)(2,1)} %bitcast.12), channel_id=1, source_target_pairs={{1,0},{3,2},{5,4},{7,6},{9,8},{11,10},{13,12},{15,14},{17,16},{19,... | collective-permute-start | bytes 6291464 | tf_op jit(solution)/shard_map/ppermute | solution.py:557
  4.7 2.9 %collective-permute-start.1 = (bf16[8,512,128]{2,1,0:T(8,128)(2,1)}, bf16[8,512,128]{2,1,0:T(8,128)(2,1)S(1)}, u32[]{:S(2)}, u32[]{:S(2)}) collective-permute-start(bf16[8,512,128]{2,1,0:T(8,128)(2,1)} %constant_dynamic-slice_fusion), channel_id=1, source_target_pairs={{0,2},{2,0},{1,3},{3,1},{4,6},{6,4},{5,7},{7,5},{8,10},{10,8},{9,1... | collective-permute-start | bytes 3145736 | tf_op jit(solution)/shard_map/ppermute | solution.py:561
  7.3 17.5 %copy-start = (f32[1,16,4,8,8,32]{5,4,3,2,1,0:T(8,128)S(1)}, f32[1,16,4,8,8,32]{5,4,3,2,1,0:T(8,128)}, u32[]{:S(2)}) copy-start(f32[1,16,4,8,8,32]{5,4,3,2,1,0:T(8,128)} %param.15) | copy-start | bytes 1572868
  7.3 17.5 %copy-start.5 = (bf16[2,256,64]{2,1,0:T(8,128)(2,1)S(1)}, bf16[2,256,64]{2,1,0:T(8,128)(2,1)}, u32[]{:S(2)}) copy-start(bf16[2,256,64]{2,1,0:T(8,128)(2,1)} %constant.33.clone.first_t_ref) | copy-start | bytes 196612
  7.3 17.5 %copy-start.6 = (bf16[2,64,256]{2,1,0:T(8,128)(2,1)S(1)}, bf16[2,64,256]{2,1,0:T(8,128)(2,1)}, u32[]{:S(2)}) copy-start(bf16[2,64,256]{2,1,0:T(8,128)(2,1)} %constant.32.clone.first_ref) | copy-start | bytes 196612
  10.1 28.1 %copy-start.1 = (bf16[1024,256]{1,0:T(8,128)(2,1)S(1)}, bf16[1024,256]{1,0:T(8,128)(2,1)}, u32[]{:S(2)}) copy-start(bf16[1024,256]{1,0:T(8,128)(2,1)} %constant.31.clone.second_t_ref) | copy-start | bytes 1572868
  10.1 28.1 %copy-start.2 = (bf16[256,1024]{1,0:T(8,128)(2,1)S(1)}, bf16[256,1024]{1,0:T(8,128)(2,1)}, u32[]{:S(2)}) copy-start(bf16[256,1024]{1,0:T(8,128)(2,1)} %constant.29.clone.third_t_ref) | copy-start | bytes 1572868
  36.8 19.6 %collective-permute-start.4 = (bf16[17,16,256]{2,1,0:T(8,128)(2,1)}, bf16[17,16,256]{2,1,0:T(8,128)(2,1)}, u32[]{:S(2)}, u32[]{:S(2)}) collective-permute-start(bf16[17,16,256]{2,1,0:T(8,128)(2,1)} %pad_maximum_fusion), channel_id=1, source_target_pairs={{1,0},{3,2},{5,4},{7,6},{9,8},{11,10},{13,12},{15,14},{17,16},{19,... | collective-permute-start | bytes 417800 | tf_op jit(solution)/shard_map/ppermute | solution.py:557
  51.9 4.5 %collective-permute-start = (bf16[8,1024,128]{2,1,0:T(8,128)(2,1)}, bf16[8,1024,128]{2,1,0:T(8,128)(2,1)}, u32[]{:S(2)}, u32[]{:S(2)}) collective-permute-start(bf16[8,1024,128]{2,1,0:T(8,128)(2,1)} %get-tuple-element.9), channel_id=1, source_target_pairs={{0,2},{2,0},{1,3},{3,1},{4,6},{6,4},{5,7},{7,5},{8,10},{10,8},{9,1... | collective-permute-start | bytes 6291464 | tf_op jit(solution)/shard_map/cond/branch_0_fun/ppermute | solution.py:561
  56.4 12.0 %copy-start.8 = (bf16[16,16,256]{2,1,0:T(8,128)(2,1)S(1)}, bf16[16,16,256]{2,1,0:T(8,128)(2,1)}, u32[]{:S(2)}) copy-start(bf16[16,16,256]{2,1,0:T(8,128)(2,1)} %get-tuple-element.52.wire_ref) | copy-start | bytes 393220
  68.4 17.3 %copy-start.3 = (bf16[2,256,1024]{2,1,0:T(8,128)(2,1)S(1)}, bf16[2,256,1024]{2,1,0:T(8,128)(2,1)}, u32[]{:S(2)}) copy-start(bf16[2,256,1024]{2,1,0:T(8,128)(2,1)} %constant.30.clone.second_hbm.second_ref) | copy-start | bytes 3145732
  68.4 17.3 %copy-start.4 = (bf16[2,1024,256]{2,1,0:T(8,128)(2,1)S(1)}, bf16[2,1024,256]{2,1,0:T(8,128)(2,1)}, u32[]{:S(2)}) copy-start(bf16[2,1024,256]{2,1,0:T(8,128)(2,1)} %constant.28.clone.third_hbm.third_ref) | copy-start | bytes 3145732
  116.0 1.1 copy-start.7
  117.0 2.8 %collective-permute-start.5 = (bf16[8,512,128]{2,1,0:T(8,128)(2,1)S(1)}, bf16[8,512,128]{2,1,0:T(8,128)(2,1)S(1)}, u32[]{:S(2)}, u32[]{:S(2)}) collective-permute-start(bf16[8,512,128]{2,1,0:T(8,128)(2,1)S(1)} %last_other.1), channel_id=1, source_target_pairs={{0,2},{2,0},{1,3},{3,1},{4,6},{6,4},{5,7},{7,5},{8,10},{10,8},{9,1... | collective-permute-start | bytes 3145736 | tf_op jit(solution)/shard_map/ppermute | solution.py:561
